TPU v7x, 512 devices: a whole 4x4x16 slice. The times are simulated.
512 devices in a mesh: cuts: 4 (over y_hi, core), mode: 128 (over y_lo, x, z).
Axes of the slice: x: 4, y: 4 (y_hi: 2, y_lo: 2; y = y_hi * 2 + y_lo), z: 16, core: 2. Of those that a mesh axis runs over, the one named last changes fastest.
Arguments:
- left_tensor: float32 [8, 2, 128, 512, 128], P('cuts', None, 'mode'), may hold values from -6 to 6
- right_tensor: float32 [8, 2, 512, 512], P('cuts', None, None, 'mode'), may hold values from -0.1875 to 0.1875
- closing_tensor: float32 [8, 2, 128, 4], P('cuts'), may hold values from -0.375 to 0.375
Outputs:
- amplitudes: float32 [512, 4, 2, 128], P(('cuts', 'mode'))
All inputs are finite; a program needn't handle non-finite values.
Results may differ from a plain program's by a relative error of at most 0.0001.
Values sent between devices are 32-bit elements; how exact they have to be, the bound alone decides.
No kernel may reach another device: no remote copies, remote signals or barrier semaphores. Data moves between devices by JAX's collectives and lax.ppermute only.
A program may use at most 64 MiB of HBM per device.

v0:
```python
import jax
import jax.numpy as jnp
from jax import lax
from jax.sharding import PartitionSpec as P


def shards(left_tensor, right_tensor, closing_tensor):
    hi = lax.Precision.HIGHEST
    left = left_tensor[:, :, 0]
    left_re, left_im = (left[:, 0], left[:, 1])
    slices_here = left.shape[0]
    rows = left.shape[3]
    cut_count = lax.axis_size("cuts")
    scale = 1.0 / jnp.sqrt(jnp.float32(slices_here * cut_count))
    piece = lax.all_gather(right_tensor, "mode", axis=3, tiled=True)
    piece_re = piece[:, 0]
    piece_im = piece[:, 1]
    mid_re = jnp.einsum("skq,skr->sqr", piece_re, left_re, precision=hi) - jnp.einsum(
        "skq,skr->sqr", piece_im, left_im, precision=hi
    )
    mid_im = jnp.einsum("skq,skr->sqr", piece_re, left_im, precision=hi) + jnp.einsum(
        "skq,skr->sqr", piece_im, left_re, precision=hi
    )
    middle = jnp.stack([mid_re, mid_im], axis=1)
    width = middle.shape[2]
    close_re, close_im = (closing_tensor[:, 0], closing_tensor[:, 1])
    shaped = middle.reshape(slices_here, 2, 1, cut_count, width // cut_count, rows)
    moved = lax.all_to_all(shaped, "mode", split_axis=4, concat_axis=2, tiled=True)
    moved_re, moved_im = (moved[:, 0], moved[:, 1])
    out_re = jnp.einsum("sho,shcwr->cwor", close_re, moved_re, precision=hi) - jnp.einsum(
        "sho,shcwr->cwor", close_im, moved_im, precision=hi
    )
    out_im = jnp.einsum("sho,shcwr->cwor", close_re, moved_im, precision=hi) + jnp.einsum(
        "sho,shcwr->cwor", close_im, moved_re, precision=hi
    )
    partial_amps = jnp.stack([out_re, out_im], axis=3) * scale
    owned = lax.psum_scatter(partial_amps, "cuts", scatter_dimension=0, tiled=True)
    return owned.reshape(owned.shape[1], owned.shape[2], 2, rows)


def solution(mesh):
    placed = (
        P("cuts", None, "mode", None, None),
        P("cuts", None, None, "mode"),
        P("cuts", None, None, None),
    )
    return jax.shard_map(
        shards,
        mesh=mesh,
        in_specs=placed,
        out_specs=P(("cuts", "mode"), None, None, None),
        check_vma=False,
    )
```

profile of v0, /device:TPU:1, one launch (start us, length us, event | category | flops | bytes accessed | tf_op | source)
XLA Modules:
  0.0 692.2 jit_solution(15370389483123603750)
XLA Ops:
  6.5 0.0 all-gather.2.cloned.1.call-start
  6.5 1.4 copy.11
  7.9 0.0 all-gather.2.cloned.1.call-update
  7.9 1.3 copy.44
  9.3 513.2 %all-gather.2.cloned.1.call-done = f32[2,2,512,512]{2,1,0,3:T(2,128)} async-done(((f32[2,2,512,4]{2,1,0,3:T(2,128)}), f32[2,2,512,512]{2,1,0,3:T(2,128)}) %all-gather.2.cloned.1.call-update) | async-done | bytes 4194320 | tf_op jit(solution)/shard_map/all_gather | solution.py:15
  522.5 7.1 %fusion.18 = (f32[2,1,512,512]{2,1,0,3:T(1,128)S(1)}, f32[2,1,512,512]{2,1,0,3:T(1,128)S(1)}) fusion(f32[2,2,512,512]{2,1,0,3:T(2,128)} %all-gather.2.cloned.1.call-done), kind=kLoop, calls=%fused_computation.33 | loop fusion | bytes 8388608 | tf_op jit(solution)/shard_map/slice | solution.py:17
  529.5 2.1 fusion
  531.6 2.1 fusion.1
  533.8 2.1 fusion.5
  535.9 0.4 copy.16
  536.3 2.3 fusion.4
  538.6 0.4 copy.15
  539.0 1.5 pad_maximum_fusion
  540.5 0.0 copy-start
  540.5 6.6 all-to-all-start
  547.2 1.3 dynamic-slice
  548.4 29.2 %all-to-all-done = f32[2,2,1,4,128,128]{5,0,3,1,2,4:T(2,128)S(1)} async-done(((f32[2,2,1,4,128,128]{5,0,3,1,2,4:T(2,128)}), f32[2,2,1,4,128,128]{5,0,3,1,2,4:T(2,128)S(1)}, u32[]{:S(2)}, u32[]{:S(2)}) %all-to-all-start) | async-done | bytes 1048608 | tf_op jit(solution)/shard_map/all_to_all | solution.py:28
  577.6 0.3 copy.43
  578.0 0.0 copy-done
  578.0 0.4 convolution_bitcast_fusion.1
  578.4 0.4 convolution_bitcast_fusion.3
  578.7 0.4 fusion.7
  579.1 0.4 fusion.9
  579.5 104.6 %all-reduce = f32[4,1,4,2,128]{4,2,0,3,1:T(4,128)S(1)} all-reduce(f32[4,1,4,2,128]{4,2,0,3,1:T(4,128)S(1)} %maximum_multiply_fusion), channel_id=2, replica_groups=mesh['cuts'=4,'mode'=128] {'cuts'}, use_global_device_ids=true, to_apply=%region_0.0.clone | all-reduce | flops 4096 | bytes 32768
  684.1 0.6 dynamic-slice_bitcast_fusion
  684.8 0.6 copy.20
  (1 shorter events, 0.0 us)
Async XLA Ops:
  6.5 515.9 %all-gather.2.cloned.1.call-start = ((), (), s32[]{:S(2)}) async-start(), calls=%async_computation.1 | async-start | bytes 4227072 | tf_op jit(solution)/shard_map/all_gather | solution.py:15
  540.5 37.5 %copy-start = (f32[2,2,128,4]{2,3,1,0:T(4,128)S(1)}, f32[2,2,128,4]{2,3,1,0:T(4,128)}, u32[]{:S(2)}) copy-start(f32[2,2,128,4]{2,3,1,0:T(4,128)} %param.5) | copy-start | bytes 24580
  540.5 37.1 %all-to-all-start = ((f32[2,2,1,4,128,128]{5,0,3,1,2,4:T(2,128)}), f32[2,2,1,4,128,128]{5,0,3,1,2,4:T(2,128)S(1)}, u32[]{:S(2)}, u32[]{:S(2)}) async-start(f32[2,2,1,4,128,128]{5,0,3,1,2,4:T(2,128)} %pad_maximum_fusion), calls=%async_computation | async-start | bytes 2097152 | tf_op jit(solution)/shard_map/all_to_all | solution.py:28
Sparse Core Ops, SparseCore 0:
  9.4 512.9 all-gather.1
where the time goes:
time: 694 us; the launch traced here: 692 us
  waiting for transfers between devices  542 us (78%)
  blocking collectives  105 us (15%)
  between operations  13.5 us (2%)
  local copies, waits for them, and re-layouts  13.4 us (2%)
  matrix products  10.1 us (1%)
    all_gather x1, waiting for transfers between devices, shards(): piece = lax.all_gather(right_tensor, 'mode', axis=3, tiled=True)  513 us
    unnamed x1, blocking collectives  105 us
    all_to_all x1, waiting for transfers between devices, shards(): lax.all_to_all(shaped, 'mode', split_axis=4, concat_axis=2, tiled=True)  29.2 us
  transfers between devices with their start and end apart: 2, of which 2 were waited for; matrix products, arithmetic and copies ran while one was open for 0% of the time, Pallas kernels for 0%

commit v1 on v0

v1 whole, which is shorter than its diff:
```python
import jax
import jax.numpy as jnp
from jax import lax
from jax.experimental import pallas as pl
from jax.experimental.pallas import tpu as pltpu
from jax.sharding import Mesh
from jax.sharding import PartitionSpec as P

PARTS = (("yh", 2), ("core", 2), ("yl", 2), ("x", 4), ("za", 8), ("zb", 2))
CUTS = ("yh", "core")
MODE = ("yl", "x", "za", "zb")
NEAR = ("yl", "x", "zb")
FAR = "za"

F32 = jnp.float32
LANES = 128
GROUP = 16


def swap_blocks(v):
    block = lax.broadcasted_iota(jnp.int32, v[0].shape, 1) // GROUP
    v = list(v)
    for bit in (1, 2, 4):
        low = (block & bit) == 0
        for i in range(8):
            if i & bit:
                continue
            a, b = v[i], v[i | bit]
            v[i] = jnp.where(low, a, pltpu.roll(b, GROUP * bit, 1))
            v[i | bit] = jnp.where(low, pltpu.roll(a, LANES - GROUP * bit, 1), b)
    return v


def close_kernel(coef_ref, left_ref, out_ref):
    heads, slices, _, depth, _ = left_ref.shape
    outs = coef_ref.shape[0] // (2 * slices)
    rows = 8
    for s in range(slices):
        acc = [[None] * (depth // rows) for _ in range(2 * outs)]
        for h in range(heads):
            co = [coef_ref[s * 2 * outs + j, h] for j in range(2 * outs)]
            for kb in range(depth // rows):
                at = pl.ds(kb * rows, rows)
                re, im = left_ref[h, s, 0, at, :], left_ref[h, s, 1, at, :]
                for o in range(outs):
                    cre, cim = co[o], co[outs + o]
                    new_re = cre * re - cim * im
                    new_im = cre * im + cim * re
                    if h:
                        new_re, new_im = acc[o][kb] + new_re, acc[outs + o][kb] + new_im
                    acc[o][kb], acc[outs + o][kb] = new_re, new_im
        for kb in range(depth // rows):
            w = swap_blocks([acc[j][kb] for j in range(2 * outs)])
            for g in range(8):
                out_ref[g, pl.ds(s * depth + kb * rows, rows), :] = w[g]


def join_kernel(parts_ref, right_ref, out_ref):
    m = parts_ref[0]
    for i in range(1, parts_ref.shape[0]):
        m = m + parts_ref[i]
    turned = pltpu.roll(m, LANES // 2, 1)
    lane = lax.broadcasted_iota(jnp.int32, m.shape, 1)
    rhs = jnp.concatenate([m, jnp.where(lane < LANES // 2, -turned, turned)], axis=0)
    out = jnp.dot(right_ref[...], rhs, precision=lax.Precision.HIGHEST, preferred_element_type=F32)
    out_ref[...] = out


def shards(left_tensor, right_tensor, closing_tensor):
    slices, _, _, depth, rows = left_tensor.shape
    width = right_tensor.shape[3]
    outs = closing_tensor.shape[3]
    near = 16
    kk = depth // near
    scale = 1.0 / jnp.sqrt(F32(slices * 4))

    with jax.named_scope("right_move"):
        r = right_tensor.reshape(slices, 2, 8, 2, kk, width)
        r = r.transpose(2, 3, 5, 1, 0, 4).reshape(8, 1, 2, width, LANES)
        r = jnp.broadcast_to(r, (8, 8, 2, width, LANES)).reshape(128, width, LANES)
        r = lax.all_to_all(r, MODE, 0, 0, tiled=True)
        r = r.reshape(32, 8, 2, LANES).transpose(0, 2, 1, 3).reshape(512, LANES)

    with jax.named_scope("left_move"):
        x = left_tensor.reshape(slices, 2, near, kk, rows).transpose(2, 0, 1, 3, 4)
        x = lax.all_to_all(x, NEAR, 0, 0, tiled=True)

    with jax.named_scope("coefs"):
        co = closing_tensor.reshape(slices, 2, 8, 8, 2, outs)
        co = lax.dynamic_index_in_dim(co, lax.axis_index(FAR), 3, keepdims=False)
        co = co.transpose(0, 1, 4, 2, 3).reshape(slices * 2 * outs, near) * scale

    with jax.named_scope("close"):
        x = pl.pallas_call(
            close_kernel,
            out_shape=jax.ShapeDtypeStruct((8, slices * kk, LANES), F32),
            in_specs=[pl.BlockSpec(memory_space=pltpu.SMEM), pl.BlockSpec(memory_space=pltpu.VMEM)],
            out_specs=pl.BlockSpec(memory_space=pltpu.VMEM),
            compiler_params=pltpu.CompilerParams(vmem_limit_bytes=16 * 2**20),
            cost_estimate=pl.CostEstimate(flops=2**22, bytes_accessed=5 * 2**18, transcendentals=0),
        )(co, x)

    with jax.named_scope("middle_move"):
        x = lax.all_to_all(x, FAR, 0, 0, tiled=True)

    with jax.named_scope("join"):
        p = pl.pallas_call(
            join_kernel,
            out_shape=jax.ShapeDtypeStruct((512, LANES), F32),
            in_specs=[pl.BlockSpec(memory_space=pltpu.VMEM)] * 2,
            out_specs=pl.BlockSpec(memory_space=pltpu.VMEM),
            compiler_params=pltpu.CompilerParams(vmem_limit_bytes=16 * 2**20),
            cost_estimate=pl.CostEstimate(flops=2**26, bytes_accessed=3 * 2**18, transcendentals=0),
        )(x, r)

    with jax.named_scope("sum_move"):
        p = lax.all_to_all(p.reshape(64, 8, LANES), CUTS + NEAR, 0, 0, tiled=True)
        p = jnp.sum(p, axis=0)

    with jax.named_scope("row_move"):
        p = lax.all_to_all(p, FAR, 0, 0, tiled=True)
        p = p.reshape(8, 2, outs, GROUP).transpose(2, 1, 0, 3)
    return p.reshape(1, outs, 2, rows)


def solution(mesh):
    fine = Mesh(mesh.devices.reshape([n for _, n in PARTS]), [name for name, _ in PARTS])
    return jax.shard_map(
        shards,
        mesh=fine,
        in_specs=(
            P(CUTS, None, MODE, None, None),
            P(CUTS, None, None, MODE),
            P(CUTS, None, None, None),
        ),
        out_specs=P(CUTS + MODE, None, None, None),
        check_vma=False,
    )
```

time: 694 us -> 122 us (0.18)
  waiting for transfers between devices: 542 us -> 44.5 us
  blocking collectives: 105 us -> 35.8 us
  starting transfers between devices: 6.64 us -> 31.4 us
  between operations: 13.5 us -> 0.12 us
  matrix products: 10.1 us -> 0 us
  local copies, waits for them, and re-layouts: 13.4 us -> 5.77 us
    all_gather x1 -> x0, waiting for transfers between devices: 513 us -> none  [shards(): piece = lax.all_gather(right_tensor, 'mode', axis=3, tiled=True)]
    unnamed x1 -> x0, blocking collectives: 105 us -> none
    all_to_all x0 -> x2, blocking collectives: none -> 35.8 us  [the longest x1 21.8 us: shards(): p = lax.all_to_all(p.reshape(64, 8, LANES), CUTS + NEAR, 0, 0, tiled=True)]
    all_to_all x1 -> x3, starting transfers between devices: 6.63 us -> 31.4 us  [the longest x1 18 us: shards(): r = lax.all_to_all(r, MODE, 0, 0, tiled=True)]
    all_to_all x1 -> x3, waiting for transfers between devices: 29.2 us -> 44.5 us  [the longest x1 16.4 us: shards(): x = lax.all_to_all(x, FAR, 0, 0, tiled=True)]
    dot_general x8 -> x0, matrix products: 10.1 us -> none  [the longest x1 2.3 us: shards(): jnp.einsum('skq,skr->sqr', piece_im, left_im, precision=hi)]
    slice x1 -> x0, local copies, waits for them, and re-layouts: 7.06 us -> none  [shards(): piece_im = piece[:, 1]]
  transfers between devices with their start and end apart: 2 -> 3, of which waited for: 2 -> 3; matrix products, arithmetic and copies ran while one was open for 0% -> 1% of each run, Pallas kernels for 0% -> 2%
where the time goes in v1:
time: 122 us; the launch traced here: 121 us
  waiting for transfers between devices  44.5 us (36%)
  blocking collectives  35.8 us (29%)
  starting transfers between devices  31.4 us (26%)
  local copies, waits for them, and re-layouts  5.77 us (5%)
  Pallas kernels  2.65 us (2%)
    all_to_all x1, blocking collectives, shards(): p = lax.all_to_all(p.reshape(64, 8, LANES), CUTS + NEAR, 0, 0, tiled=True)  21.8 us
    all_to_all x1, starting transfers between devices, shards(): r = lax.all_to_all(r, MODE, 0, 0, tiled=True)  18 us
    all_to_all x1, waiting for transfers between devices, shards(): x = lax.all_to_all(x, FAR, 0, 0, tiled=True)  16.4 us
    all_to_all x1, waiting for transfers between devices, shards(): r = lax.all_to_all(r, MODE, 0, 0, tiled=True)  14.4 us
    all_to_all x1, blocking collectives, shards(): p = lax.all_to_all(p, FAR, 0, 0, tiled=True)  14 us
    all_to_all x1, waiting for transfers between devices, shards(): x = lax.all_to_all(x, NEAR, 0, 0, tiled=True)  13.7 us
    all_to_all x1, starting transfers between devices, shards(): x = lax.all_to_all(x, NEAR, 0, 0, tiled=True)  7.45 us
    all_to_all x1, starting transfers between devices, shards(): x = lax.all_to_all(x, FAR, 0, 0, tiled=True)  6 us
  transfers between devices with their start and end apart: 3, of which 3 were waited for; matrix products, arithmetic and copies ran while one was open for 1% of the time, Pallas kernels for 2%

profile of v1, /device:TPU:1, one launch (start us, length us, event | category | flops | bytes accessed | tf_op | source)
XLA Modules:
  0.0 121.0 jit_solution(16965129556131555566)
XLA Ops:
  0.0 2.3 %copy.30 = f32[2,2,16,32,128]{4,3,1,0,2:T(8,128)} copy(f32[2,2,16,32,128]{4,3,2,1,0:T(8,128)} %bitcast.30) | data formatting | bytes 2097152 | tf_op jit(solution)/shard_map/left_move/reshape | solution.py:85
  2.3 0.0 copy-start
  2.3 7.5 %all-to-all-start = ((f32[16,2,2,32,128]{4,3,2,1,0:T(8,128)}), f32[16,2,2,32,128]{4,3,2,1,0:T(8,128)S(1)}, u32[]{:S(2)}, u32[]{:S(2)}) async-start(f32[16,2,2,32,128]{4,3,2,1,0:T(8,128)} %bitcast.26), calls=%async_computation | async-start | bytes 2097152 | tf_op jit(solution)/shard_map/left_move/all_to_all | solution.py:86
  9.8 0.0 copy-done
  9.8 0.2 reshape.39
  9.9 0.1 copy.31
  10.0 0.2 broadcast_in_dim.7
  10.2 13.7 %all-to-all-done.left_ref = f32[16,2,2,32,128]{4,3,2,1,0:T(8,128)S(1)} async-done(((f32[16,2,2,32,128]{4,3,2,1,0:T(8,128)}), f32[16,2,2,32,128]{4,3,2,1,0:T(8,128)S(1)}, u32[]{:S(2)}, u32[]{:S(2)}) %all-to-all-start) | async-done | bytes 1048608 | tf_op jit(solution)/shard_map/left_move/all_to_all | solution.py:86
  23.9 0.7 broadcast_in_dim.8
  24.7 18.0 %all-to-all-start.2 = ((f32[128,4,128]{2,1,0:T(4,128)}), f32[128,4,128]{2,1,0:T(4,128)S(1)}, u32[]{:S(2)}, u32[]{:S(2)}) async-start(f32[128,4,128]{2,1,0:T(4,128)} %bitcast.6), calls=%async_computation.2 | async-start | bytes 524288 | tf_op jit(solution)/shard_map/right_move/all_to_all | solution.py:81
  42.6 0.0 copy-start.1
  42.6 0.7 copy-done.1
  43.3 0.1 copy.20
  43.5 0.1 mul.16
  43.6 0.1 copy.23.coef_ref
  43.7 2.2 %close.1 = f32[8,64,128]{2,1,0:T(8,128)} custom-call(f32[16,16]{1,0:T(8,128)S(1)} %copy.23.coef_ref, f32[16,2,2,32,128]{4,3,2,1,0:T(8,128)S(1)} %all-to-all-done.left_ref), custom_call_target="tpu_custom_call" | custom-call | flops 4194304 | bytes 1310720 | tf_op jit(solution)/shard_map/close/pallas_call | solution.py:94
  45.9 14.4 %all-to-all-done.2 = f32[128,4,128]{2,1,0:T(4,128)S(1)} async-done(((f32[128,4,128]{2,1,0:T(4,128)}), f32[128,4,128]{2,1,0:T(4,128)S(1)}, u32[]{:S(2)}, u32[]{:S(2)}) %all-to-all-start.2) | async-done | bytes 262176 | tf_op jit(solution)/shard_map/right_move/all_to_all | solution.py:81
  60.3 6.0 %all-to-all-start.1 = ((f32[8,64,128]{2,1,0:T(8,128)}), f32[8,64,128]{2,1,0:T(8,128)S(1)}, u32[]{:S(2)}, u32[]{:S(2)}) async-start(f32[8,64,128]{2,1,0:T(8,128)} %close.1), calls=%async_computation.1 | async-start | bytes 524288 | tf_op jit(solution)/shard_map/middle_move/all_to_all | solution.py:104
  66.4 16.4 %all-to-all-done.1.parts_ref = f32[8,64,128]{2,1,0:T(8,128)S(1)} async-done(((f32[8,64,128]{2,1,0:T(8,128)}), f32[8,64,128]{2,1,0:T(8,128)S(1)}, u32[]{:S(2)}, u32[]{:S(2)}) %all-to-all-start.1) | async-done | bytes 262176 | tf_op jit(solution)/shard_map/middle_move/all_to_all | solution.py:104
  82.7 0.4 join.1
  83.2 21.8 %all_to_all.29 = f32[64,8,128]{2,1,0:T(8,128)S(1)} all-to-all(f32[64,8,128]{2,1,0:T(8,128)S(1)} %bitcast.29), channel_id=1, replica_groups=mesh['yh'=2,'core'=2,'yl'=2,'x'=4,'za'=8,'zb'=2] {'yh','core','yl','x','..., dimensions={0} | all-to-all | bytes 524288 | tf_op jit(solution)/shard_map/sum_move/all_to_all | solution.py:117
  104.9 0.1 reduce_sum.9
  105.0 14.0 %all_to_all.30 = f32[8,1,128]{2,1,0:T(1,128)S(1)} all-to-all(f32[8,1,128]{2,1,0:T(1,128)S(1)} %bitcast.35), channel_id=1, replica_groups=mesh['yh'=2,'core'=2,'yl'=2,'x'=4,'za'=8,'zb'=2] {'za'}, dimensions={0} | all-to-all | bytes 8192 | tf_op jit(solution)/shard_map/row_move/all_to_all | solution.py:121
  119.0 0.5 broadcast.9
  119.6 0.7 reduce.3
  120.2 0.1 reshape.44
  120.3 0.7 reshape.45
  (5 shorter events, 0.1 us)
Async XLA Ops:
  2.3 7.5 %copy-start = (f32[2,2,512,4]{2,3,1,0:T(4,128)S(1)}, f32[2,2,512,4]{2,3,1,0:T(4,128)}, u32[]{:S(2)}) copy-start(f32[2,2,512,4]{2,3,1,0:T(4,128)} %param.4) | copy-start | bytes 98308
  2.3 21.6 %all-to-all-start = ((f32[16,2,2,32,128]{4,3,2,1,0:T(8,128)}), f32[16,2,2,32,128]{4,3,2,1,0:T(8,128)S(1)}, u32[]{:S(2)}, u32[]{:S(2)}) async-start(f32[16,2,2,32,128]{4,3,2,1,0:T(8,128)} %bitcast.26), calls=%async_computation | async-start | bytes 2097152 | tf_op jit(solution)/shard_map/left_move/all_to_all | solution.py:86
  24.7 35.7 %all-to-all-start.2 = ((f32[128,4,128]{2,1,0:T(4,128)}), f32[128,4,128]{2,1,0:T(4,128)S(1)}, u32[]{:S(2)}, u32[]{:S(2)}) async-start(f32[128,4,128]{2,1,0:T(4,128)} %bitcast.6), calls=%async_computation.2 | async-start | bytes 524288 | tf_op jit(solution)/shard_map/right_move/all_to_all | solution.py:81
  42.6 0.7 copy-start.1
  60.3 22.4 %all-to-all-start.1 = ((f32[8,64,128]{2,1,0:T(8,128)}), f32[8,64,128]{2,1,0:T(8,128)S(1)}, u32[]{:S(2)}, u32[]{:S(2)}) async-start(f32[8,64,128]{2,1,0:T(8,128)} %close.1), calls=%async_computation.1 | async-start | bytes 524288 | tf_op jit(solution)/shard_map/middle_move/all_to_all | solution.py:104

commit v2 on v1

--- a/solution.py
+++ b/solution.py
@@ -18,30 +18,56 @@
 
 
 def swap_blocks(v):
-    block = lax.broadcasted_iota(jnp.int32, v[0].shape, 1) // GROUP
+    n = len(v)
+    size = LANES // n
+    block = lax.broadcasted_iota(jnp.int32, v[0].shape, 1) // size
     v = list(v)
-    for bit in (1, 2, 4):
+    bit = 1
+    while bit < n:
         low = (block & bit) == 0
-        for i in range(8):
+        for i in range(n):
             if i & bit:
                 continue
             a, b = v[i], v[i | bit]
-            v[i] = jnp.where(low, a, pltpu.roll(b, GROUP * bit, 1))
-            v[i | bit] = jnp.where(low, pltpu.roll(a, LANES - GROUP * bit, 1), b)
+            v[i] = jnp.where(low, a, pltpu.roll(b, size * bit, 1))
+            v[i | bit] = jnp.where(low, pltpu.roll(a, LANES - size * bit, 1), b)
+        bit *= 2
     return v
 
 
-def close_kernel(coef_ref, left_ref, out_ref):
-    heads, slices, _, depth, _ = left_ref.shape
-    outs = coef_ref.shape[0] // (2 * slices)
+def pack_kernel(left_ref, right_ref, out_ref, sems):
+    slices, _, near, depth, _ = left_ref.shape
+    copies = []
+    for i in range(2 * slices):
+        to = out_ref.at[:, pl.ds(i * depth, depth), :]
+        copies.append(pltpu.make_async_copy(left_ref.at[i // 2, i % 2], to, sems.at[i]))
+        copies[-1].start()
+    width = right_ref.shape[2]
+    each = 2 * slices
+    for t in range(near // each):
+        lanes = pl.ds(t * LANES, LANES)
+        w = swap_blocks([right_ref[j % slices, j // slices, :, lanes] for j in range(each)])
+        for g in range(each):
+            out_ref[t * each + g, pl.ds(each * depth, width), :] = w[g]
+    for copy in copies:
+        copy.wait()
+
+
+def close_kernel(far_ref, coef_ref, left_ref, out_ref):
+    heads = left_ref.shape[0]
+    slices, _, outs, _ = coef_ref.shape
+    depth = out_ref.shape[1] // slices
+    first = far_ref[0] * 2
     rows = 8
     for s in range(slices):
         acc = [[None] * (depth // rows) for _ in range(2 * outs)]
         for h in range(heads):
-            co = [coef_ref[s * 2 * outs + j, h] for j in range(2 * outs)]
+            head = (h // 2) * 16 + first + h % 2
+            co = [coef_ref[s, j // outs, j % outs, head] for j in range(2 * outs)]
             for kb in range(depth // rows):
-                at = pl.ds(kb * rows, rows)
-                re, im = left_ref[h, s, 0, at, :], left_ref[h, s, 1, at, :]
+                at = 2 * s * depth + kb * rows
+                re = left_ref[h, pl.ds(at, rows), :]
+                im = left_ref[h, pl.ds(at + depth, rows), :]
                 for o in range(outs):
                     cre, cim = co[o], co[outs + o]
                     new_re = cre * re - cim * im
@@ -74,31 +100,35 @@
     kk = depth // near
     scale = 1.0 / jnp.sqrt(F32(slices * 4))
 
-    with jax.named_scope("right_move"):
-        r = right_tensor.reshape(slices, 2, 8, 2, kk, width)
-        r = r.transpose(2, 3, 5, 1, 0, 4).reshape(8, 1, 2, width, LANES)
-        r = jnp.broadcast_to(r, (8, 8, 2, width, LANES)).reshape(128, width, LANES)
-        r = lax.all_to_all(r, MODE, 0, 0, tiled=True)
-        r = r.reshape(32, 8, 2, LANES).transpose(0, 2, 1, 3).reshape(512, LANES)
+    with jax.named_scope("pack"):
+        body = slices * 2 * kk
+        x = pl.pallas_call(
+            pack_kernel,
+            out_shape=jax.ShapeDtypeStruct((near, body + width, LANES), F32),
+            in_specs=[pl.BlockSpec(memory_space=pl.ANY), pl.BlockSpec(memory_space=pltpu.VMEM)],
+            out_specs=pl.BlockSpec(memory_space=pltpu.VMEM),
+            scratch_shapes=[pltpu.SemaphoreType.DMA((slices * 2,))],
+            compiler_params=pltpu.CompilerParams(vmem_limit_bytes=16 * 2**20),
+            cost_estimate=pl.CostEstimate(flops=0, bytes_accessed=2**21, transcendentals=0),
+        )(left_tensor.reshape(slices, 2, near, kk, rows), right_tensor.transpose(0, 1, 3, 2))
 
-    with jax.named_scope("left_move"):
-        x = left_tensor.reshape(slices, 2, near, kk, rows).transpose(2, 0, 1, 3, 4)
+    with jax.named_scope("near_move"):
         x = lax.all_to_all(x, NEAR, 0, 0, tiled=True)
 
-    with jax.named_scope("coefs"):
-        co = closing_tensor.reshape(slices, 2, 8, 8, 2, outs)
-        co = lax.dynamic_index_in_dim(co, lax.axis_index(FAR), 3, keepdims=False)
-        co = co.transpose(0, 1, 4, 2, 3).reshape(slices * 2 * outs, near) * scale
+    with jax.named_scope("right_move"):
+        r = lax.all_gather(x[:, body:], FAR, axis=0, tiled=True)
+        r = r.reshape(4, 2, 2, 4, 2, 2, 2, LANES)
+        r = r.transpose(2, 3, 0, 6, 1, 4, 5, 7).reshape(512, LANES)
 
     with jax.named_scope("close"):
         x = pl.pallas_call(
             close_kernel,
             out_shape=jax.ShapeDtypeStruct((8, slices * kk, LANES), F32),
-            in_specs=[pl.BlockSpec(memory_space=pltpu.SMEM), pl.BlockSpec(memory_space=pltpu.VMEM)],
+            in_specs=[pl.BlockSpec(memory_space=pltpu.SMEM)] * 2 + [pl.BlockSpec(memory_space=pltpu.VMEM)],
             out_specs=pl.BlockSpec(memory_space=pltpu.VMEM),
             compiler_params=pltpu.CompilerParams(vmem_limit_bytes=16 * 2**20),
             cost_estimate=pl.CostEstimate(flops=2**22, bytes_accessed=5 * 2**18, transcendentals=0),
-        )(co, x)
+        )(lax.axis_index(FAR).reshape(1), closing_tensor.transpose(0, 1, 3, 2), x)
 
     with jax.named_scope("middle_move"):
         x = lax.all_to_all(x, FAR, 0, 0, tiled=True)
@@ -115,7 +145,7 @@
 
     with jax.named_scope("sum_move"):
         p = lax.all_to_all(p.reshape(64, 8, LANES), CUTS + NEAR, 0, 0, tiled=True)
-        p = jnp.sum(p, axis=0)
+        p = jnp.sum(p, axis=0) * scale
 
     with jax.named_scope("row_move"):
         p = lax.all_to_all(p, FAR, 0, 0, tiled=True)

time: 122 us -> 120 us (0.984)
  blocking collectives: 35.8 us -> 73.5 us
  waiting for transfers between devices: 44.5 us -> 14.8 us
  starting transfers between devices: 31.4 us -> 23 us
  local copies, waits for them, and re-layouts: 5.77 us -> 3.41 us
  Pallas kernels: 2.65 us -> 4.01 us
    all_gather x0 -> x1, blocking collectives: none -> 33.4 us  [shards(): r = lax.all_gather(x[:, body:], FAR, axis=0, tiled=True)]
    all_to_all x1 -> x0, starting transfers between devices: 18 us -> none  [shards(): r = lax.all_to_all(r, MODE, 0, 0, tiled=True)]
    all_to_all x1, waiting for transfers between devices: 16.4 us -> 0.01 us  [shards(): x = lax.all_to_all(x, FAR, 0, 0, tiled=True)]
    all_to_all x1 -> x0, waiting for transfers between devices: 14.4 us -> none  [shards(): r = lax.all_to_all(r, MODE, 0, 0, tiled=True)]
    all_to_all x1, starting transfers between devices: 6 us -> 15.7 us  [shards(): x = lax.all_to_all(x, FAR, 0, 0, tiled=True)]
    all_to_all x1, blocking collectives: 14 us -> 18.7 us  [shards(): p = lax.all_to_all(p, FAR, 0, 0, tiled=True)]
    reshape x3 -> x1, local copies, waits for them, and re-layouts: 2.55 us -> 0.14 us  [shards(): r = r.reshape(4, 2, 2, 4, 2, 2, 2, LANES)]
    pallas_call x0 -> x1, Pallas kernels: none -> 1.26 us  [shards(): pl.pallas_call(pack_kernel, out_shape=jax.ShapeDtypeStruct((near, body +...]
  transfers between devices with their start and end apart: 3 -> 2, of which waited for: 3 -> 1; matrix products, arithmetic and copies ran while one was open for 1% -> 0% of each run, Pallas kernels for 2% -> 0%
where the time goes in v2:
time: 120 us; the launch traced here: 119 us
  blocking collectives  73.5 us (61%)
  starting transfers between devices  23 us (19%)
  waiting for transfers between devices  14.8 us (12%)
  Pallas kernels  4.01 us (3%)
  local copies, waits for them, and re-layouts  3.41 us (3%)
    all_gather x1, blocking collectives, shards(): r = lax.all_gather(x[:, body:], FAR, axis=0, tiled=True)  33.4 us
    all_to_all x1, blocking collectives, shards(): p = lax.all_to_all(p.reshape(64, 8, LANES), CUTS + NEAR, 0, 0, tiled=True)  21.4 us
    all_to_all x1, blocking collectives, shards(): p = lax.all_to_all(p, FAR, 0, 0, tiled=True)  18.7 us
    all_to_all x1, starting transfers between devices, shards(): x = lax.all_to_all(x, FAR, 0, 0, tiled=True)  15.7 us
    all_to_all x1, waiting for transfers between devices, shards(): x = lax.all_to_all(x, NEAR, 0, 0, tiled=True)  14.8 us
    all_to_all x1, starting transfers between devices, shards(): x = lax.all_to_all(x, NEAR, 0, 0, tiled=True)  7.33 us
  transfers between devices with their start and end apart: 2, of which 1 were waited for; matrix products, arithmetic and copies ran while one was open for 0% of the time, Pallas kernels for 0%

profile of v2, /device:TPU:1, one launch (start us, length us, event | category | flops | bytes accessed | tf_op | source)
XLA Modules:
  0.0 119.5 jit_solution(15189280937915751478)
XLA Ops:
  0.0 0.0 copy-start
  0.0 1.2 %copy-done = f32[2,2,1,512,128]{4,3,2,1,0:T(8,128)S(1)} copy-done((f32[2,2,1,512,128]{4,3,2,1,0:T(8,128)S(1)}, f32[2,2,1,512,128]{4,3,2,1,0:T(8,128)}, u32[]{:S(2)}) %copy-start) | copy-done | bytes 1048600
  1.2 0.0 copy-start.1
  1.2 0.8 copy-done.1
  2.0 1.3 %pack.1 = f32[16,132,128]{2,1,0:T(8,128)} custom-call(f32[2,2,16,32,128]{4,3,2,1,0:T(8,128)S(1)} %bitcast.15, f32[2,2,4,512]{3,2,1,0:T(4,128)S(1)} %bitcast.16), custom_call_target="tpu_custom_call" | custom-call | bytes 2097152 | tf_op jit(solution)/shard_map/pack/pallas_call | solution.py:105
  3.3 0.0 copy-start.2
  3.3 7.3 %all-to-all-start = ((f32[16,132,128]{2,1,0:T(8,128)}), f32[16,132,128]{2,1,0:T(8,128)S(1)}, u32[]{:S(2)}, u32[]{:S(2)}) async-start(f32[16,132,128]{2,1,0:T(8,128)} %pack.1), calls=%async_computation | async-start | bytes 2228224 | tf_op jit(solution)/shard_map/near_move/all_to_all | solution.py:116
  10.6 14.8 %all-to-all-done.left_ref = f32[16,132,128]{2,1,0:T(8,128)S(1)} async-done(((f32[16,132,128]{2,1,0:T(8,128)}), f32[16,132,128]{2,1,0:T(8,128)S(1)}, u32[]{:S(2)}, u32[]{:S(2)}) %all-to-all-start) | async-done | bytes 1081376 | tf_op jit(solution)/shard_map/near_move/all_to_all | solution.py:116
  25.4 0.0 copy-done.2
  25.4 2.3 %close.1 = f32[8,64,128]{2,1,0:T(8,128)} custom-call(s32[1]{0:T(128)} %bitcast.far_ref, f32[2,2,4,128]{3,2,1,0:T(4,128)S(1)} %bitcast.17, f32[16,132,128]{2,1,0:T(8,128)S(1)} %all-to-all-done.left_ref), custom_call_target="tpu_custom_call" | custom-call | flops 4194304 | bytes 1310720 | tf_op jit(solution)/shard_map/close/pallas_call | solution.py:124
  27.7 15.7 %all-to-all-start.1 = ((f32[8,64,128]{2,1,0:T(8,128)}), f32[8,64,128]{2,1,0:T(8,128)S(1)}, u32[]{:S(2)}, u32[]{:S(2)}) async-start(f32[8,64,128]{2,1,0:T(8,128)} %close.1), calls=%async_computation.1 | async-start | bytes 524288 | tf_op jit(solution)/shard_map/middle_move/all_to_all | solution.py:134
  43.4 33.4 %all_gather.3 = f32[128,4,128]{2,1,0:T(4,128)S(1)} all-gather(f32[16,4,128]{2,1,0:T(4,128)S(1)} %slice.4), channel_id=1, replica_groups=mesh['yh'=2,'core'=2,'yl'=2,'x'=4,'za'=8,'zb'=2] {'za'}, dimensions={0}, use_global_device_ids=true | all-gather | bytes 294912 | tf_op jit(solution)/shard_map/right_move/all_gather | solution.py:119
  76.8 0.1 copy.8
  77.0 0.0 all-to-all-done.1.parts_ref
  77.0 0.4 join.1
  77.4 21.4 %all_to_all.21 = f32[64,8,128]{2,1,0:T(8,128)S(1)} all-to-all(f32[64,8,128]{2,1,0:T(8,128)S(1)} %bitcast.14), channel_id=1, replica_groups=mesh['yh'=2,'core'=2,'yl'=2,'x'=4,'za'=8,'zb'=2] {'yh','core','yl','x','..., dimensions={0} | all-to-all | bytes 524288 | tf_op jit(solution)/shard_map/sum_move/all_to_all | solution.py:147
  98.8 0.1 reduce_sum.9
  98.9 18.7 %all_to_all.22 = f32[8,1,128]{2,1,0:T(1,128)S(1)} all-to-all(f32[8,1,128]{2,1,0:T(1,128)S(1)} %bitcast.20), channel_id=1, replica_groups=mesh['yh'=2,'core'=2,'yl'=2,'x'=4,'za'=8,'zb'=2] {'za'}, dimensions={0} | all-to-all | bytes 8192 | tf_op jit(solution)/shard_map/row_move/all_to_all | solution.py:151
  117.5 0.5 broadcast.12
  118.0 0.7 reduce.3
  118.7 0.1 reshape.38
  118.8 0.7 reshape.39
  (3 shorter events, 0.0 us)
Async XLA Ops:
  0.0 1.2 %copy-start = (f32[2,2,1,512,128]{4,3,2,1,0:T(8,128)S(1)}, f32[2,2,1,512,128]{4,3,2,1,0:T(8,128)}, u32[]{:S(2)}) copy-start(f32[2,2,1,512,128]{4,3,2,1,0:T(8,128)} %param.3) | copy-start | bytes 3145732
  1.2 0.8 copy-start.1
  3.3 22.1 %copy-start.2 = (f32[2,2,128,4]{2,3,1,0:T(4,128)S(1)}, f32[2,2,128,4]{2,3,1,0:T(4,128)}, u32[]{:S(2)}) copy-start(f32[2,2,128,4]{2,3,1,0:T(4,128)} %param.5) | copy-start | bytes 24580
  3.3 22.1 %all-to-all-start = ((f32[16,132,128]{2,1,0:T(8,128)}), f32[16,132,128]{2,1,0:T(8,128)S(1)}, u32[]{:S(2)}, u32[]{:S(2)}) async-start(f32[16,132,128]{2,1,0:T(8,128)} %pack.1), calls=%async_computation | async-start | bytes 2228224 | tf_op jit(solution)/shard_map/near_move/all_to_all | solution.py:116
  27.7 49.3 %all-to-all-start.1 = ((f32[8,64,128]{2,1,0:T(8,128)}), f32[8,64,128]{2,1,0:T(8,128)S(1)}, u32[]{:S(2)}, u32[]{:S(2)}) async-start(f32[8,64,128]{2,1,0:T(8,128)} %close.1), calls=%async_computation.1 | async-start | bytes 524288 | tf_op jit(solution)/shard_map/middle_move/all_to_all | solution.py:134

commit v3 on v2

--- a/solution.py
+++ b/solution.py
@@ -15,6 +15,9 @@
 F32 = jnp.float32
 LANES = 128
 GROUP = 16
+OTHERS = (0, 4, 2, 6)
+SMEM = pl.BlockSpec(memory_space=pltpu.SMEM)
+VMEM = pl.BlockSpec(memory_space=pltpu.VMEM)
 
 
 def swap_blocks(v):
@@ -81,15 +84,52 @@
                 out_ref[g, pl.ds(s * depth + kb * rows, rows), :] = w[g]
 
 
-def join_kernel(parts_ref, right_ref, out_ref):
+def join_kernel(far_ref, parts_ref, even_ref, odd_ref, out_ref):
     m = parts_ref[0]
     for i in range(1, parts_ref.shape[0]):
         m = m + parts_ref[i]
     turned = pltpu.roll(m, LANES // 2, 1)
     lane = lax.broadcasted_iota(jnp.int32, m.shape, 1)
     rhs = jnp.concatenate([m, jnp.where(lane < LANES // 2, -turned, turned)], axis=0)
-    out = jnp.dot(right_ref[...], rhs, precision=lax.Precision.HIGHEST, preferred_element_type=F32)
-    out_ref[...] = out
+
+    def times(ref):
+        out = jnp.dot(ref[...], rhs, precision=lax.Precision.HIGHEST, preferred_element_type=F32)
+        return out.reshape(4, 8, 8, LANES)
+
+    even, odd = times(even_ref), times(odd_ref)
+    here = far_ref[0]
+    straight = (here & 1) == 0
+    first = lax.broadcasted_iota(jnp.int32, even.shape[1:], 1) < 4
+    for i, other in enumerate(OTHERS):
+        low = jnp.where(straight, even[i], odd[i])
+        high = jnp.where(straight, odd[i], even[i])
+        top = jnp.where(first, low, pltpu.roll(high, 4, 1))
+        bottom = jnp.where(first, pltpu.roll(low, 4, 1), high)
+        at = (here ^ other) // 2
+        out_ref[:, at, :, 0:8, :] = top.reshape(4, 2, 8, LANES)
+        out_ref[:, at, :, 8:16, :] = bottom.reshape(4, 2, 8, LANES)
+
+
+def finish_kernel(parts_ref, out_ref):
+    w = swap_blocks([parts_ref[i] for i in range(parts_ref.shape[0])])
+    outs = out_ref.shape[0]
+    for c in range(2):
+        for o in range(outs):
+            out_ref[o, pl.ds(c, 1), :] = w[c * outs + o]
+
+
+def kernel_call(body, shape, specs, cost, name, scratch=(), vmem=16):
+    flops, size = cost
+    return pl.pallas_call(
+        body,
+        out_shape=jax.ShapeDtypeStruct(shape, F32),
+        in_specs=specs,
+        out_specs=VMEM,
+        scratch_shapes=scratch,
+        compiler_params=pltpu.CompilerParams(vmem_limit_bytes=vmem * 2**20),
+        cost_estimate=pl.CostEstimate(flops=flops, bytes_accessed=size, transcendentals=0),
+        name=name,
+    )
 
 
 def shards(left_tensor, right_tensor, closing_tensor):
@@ -98,58 +138,50 @@
     outs = closing_tensor.shape[3]
     near = 16
     kk = depth // near
+    body = slices * 2 * kk
     scale = 1.0 / jnp.sqrt(F32(slices * 4))
-
-    with jax.named_scope("pack"):
-        body = slices * 2 * kk
-        x = pl.pallas_call(
-            pack_kernel,
-            out_shape=jax.ShapeDtypeStruct((near, body + width, LANES), F32),
-            in_specs=[pl.BlockSpec(memory_space=pl.ANY), pl.BlockSpec(memory_space=pltpu.VMEM)],
-            out_specs=pl.BlockSpec(memory_space=pltpu.VMEM),
-            scratch_shapes=[pltpu.SemaphoreType.DMA((slices * 2,))],
-            compiler_params=pltpu.CompilerParams(vmem_limit_bytes=16 * 2**20),
-            cost_estimate=pl.CostEstimate(flops=0, bytes_accessed=2**21, transcendentals=0),
-        )(left_tensor.reshape(slices, 2, near, kk, rows), right_tensor.transpose(0, 1, 3, 2))
+    here = lax.axis_index(FAR).reshape(1)
+
+    x = kernel_call(
+        pack_kernel,
+        (near, body + width, LANES),
+        [pl.BlockSpec(memory_space=pltpu.HBM), VMEM],
+        (0, 2**21),
+        "pack",
+        [pltpu.SemaphoreType.DMA((slices * 2,))],
+        60,
+    )(left_tensor.reshape(slices, 2, near, kk, rows), right_tensor.transpose(0, 1, 3, 2))
 
     with jax.named_scope("near_move"):
         x = lax.all_to_all(x, NEAR, 0, 0, tiled=True)
 
     with jax.named_scope("right_move"):
-        r = lax.all_gather(x[:, body:], FAR, axis=0, tiled=True)
-        r = r.reshape(4, 2, 2, 4, 2, 2, 2, LANES)
-        r = r.transpose(2, 3, 0, 6, 1, 4, 5, 7).reshape(512, LANES)
-
-    with jax.named_scope("close"):
-        x = pl.pallas_call(
-            close_kernel,
-            out_shape=jax.ShapeDtypeStruct((8, slices * kk, LANES), F32),
-            in_specs=[pl.BlockSpec(memory_space=pltpu.SMEM)] * 2 + [pl.BlockSpec(memory_space=pltpu.VMEM)],
-            out_specs=pl.BlockSpec(memory_space=pltpu.VMEM),
-            compiler_params=pltpu.CompilerParams(vmem_limit_bytes=16 * 2**20),
-            cost_estimate=pl.CostEstimate(flops=2**22, bytes_accessed=5 * 2**18, transcendentals=0),
-        )(lax.axis_index(FAR).reshape(1), closing_tensor.transpose(0, 1, 3, 2), x)
+        r = x[:, body:].reshape(2, 2, 2, 2, 2, 2, LANES).transpose(1, 2, 5, 0, 3, 4, 6)
+        r = r.reshape(near * width, LANES)
+        for step in (4, 2):
+            r = jnp.concatenate([r, lax.ppermute(r, FAR, [(i, i ^ step) for i in range(8)])])
+        odd = lax.ppermute(r, FAR, [(i, i ^ 1) for i in range(8)])
+
+    x = kernel_call(
+        close_kernel, (8, slices * kk, LANES), [SMEM, SMEM, VMEM], (2**22, 5 * 2**18), "close"
+    )(here, closing_tensor.transpose(0, 1, 3, 2), x)
 
     with jax.named_scope("middle_move"):
         x = lax.all_to_all(x, FAR, 0, 0, tiled=True)
 
-    with jax.named_scope("join"):
-        p = pl.pallas_call(
-            join_kernel,
-            out_shape=jax.ShapeDtypeStruct((512, LANES), F32),
-            in_specs=[pl.BlockSpec(memory_space=pltpu.VMEM)] * 2,
-            out_specs=pl.BlockSpec(memory_space=pltpu.VMEM),
-            compiler_params=pltpu.CompilerParams(vmem_limit_bytes=16 * 2**20),
-            cost_estimate=pl.CostEstimate(flops=2**26, bytes_accessed=3 * 2**18, transcendentals=0),
-        )(x, r)
+    p = kernel_call(
+        join_kernel, (4, 4, 2, 16, LANES), [SMEM, VMEM, VMEM, VMEM], (2**26, 3 * 2**18), "join"
+    )(here, x, r, odd)
 
     with jax.named_scope("sum_move"):
-        p = lax.all_to_all(p.reshape(64, 8, LANES), CUTS + NEAR, 0, 0, tiled=True)
+        p = lax.all_to_all(p.reshape(32, 16, LANES), ("core",) + NEAR, 0, 0, tiled=True)
         p = jnp.sum(p, axis=0) * scale
 
     with jax.named_scope("row_move"):
-        p = lax.all_to_all(p, FAR, 0, 0, tiled=True)
-        p = p.reshape(8, 2, outs, GROUP).transpose(2, 1, 0, 3)
+        p = lax.all_to_all(p.reshape(16, 1, LANES), ("yh", FAR), 0, 0, tiled=True)
+        p = p[:8] + p[8:]
+
+    p = kernel_call(finish_kernel, (outs, 2, rows), [VMEM], (0, 2**13), "finish")(p)
     return p.reshape(1, outs, 2, rows)
 
 

time: 120 us -> 122 us (1.017)
  blocking collectives: 73.5 us -> 38.2 us
  waiting for transfers between devices: 14.8 us -> 36.7 us
  starting transfers between devices: 23 us -> 39.4 us
  local copies, waits for them, and re-layouts: 3.41 us -> 0.03 us
  Pallas kernels: 4.01 us -> 6.55 us
    all_gather x1 -> x0, blocking collectives: 33.4 us -> none  [shards(): r = lax.all_gather(x[:, body:], FAR, axis=0, tiled=True)]
    ppermute x0 -> x3, waiting for transfers between devices: none -> 21.9 us  [the longest x2 16.6 us: shards(): lax.ppermute(r, FAR, [(i, i ^ step) for i in range(8)])]
    ppermute x0 -> x3, starting transfers between devices: none -> 16.4 us  [the longest x2 14.4 us: shards(): lax.ppermute(r, FAR, [(i, i ^ step) for i in range(8)])]
    pallas_call x3 -> x4, Pallas kernels: 4.01 us -> 6.55 us  [the longest x1 2.97 us: shards(): kernel_call(pack_kernel, (near, body + width, LANES), [pl.BlockSpec(memor...]
    unnamed x6 -> x2, local copies, waits for them, and re-layouts: 1.99 us -> 0.01 us
    all_to_all x2, blocking collectives: 40 us -> 38.2 us  [the longest x1 19.5 us: shards(): p = lax.all_to_all(p.reshape(16, 1, LANES), ('yh', FAR), 0, 0, tiled=True)]
  transfers between devices with their start and end apart: 2 -> 5, of which waited for: 1 -> 4; matrix products, arithmetic and copies ran while one was open for 0% -> 0% of each run, Pallas kernels for 0% -> 0%
where the time goes in v3:
time: 122 us; the launch traced here: 121 us
  starting transfers between devices  39.4 us (32%)
  blocking collectives  38.2 us (31%)
  waiting for transfers between devices  36.7 us (30%)
  Pallas kernels  6.55 us (5%)
    all_to_all x1, blocking collectives, shards(): p = lax.all_to_all(p.reshape(16, 1, LANES), ('yh', FAR), 0, 0, tiled=True)  19.5 us
    all_to_all x1, blocking collectives, shards(): lax.all_to_all(p.reshape(32, 16, LANES), ('core',) + NEAR, 0, 0, tiled=True)  18.7 us
    ppermute x2, waiting for transfers between devices, shards(): lax.ppermute(r, FAR, [(i, i ^ step) for i in range(8)])  16.6 us
    all_to_all x1, starting transfers between devices, shards(): x = lax.all_to_all(x, FAR, 0, 0, tiled=True)  15.7 us
    all_to_all x1, waiting for transfers between devices, shards(): x = lax.all_to_all(x, NEAR, 0, 0, tiled=True)  14.8 us
    ppermute x2, starting transfers between devices, shards(): lax.ppermute(r, FAR, [(i, i ^ step) for i in range(8)])  14.4 us
    all_to_all x1, starting transfers between devices, shards(): x = lax.all_to_all(x, NEAR, 0, 0, tiled=True)  7.33 us
    ppermute x1, waiting for transfers between devices, shards(): odd = lax.ppermute(r, FAR, [(i, i ^ 1) for i in range(8)])  5.35 us
  transfers between devices with their start and end apart: 5, of which 4 were waited for; matrix products, arithmetic and copies ran while one was open for 0% of the time, Pallas kernels for 0%

profile of v3, /device:TPU:1, one launch (start us, length us, event | category | flops | bytes accessed | tf_op | source)
XLA Modules:
  0.0 121.0 jit_solution(3977843012884293357)
XLA Ops:
  0.0 3.0 %pack.1 = f32[16,132,128]{2,1,0:T(8,128)} custom-call(f32[2,2,16,32,128]{4,3,2,1,0:T(8,128)} %bitcast.13, f32[2,2,4,512]{3,2,1,0:T(4,128)} %bitcast.18), custom_call_target="tpu_custom_call" | custom-call | bytes 2097152 | tf_op jit(solution)/shard_map/pack/pallas_call | solution.py:145
  3.0 0.0 copy-start
  3.0 7.3 %all-to-all-start = ((f32[16,132,128]{2,1,0:T(8,128)}), f32[16,132,128]{2,1,0:T(8,128)S(1)}, u32[]{:S(2)}, u32[]{:S(2)}) async-start(f32[16,132,128]{2,1,0:T(8,128)} %pack.1), calls=%async_computation | async-start | bytes 2228224 | tf_op jit(solution)/shard_map/near_move/all_to_all | solution.py:156
  10.3 14.8 %all-to-all-done.left_ref = f32[16,132,128]{2,1,0:T(8,128)S(1)} async-done(((f32[16,132,128]{2,1,0:T(8,128)}), f32[16,132,128]{2,1,0:T(8,128)S(1)}, u32[]{:S(2)}, u32[]{:S(2)}) %all-to-all-start) | async-done | bytes 1081376 | tf_op jit(solution)/shard_map/near_move/all_to_all | solution.py:156
  25.1 0.0 copy-done
  25.1 2.3 %close.1 = f32[8,64,128]{2,1,0:T(8,128)} custom-call(s32[1]{0:T(128)} %bitcast.far_ref, f32[2,2,4,128]{3,2,1,0:T(4,128)S(1)} %bitcast.12, f32[16,132,128]{2,1,0:T(8,128)S(1)} %all-to-all-done.left_ref), custom_call_target="tpu_custom_call" | custom-call | flops 4194304 | bytes 1310720 | tf_op jit(solution)/shard_map/close/pallas_call | solution.py:165
  27.4 15.7 %all-to-all-start.1 = ((f32[8,64,128]{2,1,0:T(8,128)}), f32[8,64,128]{2,1,0:T(8,128)S(1)}, u32[]{:S(2)}, u32[]{:S(2)}) async-start(f32[8,64,128]{2,1,0:T(8,128)} %close.1), calls=%async_computation.1 | async-start | bytes 524288 | tf_op jit(solution)/shard_map/middle_move/all_to_all | solution.py:170
  43.2 12.1 %collective-permute-start = (f32[64,128]{1,0:T(8,128)S(1)}, f32[64,128]{1,0:T(8,128)S(1)}, u32[]{:S(2)}, u32[]{:S(2)}) collective-permute-start(f32[64,128]{1,0:T(8,128)S(1)} %bitcast.14), channel_id=1, source_target_pairs={{0,8},{2,10},{4,12},{6,14},{8,0},{10,2},{12,4},{14,6},{1,9},{3,11}... | collective-permute-start | bytes 98312 | tf_op jit(solution)/shard_map/right_move/ppermute | solution.py:162
  55.3 10.0 %collective-permute-done = f32[64,128]{1,0:T(8,128)S(1)} collective-permute-done((f32[64,128]{1,0:T(8,128)S(1)}, f32[64,128]{1,0:T(8,128)S(1)}, u32[]{:S(2)}, u32[]{:S(2)}) %collective-permute-start) | collective-permute-done | bytes 32800 | tf_op jit(solution)/shard_map/right_move/ppermute | solution.py:162
  65.3 2.4 %collective-permute-start.1 = (f32[128,128]{1,0:T(8,128)S(1)}, f32[128,128]{1,0:T(8,128)S(1)}, u32[]{:S(2)}, u32[]{:S(2)}) collective-permute-start(f32[128,128]{1,0:T(8,128)S(1)} %pad_maximum_fusion.1), channel_id=1, source_target_pairs={{0,4},{2,6},{4,0},{6,2},{8,12},{10,14},{12,8},{14,10},{1,5},{3,7},... | collective-permute-start | bytes 196616 | tf_op jit(solution)/shard_map/right_move/ppermute | solution.py:162
  67.7 6.5 %collective-permute-done.1 = f32[128,128]{1,0:T(8,128)S(1)} collective-permute-done((f32[128,128]{1,0:T(8,128)S(1)}, f32[128,128]{1,0:T(8,128)S(1)}, u32[]{:S(2)}, u32[]{:S(2)}) %collective-permute-start.1) | collective-permute-done | bytes 65568 | tf_op jit(solution)/shard_map/right_move/ppermute | solution.py:162
  74.2 1.9 %collective-permute-start.2 = (f32[256,128]{1,0:T(8,128)S(1)}, f32[256,128]{1,0:T(8,128)S(1)}, u32[]{:S(2)}, u32[]{:S(2)}) collective-permute-start(f32[256,128]{1,0:T(8,128)S(1)} %pad_maximum_fusion.even_ref), channel_id=1, source_target_pairs={{0,2},{2,0},{4,6},{6,4},{8,10},{10,8},{12,14},{14,12},{1,3},{3,1},... | collective-permute-start | bytes 393224 | tf_op jit(solution)/shard_map/right_move/ppermute | solution.py:163
  76.2 5.4 %collective-permute-done.2.odd_ref = f32[256,128]{1,0:T(8,128)S(1)} collective-permute-done((f32[256,128]{1,0:T(8,128)S(1)}, f32[256,128]{1,0:T(8,128)S(1)}, u32[]{:S(2)}, u32[]{:S(2)}) %collective-permute-start.2) | collective-permute-done | bytes 131104 | tf_op jit(solution)/shard_map/right_move/ppermute | solution.py:163
  81.5 0.0 all-to-all-done.1.parts_ref
  81.5 0.4 join.1
  82.0 18.7 %all_to_all.20 = f32[32,16,128]{2,1,0:T(8,128)S(1)} all-to-all(f32[32,16,128]{2,1,0:T(8,128)S(1)} %bitcast.11), channel_id=1, replica_groups=mesh['yh'=2,'core'=2,'yl'=2,'x'=4,'za'=8,'zb'=2] {'core','yl','x','zb'}, dimensions={0} | all-to-all | bytes 524288 | tf_op jit(solution)/shard_map/sum_move/all_to_all | solution.py:177
  100.7 19.5 %all_to_all.21 = f32[16,1,128]{2,1,0:T(1,128)S(1)} all-to-all(f32[16,1,128]{2,1,0:T(1,128)S(1)} %bitcast.19), channel_id=1, replica_groups=mesh['yh'=2,'core'=2,'yl'=2,'x'=4,'za'=8,'zb'=2] {'yh','za'}, dimensions={0} | all-to-all | bytes 16384 | tf_op jit(solution)/shard_map/row_move/all_to_all | solution.py:181
  120.2 0.8 finish.1
  (7 shorter events, 0.1 us)
Async XLA Ops:
  3.0 22.1 %copy-start = (f32[2,2,128,4]{2,3,1,0:T(4,128)S(1)}, f32[2,2,128,4]{2,3,1,0:T(4,128)}, u32[]{:S(2)}) copy-start(f32[2,2,128,4]{2,3,1,0:T(4,128)} %param.5) | copy-start | bytes 24580
  3.0 22.1 %all-to-all-start = ((f32[16,132,128]{2,1,0:T(8,128)}), f32[16,132,128]{2,1,0:T(8,128)S(1)}, u32[]{:S(2)}, u32[]{:S(2)}) async-start(f32[16,132,128]{2,1,0:T(8,128)} %pack.1), calls=%async_computation | async-start | bytes 2228224 | tf_op jit(solution)/shard_map/near_move/all_to_all | solution.py:156
  27.4 54.1 %all-to-all-start.1 = ((f32[8,64,128]{2,1,0:T(8,128)}), f32[8,64,128]{2,1,0:T(8,128)S(1)}, u32[]{:S(2)}, u32[]{:S(2)}) async-start(f32[8,64,128]{2,1,0:T(8,128)} %close.1), calls=%async_computation.1 | async-start | bytes 524288 | tf_op jit(solution)/shard_map/middle_move/all_to_all | solution.py:170
  43.2 22.1 %collective-permute-start = (f32[64,128]{1,0:T(8,128)S(1)}, f32[64,128]{1,0:T(8,128)S(1)}, u32[]{:S(2)}, u32[]{:S(2)}) collective-permute-start(f32[64,128]{1,0:T(8,128)S(1)} %bitcast.14), channel_id=1, source_target_pairs={{0,8},{2,10},{4,12},{6,14},{8,0},{10,2},{12,4},{14,6},{1,9},{3,11}... | collective-permute-start | bytes 98312 | tf_op jit(solution)/shard_map/right_move/ppermute | solution.py:162
  65.3 8.9 %collective-permute-start.1 = (f32[128,128]{1,0:T(8,128)S(1)}, f32[128,128]{1,0:T(8,128)S(1)}, u32[]{:S(2)}, u32[]{:S(2)}) collective-permute-start(f32[128,128]{1,0:T(8,128)S(1)} %pad_maximum_fusion.1), channel_id=1, source_target_pairs={{0,4},{2,6},{4,0},{6,2},{8,12},{10,14},{12,8},{14,10},{1,5},{3,7},... | collective-permute-start | bytes 196616 | tf_op jit(solution)/shard_map/right_move/ppermute | solution.py:162
  74.2 7.3 %collective-permute-start.2 = (f32[256,128]{1,0:T(8,128)S(1)}, f32[256,128]{1,0:T(8,128)S(1)}, u32[]{:S(2)}, u32[]{:S(2)}) collective-permute-start(f32[256,128]{1,0:T(8,128)S(1)} %pad_maximum_fusion.even_ref), channel_id=1, source_target_pairs={{0,2},{2,0},{4,6},{6,4},{8,10},{10,8},{12,14},{14,12},{1,3},{3,1},... | collective-permute-start | bytes 393224 | tf_op jit(solution)/shard_map/right_move/ppermute | solution.py:163

commit v4 on v3

--- a/solution.py
+++ b/solution.py
@@ -15,9 +15,9 @@
 F32 = jnp.float32
 LANES = 128
 GROUP = 16
-OTHERS = (0, 4, 2, 6)
 SMEM = pl.BlockSpec(memory_space=pltpu.SMEM)
 VMEM = pl.BlockSpec(memory_space=pltpu.VMEM)
+ANY = pl.BlockSpec(memory_space=pl.ANY)
 
 
 def swap_blocks(v):
@@ -38,7 +38,7 @@
     return v
 
 
-def pack_kernel(left_ref, right_ref, out_ref, sems):
+def pack_kernel(left_ref, right_ref, out_ref, held, sems):
     slices, _, near, depth, _ = left_ref.shape
     copies = []
     for i in range(2 * slices):
@@ -51,15 +51,27 @@
         lanes = pl.ds(t * LANES, LANES)
         w = swap_blocks([right_ref[j % slices, j // slices, :, lanes] for j in range(each)])
         for g in range(each):
-            out_ref[t * each + g, pl.ds(each * depth, width), :] = w[g]
+            held[t * each + g] = w[g]
+    to = out_ref.at[:, pl.ds(each * depth, width), :]
+    copies.append(pltpu.make_async_copy(held, to, sems.at[2 * slices]))
+    copies[-1].start()
     for copy in copies:
         copy.wait()
 
 
-def close_kernel(far_ref, coef_ref, left_ref, out_ref):
+def close_kernel(far_ref, coef_ref, left_ref, out_ref, held):
     heads = left_ref.shape[0]
     slices, _, outs, _ = coef_ref.shape
-    depth = out_ref.shape[1] // slices
+    body = left_ref.shape[1] - held.shape[0] // heads
+    depth = body // (2 * slices)
+    for q8 in range(2):
+        for q76 in range(4):
+            for q0 in range(2):
+                for q2 in range(2):
+                    two = left_ref[q8 * 8 + q76 * 2 + q2, pl.ds(body + q0, 2, stride=2), :]
+                    held[pl.ds(q76 * 16 + q0 * 8 + q8 * 4 + q2 * 2, 2), :] = two
+    for g in range(8):
+        out_ref[g, pl.ds(slices * depth, 64), :] = held[...]
     first = far_ref[0] * 2
     rows = 8
     for s in range(slices):
@@ -84,30 +96,24 @@
                 out_ref[g, pl.ds(s * depth + kb * rows, rows), :] = w[g]
 
 
-def join_kernel(far_ref, parts_ref, even_ref, odd_ref, out_ref):
-    m = parts_ref[0]
+def join_kernel(parts_ref, out_ref):
+    half = parts_ref.shape[1] // 2
+    m = parts_ref[0, :half, :]
     for i in range(1, parts_ref.shape[0]):
-        m = m + parts_ref[i]
+        m = m + parts_ref[i, :half, :]
     turned = pltpu.roll(m, LANES // 2, 1)
     lane = lax.broadcasted_iota(jnp.int32, m.shape, 1)
     rhs = jnp.concatenate([m, jnp.where(lane < LANES // 2, -turned, turned)], axis=0)
-
-    def times(ref):
-        out = jnp.dot(ref[...], rhs, precision=lax.Precision.HIGHEST, preferred_element_type=F32)
-        return out.reshape(4, 8, 8, LANES)
-
-    even, odd = times(even_ref), times(odd_ref)
-    here = far_ref[0]
-    straight = (here & 1) == 0
-    first = lax.broadcasted_iota(jnp.int32, even.shape[1:], 1) < 4
-    for i, other in enumerate(OTHERS):
-        low = jnp.where(straight, even[i], odd[i])
-        high = jnp.where(straight, odd[i], even[i])
+    right = parts_ref[:, half:, :].reshape(8 * half, LANES)
+    out = jnp.dot(right, rhs, precision=lax.Precision.HIGHEST, preferred_element_type=F32)
+    out = out.reshape(4, 2, 8, 8, LANES)
+    first = lax.broadcasted_iota(jnp.int32, (8, 8, LANES), 1) < 4
+    for i in range(4):
+        low, high = out[i, 0], out[i, 1]
         top = jnp.where(first, low, pltpu.roll(high, 4, 1))
         bottom = jnp.where(first, pltpu.roll(low, 4, 1), high)
-        at = (here ^ other) // 2
-        out_ref[:, at, :, 0:8, :] = top.reshape(4, 2, 8, LANES)
-        out_ref[:, at, :, 8:16, :] = bottom.reshape(4, 2, 8, LANES)
+        out_ref[:, i, :, 0:8, :] = top.reshape(4, 2, 8, LANES)
+        out_ref[:, i, :, 8:16, :] = bottom.reshape(4, 2, 8, LANES)
 
 
 def finish_kernel(parts_ref, out_ref):
@@ -118,13 +124,13 @@
             out_ref[o, pl.ds(c, 1), :] = w[c * outs + o]
 
 
-def kernel_call(body, shape, specs, cost, name, scratch=(), vmem=16):
+def kernel_call(body, shape, specs, cost, name, scratch=(), vmem=16, to=VMEM):
     flops, size = cost
     return pl.pallas_call(
         body,
         out_shape=jax.ShapeDtypeStruct(shape, F32),
         in_specs=specs,
-        out_specs=VMEM,
+        out_specs=to,
         scratch_shapes=scratch,
         compiler_params=pltpu.CompilerParams(vmem_limit_bytes=vmem * 2**20),
         cost_estimate=pl.CostEstimate(flops=flops, bytes_accessed=size, transcendentals=0),
@@ -145,33 +151,30 @@
     x = kernel_call(
         pack_kernel,
         (near, body + width, LANES),
-        [pl.BlockSpec(memory_space=pltpu.HBM), VMEM],
+        [ANY, VMEM],
         (0, 2**21),
         "pack",
-        [pltpu.SemaphoreType.DMA((slices * 2,))],
+        [pltpu.VMEM((near, width, LANES), F32), pltpu.SemaphoreType.DMA((slices * 2 + 1,))],
         60,
+        ANY,
     )(left_tensor.reshape(slices, 2, near, kk, rows), right_tensor.transpose(0, 1, 3, 2))
 
     with jax.named_scope("near_move"):
         x = lax.all_to_all(x, NEAR, 0, 0, tiled=True)
 
-    with jax.named_scope("right_move"):
-        r = x[:, body:].reshape(2, 2, 2, 2, 2, 2, LANES).transpose(1, 2, 5, 0, 3, 4, 6)
-        r = r.reshape(near * width, LANES)
-        for step in (4, 2):
-            r = jnp.concatenate([r, lax.ppermute(r, FAR, [(i, i ^ step) for i in range(8)])])
-        odd = lax.ppermute(r, FAR, [(i, i ^ 1) for i in range(8)])
-
     x = kernel_call(
-        close_kernel, (8, slices * kk, LANES), [SMEM, SMEM, VMEM], (2**22, 5 * 2**18), "close"
+        close_kernel,
+        (8, slices * kk + near * width, LANES),
+        [SMEM, SMEM, VMEM],
+        (2**22, 6 * 2**18),
+        "close",
+        [pltpu.VMEM((near * width, LANES), F32)],
     )(here, closing_tensor.transpose(0, 1, 3, 2), x)
 
-    with jax.named_scope("middle_move"):
+    with jax.named_scope("far_move"):
         x = lax.all_to_all(x, FAR, 0, 0, tiled=True)
 
-    p = kernel_call(
-        join_kernel, (4, 4, 2, 16, LANES), [SMEM, VMEM, VMEM, VMEM], (2**26, 3 * 2**18), "join"
-    )(here, x, r, odd)
+    p = kernel_call(join_kernel, (4, 4, 2, 16, LANES), [VMEM], (2**26, 3 * 2**18), "join")(x)
 
     with jax.named_scope("sum_move"):
         p = lax.all_to_all(p.reshape(32, 16, LANES), ("core",) + NEAR, 0, 0, tiled=True)

time: 122 us -> 138 us (1.13)
  blocking collectives: 38.2 us -> 78.8 us
  starting transfers between devices: 39.4 us -> 7.33 us
  Pallas kernels: 6.55 us -> 36.6 us
  waiting for transfers between devices: 36.7 us -> 14.8 us
    all_to_all x0 -> x1, blocking collectives: none -> 43.2 us  [shards(): x = lax.all_to_all(x, FAR, 0, 0, tiled=True)]
    pallas_call x3, Pallas kernels: 5.74 us -> 35.8 us  [the longest x1 33.7 us: shards(): kernel_call(pack_kernel, (near, body + width, LANES), [ANY, VMEM], (0, 2...]
    ppermute x3 -> x0, waiting for transfers between devices: 21.9 us -> none  [the longest x2 16.6 us: shards(): lax.ppermute(r, FAR, [(i, i ^ step) for i in range(8)])]
    ppermute x3 -> x0, starting transfers between devices: 16.4 us -> none  [the longest x2 14.4 us: shards(): lax.ppermute(r, FAR, [(i, i ^ step) for i in range(8)])]
    all_to_all x1 -> x0, starting transfers between devices: 15.7 us -> none  [shards(): x = lax.all_to_all(x, FAR, 0, 0, tiled=True)]
    all_to_all x1, blocking collectives: 18.7 us -> 16.7 us  [shards(): lax.all_to_all(p.reshape(32, 16, LANES), ('core',) + NEAR, 0, 0, tiled=True)]
  transfers between devices with their start and end apart: 5 -> 1, of which waited for: 4 -> 1; matrix products, arithmetic and copies ran while one was open for 0% -> 0% of each run, Pallas kernels for 0% -> 0%
where the time goes in v4:
time: 138 us
  blocking collectives  78.8 us (57%)
  Pallas kernels  36.6 us (27%)
  waiting for transfers between devices  14.8 us (11%)
  starting transfers between devices  7.33 us (5%)
    all_to_all x1, blocking collectives, shards(): x = lax.all_to_all(x, FAR, 0, 0, tiled=True)  43.2 us
    pallas_call x1, Pallas kernels, shards(): kernel_call(pack_kernel, (near, body + width, LANES), [ANY, VMEM], (0, 2...  33.7 us
    all_to_all x1, blocking collectives, shards(): p = lax.all_to_all(p.reshape(16, 1, LANES), ('yh', FAR), 0, 0, tiled=True)  18.8 us
    all_to_all x1, blocking collectives, shards(): lax.all_to_all(p.reshape(32, 16, LANES), ('core',) + NEAR, 0, 0, tiled=True)  16.7 us
    all_to_all x1, waiting for transfers between devices, shards(): x = lax.all_to_all(x, NEAR, 0, 0, tiled=True)  14.8 us
    all_to_all x1, starting transfers between devices, shards(): x = lax.all_to_all(x, NEAR, 0, 0, tiled=True)  7.33 us
  transfers between devices with their start and end apart: 1, of which 1 were waited for; matrix products, arithmetic and copies ran while one was open for 0% of the time, Pallas kernels for 0%

profile of v4, /device:TPU:1, one launch (start us, length us, event | category | flops | bytes accessed | tf_op | source)
XLA Modules:
  0.0 137.6 jit_solution(1348529043562918468)
XLA Ops:
  0.0 33.7 %pack.1 = f32[16,132,128]{2,1,0:T(8,128)} custom-call(f32[2,2,16,32,128]{4,3,2,1,0:T(8,128)} %bitcast.9, f32[2,2,4,512]{3,2,1,0:T(4,128)} %bitcast.10), custom_call_target="tpu_custom_call" | custom-call | bytes 2097152 | tf_op jit(solution)/shard_map/pack/pallas_call | solution.py:151
  33.7 0.0 copy-start
  33.7 7.3 %all-to-all-start = ((f32[16,132,128]{2,1,0:T(8,128)}), f32[16,132,128]{2,1,0:T(8,128)S(1)}, u32[]{:S(2)}, u32[]{:S(2)}) async-start(f32[16,132,128]{2,1,0:T(8,128)} %pack.1), calls=%async_computation | async-start | bytes 2228224 | tf_op jit(solution)/shard_map/near_move/all_to_all | solution.py:163
  41.0 14.8 %all-to-all-done.left_ref = f32[16,132,128]{2,1,0:T(8,128)S(1)} async-done(((f32[16,132,128]{2,1,0:T(8,128)}), f32[16,132,128]{2,1,0:T(8,128)S(1)}, u32[]{:S(2)}, u32[]{:S(2)}) %all-to-all-start) | async-done | bytes 1081376 | tf_op jit(solution)/shard_map/near_move/all_to_all | solution.py:163
  55.8 0.0 copy-done
  55.8 1.7 %close.1 = f32[8,128,128]{2,1,0:T(8,128)S(1)} custom-call(s32[1]{0:T(128)} %bitcast.far_ref, f32[2,2,4,128]{3,2,1,0:T(4,128)S(1)} %bitcast.8, f32[16,132,128]{2,1,0:T(8,128)S(1)} %all-to-all-done.left_ref), custom_call_target="tpu_custom_call" | custom-call | flops 4194304 | bytes 1572864 | tf_op jit(solution)/shard_map/close/pallas_call | solution.py:165
  57.5 43.2 %all_to_all.20.parts_ref = f32[8,128,128]{2,1,0:T(8,128)S(1)} all-to-all(f32[8,128,128]{2,1,0:T(8,128)S(1)} %close.1), channel_id=1, replica_groups=mesh['yh'=2,'core'=2,'yl'=2,'x'=4,'za'=8,'zb'=2] {'za'}, dimensions={0} | all-to-all | bytes 1048576 | tf_op jit(solution)/shard_map/far_move/all_to_all | solution.py:175
  100.7 0.4 join.1
  101.2 16.7 %all_to_all.21 = f32[32,16,128]{2,1,0:T(8,128)S(1)} all-to-all(f32[32,16,128]{2,1,0:T(8,128)S(1)} %bitcast.7), channel_id=1, replica_groups=mesh['yh'=2,'core'=2,'yl'=2,'x'=4,'za'=8,'zb'=2] {'core','yl','x','zb'}, dimensions={0} | all-to-all | bytes 524288 | tf_op jit(solution)/shard_map/sum_move/all_to_all | solution.py:180
  118.0 18.8 %all_to_all.22 = f32[16,1,128]{2,1,0:T(1,128)S(1)} all-to-all(f32[16,1,128]{2,1,0:T(1,128)S(1)} %bitcast.11), channel_id=1, replica_groups=mesh['yh'=2,'core'=2,'yl'=2,'x'=4,'za'=8,'zb'=2] {'yh','za'}, dimensions={0} | all-to-all | bytes 16384 | tf_op jit(solution)/shard_map/row_move/all_to_all | solution.py:184
  136.8 0.8 finish.1
  (3 shorter events, 0.0 us)
Async XLA Ops:
  33.7 22.1 %copy-start = (f32[2,2,128,4]{2,3,1,0:T(4,128)S(1)}, f32[2,2,128,4]{2,3,1,0:T(4,128)}, u32[]{:S(2)}) copy-start(f32[2,2,128,4]{2,3,1,0:T(4,128)} %param.5) | copy-start | bytes 24580
  33.7 22.1 %all-to-all-start = ((f32[16,132,128]{2,1,0:T(8,128)}), f32[16,132,128]{2,1,0:T(8,128)S(1)}, u32[]{:S(2)}, u32[]{:S(2)}) async-start(f32[16,132,128]{2,1,0:T(8,128)} %pack.1), calls=%async_computation | async-start | bytes 2228224 | tf_op jit(solution)/shard_map/near_move/all_to_all | solution.py:163

commit v5 on v4

--- a/solution.py
+++ b/solution.py
@@ -38,24 +38,28 @@
     return v
 
 
-def pack_kernel(left_ref, right_ref, out_ref, held, sems):
+def pack_kernel(left_ref, right_ref, out_ref, held, piece, into, out_of):
     slices, _, near, depth, _ = left_ref.shape
+    each = 2 * slices
     copies = []
-    for i in range(2 * slices):
-        to = out_ref.at[:, pl.ds(i * depth, depth), :]
-        copies.append(pltpu.make_async_copy(left_ref.at[i // 2, i % 2], to, sems.at[i]))
+    for i in range(each):
+        copies.append(pltpu.make_async_copy(left_ref.at[i // 2, i % 2], held.at[i], into.at[i]))
         copies[-1].start()
     width = right_ref.shape[2]
-    each = 2 * slices
     for t in range(near // each):
         lanes = pl.ds(t * LANES, LANES)
         w = swap_blocks([right_ref[j % slices, j // slices, :, lanes] for j in range(each)])
         for g in range(each):
-            held[t * each + g] = w[g]
+            piece[t * each + g] = w[g]
     to = out_ref.at[:, pl.ds(each * depth, width), :]
-    copies.append(pltpu.make_async_copy(held, to, sems.at[2 * slices]))
-    copies[-1].start()
-    for copy in copies:
+    last = [pltpu.make_async_copy(piece, to, out_of.at[each])]
+    last[0].start()
+    for i in range(each):
+        copies[i].wait()
+        to = out_ref.at[:, pl.ds(i * depth, depth), :]
+        last.append(pltpu.make_async_copy(held.at[i], to, out_of.at[i]))
+        last[-1].start()
+    for copy in last:
         copy.wait()
 
 
@@ -154,7 +158,12 @@
         [ANY, VMEM],
         (0, 2**21),
         "pack",
-        [pltpu.VMEM((near, width, LANES), F32), pltpu.SemaphoreType.DMA((slices * 2 + 1,))],
+        [
+            pltpu.VMEM((slices * 2, near, kk, rows), F32),
+            pltpu.VMEM((near, width, LANES), F32),
+            pltpu.SemaphoreType.DMA((slices * 2,)),
+            pltpu.SemaphoreType.DMA((slices * 2 + 1,)),
+        ],
         60,
         ANY,
     )(left_tensor.reshape(slices, 2, near, kk, rows), right_tensor.transpose(0, 1, 3, 2))

time: 138 us -> 107 us (0.78)
  Pallas kernels: 36.6 us -> 5.73 us
    pallas_call x1, Pallas kernels: 33.7 us -> 2.78 us  [shards(): kernel_call(pack_kernel, (near, body + width, LANES), [ANY, VMEM], (0, 2...]
where the time goes in v5:
time: 107 us
  blocking collectives  78.8 us (74%)
  waiting for transfers between devices  14.8 us (14%)
  starting transfers between devices  7.33 us (7%)
  Pallas kernels  5.73 us (5%)
    all_to_all x1, blocking collectives, shards(): x = lax.all_to_all(x, FAR, 0, 0, tiled=True)  43.2 us
    all_to_all x1, blocking collectives, shards(): p = lax.all_to_all(p.reshape(16, 1, LANES), ('yh', FAR), 0, 0, tiled=True)  18.8 us
    all_to_all x1, blocking collectives, shards(): lax.all_to_all(p.reshape(32, 16, LANES), ('core',) + NEAR, 0, 0, tiled=True)  16.7 us
    all_to_all x1, waiting for transfers between devices, shards(): x = lax.all_to_all(x, NEAR, 0, 0, tiled=True)  14.8 us
    all_to_all x1, starting transfers between devices, shards(): x = lax.all_to_all(x, NEAR, 0, 0, tiled=True)  7.33 us
    pallas_call x1, Pallas kernels, shards(): kernel_call(pack_kernel, (near, body + width, LANES), [ANY, VMEM], (0, 2...  2.78 us
  transfers between devices with their start and end apart: 1, of which 1 were waited for; matrix products, arithmetic and copies ran while one was open for 0% of the time, Pallas kernels for 0%

profile of v5, /device:TPU:1, one launch (start us, length us, event | category | flops | bytes accessed | tf_op | source)
XLA Modules:
  0.0 106.7 jit_solution(18304543710773000658)
XLA Ops:
  0.0 2.8 %pack.1 = f32[16,132,128]{2,1,0:T(8,128)} custom-call(f32[2,2,16,32,128]{4,3,2,1,0:T(8,128)} %bitcast.9, f32[2,2,4,512]{3,2,1,0:T(4,128)} %bitcast.10), custom_call_target="tpu_custom_call" | custom-call | bytes 2097152 | tf_op jit(solution)/shard_map/pack/pallas_call | solution.py:155
  2.8 0.0 copy-start
  2.8 7.3 %all-to-all-start = ((f32[16,132,128]{2,1,0:T(8,128)}), f32[16,132,128]{2,1,0:T(8,128)S(1)}, u32[]{:S(2)}, u32[]{:S(2)}) async-start(f32[16,132,128]{2,1,0:T(8,128)} %pack.1), calls=%async_computation | async-start | bytes 2228224 | tf_op jit(solution)/shard_map/near_move/all_to_all | solution.py:172
  10.1 14.8 %all-to-all-done.left_ref = f32[16,132,128]{2,1,0:T(8,128)S(1)} async-done(((f32[16,132,128]{2,1,0:T(8,128)}), f32[16,132,128]{2,1,0:T(8,128)S(1)}, u32[]{:S(2)}, u32[]{:S(2)}) %all-to-all-start) | async-done | bytes 1081376 | tf_op jit(solution)/shard_map/near_move/all_to_all | solution.py:172
  24.9 0.0 copy-done
  24.9 1.7 %close.1 = f32[8,128,128]{2,1,0:T(8,128)S(1)} custom-call(s32[1]{0:T(128)} %bitcast.far_ref, f32[2,2,4,128]{3,2,1,0:T(4,128)S(1)} %bitcast.8, f32[16,132,128]{2,1,0:T(8,128)S(1)} %all-to-all-done.left_ref), custom_call_target="tpu_custom_call" | custom-call | flops 4194304 | bytes 1572864 | tf_op jit(solution)/shard_map/close/pallas_call | solution.py:174
  26.6 43.2 %all_to_all.20.parts_ref = f32[8,128,128]{2,1,0:T(8,128)S(1)} all-to-all(f32[8,128,128]{2,1,0:T(8,128)S(1)} %close.1), channel_id=1, replica_groups=mesh['yh'=2,'core'=2,'yl'=2,'x'=4,'za'=8,'zb'=2] {'za'}, dimensions={0} | all-to-all | bytes 1048576 | tf_op jit(solution)/shard_map/far_move/all_to_all | solution.py:184
  69.8 0.4 join.1
  70.3 16.7 %all_to_all.21 = f32[32,16,128]{2,1,0:T(8,128)S(1)} all-to-all(f32[32,16,128]{2,1,0:T(8,128)S(1)} %bitcast.7), channel_id=1, replica_groups=mesh['yh'=2,'core'=2,'yl'=2,'x'=4,'za'=8,'zb'=2] {'core','yl','x','zb'}, dimensions={0} | all-to-all | bytes 524288 | tf_op jit(solution)/shard_map/sum_move/all_to_all | solution.py:189
  87.1 18.8 %all_to_all.22 = f32[16,1,128]{2,1,0:T(1,128)S(1)} all-to-all(f32[16,1,128]{2,1,0:T(1,128)S(1)} %bitcast.11), channel_id=1, replica_groups=mesh['yh'=2,'core'=2,'yl'=2,'x'=4,'za'=8,'zb'=2] {'yh','za'}, dimensions={0} | all-to-all | bytes 16384 | tf_op jit(solution)/shard_map/row_move/all_to_all | solution.py:193
  105.9 0.8 finish.1
  (3 shorter events, 0.0 us)
Async XLA Ops:
  2.8 22.1 %copy-start = (f32[2,2,128,4]{2,3,1,0:T(4,128)S(1)}, f32[2,2,128,4]{2,3,1,0:T(4,128)}, u32[]{:S(2)}) copy-start(f32[2,2,128,4]{2,3,1,0:T(4,128)} %param.5) | copy-start | bytes 24580
  2.8 22.1 %all-to-all-start = ((f32[16,132,128]{2,1,0:T(8,128)}), f32[16,132,128]{2,1,0:T(8,128)S(1)}, u32[]{:S(2)}, u32[]{:S(2)}) async-start(f32[16,132,128]{2,1,0:T(8,128)} %pack.1), calls=%async_computation | async-start | bytes 2228224 | tf_op jit(solution)/shard_map/near_move/all_to_all | solution.py:172

commit v6 on v5

--- a/solution.py
+++ b/solution.py
@@ -1,3 +1,5 @@
+import functools
+
 import jax
 import jax.numpy as jnp
 from jax import lax
@@ -14,7 +16,6 @@
 
 F32 = jnp.float32
 LANES = 128
-GROUP = 16
 SMEM = pl.BlockSpec(memory_space=pltpu.SMEM)
 VMEM = pl.BlockSpec(memory_space=pltpu.VMEM)
 ANY = pl.BlockSpec(memory_space=pl.ANY)
@@ -63,19 +64,25 @@
         copy.wait()
 
 
-def close_kernel(far_ref, coef_ref, left_ref, out_ref, held):
+def spread_kernel(near_ref, out_ref):
+    heads = near_ref.shape[0]
+    body = near_ref.shape[1] - out_ref.shape[2] * 2 // heads
+    for q7 in range(2):
+        for q6 in range(2):
+            for q0 in range(2):
+                for q8 in range(2):
+                    for q2 in range(2):
+                        two = near_ref[q8 * 8 + q7 * 4 + q6 * 2 + q2, pl.ds(body + q0, 2, stride=2), :]
+                        out_ref[q7, 0, pl.ds(q6 * 16 + q0 * 8 + q8 * 4 + q2 * 2, 2), :] = two
+    for q7 in range(2):
+        for g in range(1, out_ref.shape[1]):
+            out_ref[q7, g] = out_ref[q7, 0]
+
+
+def close_kernel(far_ref, coef_ref, left_ref, out_ref):
     heads = left_ref.shape[0]
     slices, _, outs, _ = coef_ref.shape
-    body = left_ref.shape[1] - held.shape[0] // heads
-    depth = body // (2 * slices)
-    for q8 in range(2):
-        for q76 in range(4):
-            for q0 in range(2):
-                for q2 in range(2):
-                    two = left_ref[q8 * 8 + q76 * 2 + q2, pl.ds(body + q0, 2, stride=2), :]
-                    held[pl.ds(q76 * 16 + q0 * 8 + q8 * 4 + q2 * 2, 2), :] = two
-    for g in range(8):
-        out_ref[g, pl.ds(slices * depth, 64), :] = held[...]
+    depth = out_ref.shape[0] // slices
     first = far_ref[0] * 2
     rows = 8
     for s in range(slices):
@@ -95,37 +102,50 @@
                         new_re, new_im = acc[o][kb] + new_re, acc[outs + o][kb] + new_im
                     acc[o][kb], acc[outs + o][kb] = new_re, new_im
         for kb in range(depth // rows):
-            w = swap_blocks([acc[j][kb] for j in range(2 * outs)])
-            for g in range(8):
-                out_ref[g, pl.ds(s * depth + kb * rows, rows), :] = w[g]
-
-
-def join_kernel(parts_ref, out_ref):
-    half = parts_ref.shape[1] // 2
-    m = parts_ref[0, :half, :]
+            for j in range(2 * outs):
+                out_ref[pl.ds(s * depth + kb * rows, rows), pl.ds(j * LANES, LANES)] = acc[j][kb]
+
+
+def join_kernel(core_ref, right_ref, mine_ref, other_ref, out_ref, lhs, rhs):
+    depth, wide = mine_ref.shape
+    half = wide // 2
+    first = lax.broadcasted_iota(jnp.int32, (8, LANES), 0) < 4
+    for i, x_ref in enumerate((mine_ref, other_ref)):
+        core = core_ref[0] ^ i
+        for t in range(4):
+            for q6 in range(2):
+                for q0 in range(2):
+                    at = pl.ds((q6 * 2 + q0) * 8, 8)
+                    low, high = right_ref[core, 2 * t, at, :], right_ref[core, 2 * t + 1, at, :]
+                    to = (q6 * 8 + t * 2 + q0) * 16
+                    lanes = pl.ds(i * LANES, LANES)
+                    lhs[pl.ds(to, 8), lanes] = jnp.where(first, low, pltpu.roll(high, 4, 0))
+                    lhs[pl.ds(to + 8, 8), lanes] = jnp.where(first, pltpu.roll(low, 4, 0), high)
+        rhs[pl.ds(2 * i * depth, depth), :] = x_ref[...]
+        rhs[pl.ds((2 * i + 1) * depth, depth), :half] = -x_ref[:, half:]
+        rhs[pl.ds((2 * i + 1) * depth, depth), half:] = x_ref[:, :half]
+    for j in range(wide // LANES):
+        right = rhs[:, pl.ds(j * LANES, LANES)]
+        out = jnp.dot(lhs[...], right, precision=lax.Precision.HIGHEST, preferred_element_type=F32)
+        out_ref[:, j, :, :] = out.reshape(16, 16, LANES)
+
+
+def sum_kernel(scale, parts_ref, out_ref):
+    for j in range(parts_ref.shape[1]):
+        total = parts_ref[0, j]
+        for i in range(1, parts_ref.shape[0]):
+            total = total + parts_ref[i, j]
+        out_ref[:, j, :] = total * scale
+
+
+def finish_kernel(parts_ref, out_ref):
+    total = parts_ref[0]
     for i in range(1, parts_ref.shape[0]):
-        m = m + parts_ref[i, :half, :]
-    turned = pltpu.roll(m, LANES // 2, 1)
-    lane = lax.broadcasted_iota(jnp.int32, m.shape, 1)
-    rhs = jnp.concatenate([m, jnp.where(lane < LANES // 2, -turned, turned)], axis=0)
-    right = parts_ref[:, half:, :].reshape(8 * half, LANES)
-    out = jnp.dot(right, rhs, precision=lax.Precision.HIGHEST, preferred_element_type=F32)
-    out = out.reshape(4, 2, 8, 8, LANES)
-    first = lax.broadcasted_iota(jnp.int32, (8, 8, LANES), 1) < 4
-    for i in range(4):
-        low, high = out[i, 0], out[i, 1]
-        top = jnp.where(first, low, pltpu.roll(high, 4, 1))
-        bottom = jnp.where(first, pltpu.roll(low, 4, 1), high)
-        out_ref[:, i, :, 0:8, :] = top.reshape(4, 2, 8, LANES)
-        out_ref[:, i, :, 8:16, :] = bottom.reshape(4, 2, 8, LANES)
-
-
-def finish_kernel(parts_ref, out_ref):
-    w = swap_blocks([parts_ref[i] for i in range(parts_ref.shape[0])])
+        total = total + parts_ref[i]
     outs = out_ref.shape[0]
     for c in range(2):
         for o in range(outs):
-            out_ref[o, pl.ds(c, 1), :] = w[c * outs + o]
+            out_ref[o, pl.ds(c, 1), :] = total[c * outs + o : c * outs + o + 1, :]
 
 
 def kernel_call(body, shape, specs, cost, name, scratch=(), vmem=16, to=VMEM):
@@ -149,7 +169,6 @@
     near = 16
     kk = depth // near
     body = slices * 2 * kk
-    scale = 1.0 / jnp.sqrt(F32(slices * 4))
     here = lax.axis_index(FAR).reshape(1)
 
     x = kernel_call(
@@ -171,29 +190,45 @@
     with jax.named_scope("near_move"):
         x = lax.all_to_all(x, NEAR, 0, 0, tiled=True)
 
+    r = kernel_call(spread_kernel, (2, 8, near * width // 2, LANES), [VMEM], (0, 2**18), "spread")(x)
+    with jax.named_scope("right_move"):
+        r = r.reshape(16, near * width // 2, LANES)
+        r = lax.all_to_all(r, ("core", FAR), 0, 0, tiled=True)
+        r = r.reshape(2, 8, near * width // 2, LANES)
+
     x = kernel_call(
         close_kernel,
-        (8, slices * kk + near * width, LANES),
+        (slices * kk, 2 * outs * rows),
         [SMEM, SMEM, VMEM],
         (2**22, 6 * 2**18),
         "close",
-        [pltpu.VMEM((near * width, LANES), F32)],
     )(here, closing_tensor.transpose(0, 1, 3, 2), x)
-
-    with jax.named_scope("far_move"):
-        x = lax.all_to_all(x, FAR, 0, 0, tiled=True)
-
-    p = kernel_call(join_kernel, (4, 4, 2, 16, LANES), [VMEM], (2**26, 3 * 2**18), "join")(x)
+    with jax.named_scope("core_swap"):
+        y = lax.ppermute(x, "core", [(0, 1), (1, 0)])
+
+    wide = 2 * outs * rows
+    p = kernel_call(
+        join_kernel,
+        (near, 2 * outs, 16, rows),
+        [SMEM, VMEM, VMEM, VMEM],
+        (2**27, 2**21),
+        "join",
+        [pltpu.VMEM((256, 2 * LANES), F32), pltpu.VMEM((4 * slices * kk, wide), F32)],
+    )(lax.axis_index("core").reshape(1), r, x, y)
 
     with jax.named_scope("sum_move"):
-        p = lax.all_to_all(p.reshape(32, 16, LANES), ("core",) + NEAR, 0, 0, tiled=True)
-        p = jnp.sum(p, axis=0) * scale
-
-    with jax.named_scope("row_move"):
-        p = lax.all_to_all(p.reshape(16, 1, LANES), ("yh", FAR), 0, 0, tiled=True)
-        p = p[:8] + p[8:]
-
-    p = kernel_call(finish_kernel, (outs, 2, rows), [VMEM], (0, 2**13), "finish")(p)
+        p = lax.all_to_all(p, NEAR, 0, 0, tiled=True)
+    p = kernel_call(
+        functools.partial(sum_kernel, (slices * 4) ** -0.5),
+        (16, 2 * outs, rows),
+        [VMEM],
+        (2**18, 2**20),
+        "sum",
+    )(p)
+
+    with jax.named_scope("last_move"):
+        p = lax.all_to_all(p, ("yh", FAR), 0, 0, tiled=True)
+    p = kernel_call(finish_kernel, (outs, 2, rows), [VMEM], (2**14, 2**17), "finish")(p)
     return p.reshape(1, outs, 2, rows)
 
 

time: 107 us -> 105 us (0.981); the launches traced: 107 us -> 103 us
  blocking collectives: 78.8 us -> 60.7 us
  starting transfers between devices: 7.33 us -> 20.9 us
  Pallas kernels: 5.73 us -> 7.41 us
    all_to_all x3, blocking collectives: 78.8 us -> 60.7 us  [the longest x1 23.3 us: shards(): p = lax.all_to_all(p, ('yh', FAR), 0, 0, tiled=True)]
    all_to_all x1, starting transfers between devices: 7.33 us -> 18.9 us  [shards(): r = lax.all_to_all(r, ('core', FAR), 0, 0, tiled=True)]
    all_to_all x1, waiting for transfers between devices: 14.8 us -> 12.5 us  [shards(): r = lax.all_to_all(r, ('core', FAR), 0, 0, tiled=True)]
    ppermute x0 -> x1, starting transfers between devices: none -> 2.01 us  [shards(): y = lax.ppermute(x, 'core', [(0, 1), (1, 0)])]
    pallas_call x3 -> x5, Pallas kernels: 2.95 us -> 4.62 us  [the longest x1 1.8 us: shards(): kernel_call(join_kernel, (near, 2 * outs, 16, rows), [SMEM, VMEM, VMEM, V...]
    ppermute x0 -> x1, waiting for transfers between devices: none -> 1.4 us  [shards(): y = lax.ppermute(x, 'core', [(0, 1), (1, 0)])]
  transfers between devices with their start and end apart: 1 -> 2, of which waited for: 1 -> 2; matrix products, arithmetic and copies ran while one was open for 0% -> 0% of each run, Pallas kernels for 0% -> 1%
where the time goes in v6:
time: 105 us; the launch traced here: 103 us
  blocking collectives  60.7 us (58%)
  starting transfers between devices  20.9 us (20%)
  waiting for transfers between devices  13.9 us (13%)
  Pallas kernels  7.41 us (7%)
    all_to_all x1, blocking collectives, shards(): p = lax.all_to_all(p, ('yh', FAR), 0, 0, tiled=True)  23.3 us
    all_to_all x1, blocking collectives, shards(): x = lax.all_to_all(x, NEAR, 0, 0, tiled=True)  20.9 us
    all_to_all x1, starting transfers between devices, shards(): r = lax.all_to_all(r, ('core', FAR), 0, 0, tiled=True)  18.9 us
    all_to_all x1, blocking collectives, shards(): p = lax.all_to_all(p, NEAR, 0, 0, tiled=True)  16.5 us
    all_to_all x1, waiting for transfers between devices, shards(): r = lax.all_to_all(r, ('core', FAR), 0, 0, tiled=True)  12.5 us
    pallas_call x1, Pallas kernels, shards(): kernel_call(pack_kernel, (near, body + width, LANES), [ANY, VMEM], (0, 2...  2.78 us
  transfers between devices with their start and end apart: 2, of which 2 were waited for; matrix products, arithmetic and copies ran while one was open for 0% of the time, Pallas kernels for 1%

profile of v6, /device:TPU:1, one launch (start us, length us, event | category | flops | bytes accessed | tf_op | source)
XLA Modules:
  0.0 103.0 jit_solution(775324818991134799)
XLA Ops:
  0.0 2.8 %pack.1 = f32[16,132,128]{2,1,0:T(8,128)} custom-call(f32[2,2,16,32,128]{4,3,2,1,0:T(8,128)} %bitcast.10, f32[2,2,4,512]{3,2,1,0:T(4,128)} %bitcast.11), custom_call_target="tpu_custom_call" | custom-call | bytes 2097152 | tf_op jit(solution)/shard_map/pack/pallas_call | solution.py:174
  2.8 20.9 %all_to_all.20.near_ref.left_ref = f32[16,132,128]{2,1,0:T(8,128)S(1)} all-to-all(f32[16,132,128]{2,1,0:T(8,128)} %pack.1), channel_id=1, replica_groups=mesh['yh'=2,'core'=2,'yl'=2,'x'=4,'za'=8,'zb'=2] {'yl','x','zb'}, dimensions={0} | all-to-all | bytes 2162688 | tf_op jit(solution)/shard_map/near_move/all_to_all | solution.py:191
  23.7 0.0 copy-start
  23.7 0.7 spread.1
  24.5 18.9 %all-to-all-start.1 = ((f32[16,32,128]{2,1,0:T(8,128)}), f32[16,32,128]{2,1,0:T(8,128)S(1)}, u32[]{:S(2)}, u32[]{:S(2)}) async-start(f32[16,32,128]{2,1,0:T(8,128)} %bitcast.3), calls=%async_computation.1 | async-start | bytes 524288 | tf_op jit(solution)/shard_map/right_move/all_to_all | solution.py:196
  43.4 0.0 copy-done
  43.4 1.4 %close.1.mine_ref = f32[64,1024]{1,0:T(8,128)S(1)} custom-call(s32[1]{0:T(128)} %bitcast.5.far_ref, f32[2,2,4,128]{3,2,1,0:T(4,128)S(1)} %bitcast.9, f32[16,132,128]{2,1,0:T(8,128)S(1)} %all_to_all.20.near_ref.left_ref), custom_call_target="tpu_custom_call" | custom-call | flops 4194304 | bytes 1572864 | tf_op jit(solution)/shard_map/close/pallas_call | solution.py:199
  44.8 2.0 %collective-permute-start = (f32[64,1024]{1,0:T(8,128)S(1)}, f32[64,1024]{1,0:T(8,128)S(1)}, u32[]{:S(2)}, u32[]{:S(2)}) collective-permute-start(f32[64,1024]{1,0:T(8,128)S(1)} %close.1.mine_ref), channel_id=1, source_target_pairs={{0,128},{128,0},{1,129},{129,1},{2,130},{130,2},{3,131},{131,3},{4... | collective-permute-start | bytes 786440 | tf_op jit(solution)/shard_map/core_swap/ppermute | solution.py:207
  46.8 1.4 %collective-permute-done.other_ref = f32[64,1024]{1,0:T(8,128)S(1)} collective-permute-done((f32[64,1024]{1,0:T(8,128)S(1)}, f32[64,1024]{1,0:T(8,128)S(1)}, u32[]{:S(2)}, u32[]{:S(2)}) %collective-permute-start) | collective-permute-done | bytes 262176 | tf_op jit(solution)/shard_map/core_swap/ppermute | solution.py:207
  48.2 12.5 %all-to-all-done.1 = f32[16,32,128]{2,1,0:T(8,128)S(1)} async-done(((f32[16,32,128]{2,1,0:T(8,128)}), f32[16,32,128]{2,1,0:T(8,128)S(1)}, u32[]{:S(2)}, u32[]{:S(2)}) %all-to-all-start.1) | async-done | bytes 262176 | tf_op jit(solution)/shard_map/right_move/all_to_all | solution.py:196
  60.7 1.8 %join.1 = f32[16,8,16,128]{3,2,1,0:T(8,128)S(1)} custom-call(s32[1]{0:T(128)} %bitcast.core_ref, f32[2,8,32,128]{3,2,1,0:T(8,128)S(1)} %bitcast.8, f32[64,1024]{1,0:T(8,128)S(1)} %close.1.mine_ref, f32[64,1024]{1,0:T(8,128)S(1)} %collective-permute-done.other_ref), custom_call_target="tpu_custom_call" | custom-call | flops 134217728 | bytes 2097152 | tf_op jit(solution)/shard_map/join/pallas_call | solution.py:210
  62.5 16.5 %all_to_all.21.parts_ref = f32[16,8,16,128]{3,2,1,0:T(8,128)S(1)} all-to-all(f32[16,8,16,128]{3,2,1,0:T(8,128)S(1)} %join.1), channel_id=1, replica_groups=mesh['yh'=2,'core'=2,'yl'=2,'x'=4,'za'=8,'zb'=2] {'yl','x','zb'}, dimensions={0} | all-to-all | bytes 2097152 | tf_op jit(solution)/shard_map/sum_move/all_to_all | solution.py:220
  79.0 0.1 sum.1
  79.1 23.3 %all_to_all.22.parts_ref = f32[16,8,128]{2,1,0:T(8,128)S(1)} all-to-all(f32[16,8,128]{2,1,0:T(8,128)S(1)} %sum.1), channel_id=1, replica_groups=mesh['yh'=2,'core'=2,'yl'=2,'x'=4,'za'=8,'zb'=2] {'yh','za'}, dimensions={0} | all-to-all | bytes 131072 | tf_op jit(solution)/shard_map/last_move/all_to_all | solution.py:230
  102.3 0.6 finish.1
Async XLA Ops:
  23.7 19.7 %copy-start = (f32[2,2,128,4]{2,3,1,0:T(4,128)S(1)}, f32[2,2,128,4]{2,3,1,0:T(4,128)}, u32[]{:S(2)}) copy-start(f32[2,2,128,4]{2,3,1,0:T(4,128)} %param.5) | copy-start | bytes 24580
  24.5 36.3 %all-to-all-start.1 = ((f32[16,32,128]{2,1,0:T(8,128)}), f32[16,32,128]{2,1,0:T(8,128)S(1)}, u32[]{:S(2)}, u32[]{:S(2)}) async-start(f32[16,32,128]{2,1,0:T(8,128)} %bitcast.3), calls=%async_computation.1 | async-start | bytes 524288 | tf_op jit(solution)/shard_map/right_move/all_to_all | solution.py:196
  44.8 3.4 %collective-permute-start = (f32[64,1024]{1,0:T(8,128)S(1)}, f32[64,1024]{1,0:T(8,128)S(1)}, u32[]{:S(2)}, u32[]{:S(2)}) collective-permute-start(f32[64,1024]{1,0:T(8,128)S(1)} %close.1.mine_ref), channel_id=1, source_target_pairs={{0,128},{128,0},{1,129},{129,1},{2,130},{130,2},{3,131},{131,3},{4... | collective-permute-start | bytes 786440 | tf_op jit(solution)/shard_map/core_swap/ppermute | solution.py:207

commit v7 on v6

--- a/solution.py
+++ b/solution.py
@@ -65,18 +65,16 @@
 
 
 def spread_kernel(near_ref, out_ref):
-    heads = near_ref.shape[0]
-    body = near_ref.shape[1] - out_ref.shape[2] * 2 // heads
-    for q7 in range(2):
+    cuts, far, width, _ = out_ref.shape
+    body = near_ref.shape[1] - cuts * width // near_ref.shape[0]
+    for q87 in range(cuts):
         for q6 in range(2):
             for q0 in range(2):
-                for q8 in range(2):
-                    for q2 in range(2):
-                        two = near_ref[q8 * 8 + q7 * 4 + q6 * 2 + q2, pl.ds(body + q0, 2, stride=2), :]
-                        out_ref[q7, 0, pl.ds(q6 * 16 + q0 * 8 + q8 * 4 + q2 * 2, 2), :] = two
-    for q7 in range(2):
-        for g in range(1, out_ref.shape[1]):
-            out_ref[q7, g] = out_ref[q7, 0]
+                for q2 in range(2):
+                    two = near_ref[q87 * 4 + q6 * 2 + q2, pl.ds(body + q0, 2, stride=2), :]
+                    out_ref[q87, 0, pl.ds(q6 * 8 + q0 * 4 + q2 * 2, 2), :] = two
+        for g in range(1, far):
+            out_ref[q87, g] = out_ref[q87, 0]
 
 
 def close_kernel(far_ref, coef_ref, left_ref, out_ref):
@@ -106,28 +104,28 @@
                 out_ref[pl.ds(s * depth + kb * rows, rows), pl.ds(j * LANES, LANES)] = acc[j][kb]
 
 
-def join_kernel(core_ref, right_ref, mine_ref, other_ref, out_ref, lhs, rhs):
-    depth, wide = mine_ref.shape
+def join_kernel(cut_ref, right_ref, x0_ref, x1_ref, x2_ref, x3_ref, out_ref, lhs, rhs):
+    depth, wide = x0_ref.shape
     half = wide // 2
     first = lax.broadcasted_iota(jnp.int32, (8, LANES), 0) < 4
-    for i, x_ref in enumerate((mine_ref, other_ref)):
-        core = core_ref[0] ^ i
+    for i, x_ref in enumerate((x0_ref, x1_ref, x2_ref, x3_ref)):
+        cut = cut_ref[0] ^ i
+        lanes = pl.ds(i * LANES, LANES)
         for t in range(4):
             for q6 in range(2):
-                for q0 in range(2):
-                    at = pl.ds((q6 * 2 + q0) * 8, 8)
-                    low, high = right_ref[core, 2 * t, at, :], right_ref[core, 2 * t + 1, at, :]
-                    to = (q6 * 8 + t * 2 + q0) * 16
-                    lanes = pl.ds(i * LANES, LANES)
-                    lhs[pl.ds(to, 8), lanes] = jnp.where(first, low, pltpu.roll(high, 4, 0))
-                    lhs[pl.ds(to + 8, 8), lanes] = jnp.where(first, pltpu.roll(low, 4, 0), high)
+                at = pl.ds(q6 * 8, 8)
+                low, high = right_ref[cut, 2 * t, at, :], right_ref[cut, 2 * t + 1, at, :]
+                to = (q6 * 8 + t * 2) * 8
+                lhs[pl.ds(to, 8), lanes] = jnp.where(first, low, pltpu.roll(high, 4, 0))
+                lhs[pl.ds(to + 8, 8), lanes] = jnp.where(first, pltpu.roll(low, 4, 0), high)
         rhs[pl.ds(2 * i * depth, depth), :] = x_ref[...]
         rhs[pl.ds((2 * i + 1) * depth, depth), :half] = -x_ref[:, half:]
         rhs[pl.ds((2 * i + 1) * depth, depth), half:] = x_ref[:, :half]
-    for j in range(wide // LANES):
-        right = rhs[:, pl.ds(j * LANES, LANES)]
+    for j in range(0, wide // LANES, 2):
+        right = rhs[:, pl.ds(j * LANES, 2 * LANES)]
         out = jnp.dot(lhs[...], right, precision=lax.Precision.HIGHEST, preferred_element_type=F32)
-        out_ref[:, j, :, :] = out.reshape(16, 16, LANES)
+        out_ref[:, j, :, :] = out[:, :LANES].reshape(16, 8, LANES)
+        out_ref[:, j + 1, :, :] = out[:, LANES:].reshape(16, 8, LANES)
 
 
 def sum_kernel(scale, parts_ref, out_ref):
@@ -190,11 +188,14 @@
     with jax.named_scope("near_move"):
         x = lax.all_to_all(x, NEAR, 0, 0, tiled=True)
 
-    r = kernel_call(spread_kernel, (2, 8, near * width // 2, LANES), [VMEM], (0, 2**18), "spread")(x)
+    cuts = 4
+    r = kernel_call(
+        spread_kernel, (cuts, 8, near * width // cuts, LANES), [VMEM], (0, 2**18), "spread"
+    )(x)
     with jax.named_scope("right_move"):
-        r = r.reshape(16, near * width // 2, LANES)
-        r = lax.all_to_all(r, ("core", FAR), 0, 0, tiled=True)
-        r = r.reshape(2, 8, near * width // 2, LANES)
+        r = r.reshape(cuts * 8, near * width // cuts, LANES)
+        r = lax.all_to_all(r, CUTS + (FAR,), 0, 0, tiled=True)
+        r = r.reshape(cuts, 8, near * width // cuts, LANES)
 
     x = kernel_call(
         close_kernel,
@@ -203,31 +204,34 @@
         (2**22, 6 * 2**18),
         "close",
     )(here, closing_tensor.transpose(0, 1, 3, 2), x)
-    with jax.named_scope("core_swap"):
-        y = lax.ppermute(x, "core", [(0, 1), (1, 0)])
+    swap = [(0, 1), (1, 0)]
+    with jax.named_scope("cuts_gather"):
+        x2 = lax.ppermute(x, "yh", swap)
+        x1 = lax.ppermute(x, "core", swap)
+        x3 = lax.ppermute(x2, "core", swap)
 
     wide = 2 * outs * rows
     p = kernel_call(
         join_kernel,
-        (near, 2 * outs, 16, rows),
-        [SMEM, VMEM, VMEM, VMEM],
+        (near, 2 * outs, 8, rows),
+        [SMEM] + [VMEM] * 5,
         (2**27, 2**21),
         "join",
-        [pltpu.VMEM((256, 2 * LANES), F32), pltpu.VMEM((4 * slices * kk, wide), F32)],
-    )(lax.axis_index("core").reshape(1), r, x, y)
+        [pltpu.VMEM((128, cuts * LANES), F32), pltpu.VMEM((2 * cuts * slices * kk, wide), F32)],
+    )(lax.axis_index(CUTS).reshape(1), r, x, x1, x2, x3)
 
     with jax.named_scope("sum_move"):
         p = lax.all_to_all(p, NEAR, 0, 0, tiled=True)
     p = kernel_call(
-        functools.partial(sum_kernel, (slices * 4) ** -0.5),
-        (16, 2 * outs, rows),
+        functools.partial(sum_kernel, (slices * cuts) ** -0.5),
+        (8, 2 * outs, rows),
         [VMEM],
         (2**18, 2**20),
         "sum",
     )(p)
 
     with jax.named_scope("last_move"):
-        p = lax.all_to_all(p, ("yh", FAR), 0, 0, tiled=True)
+        p = lax.all_to_all(p, FAR, 0, 0, tiled=True)
     p = kernel_call(finish_kernel, (outs, 2, rows), [VMEM], (2**14, 2**17), "finish")(p)
     return p.reshape(1, outs, 2, rows)
 

time: 105 us -> 102 us (0.971)
  starting transfers between devices: 20.9 us -> 31.7 us
  blocking collectives: 60.7 us -> 54 us
  waiting for transfers between devices: 13.9 us -> 8.04 us
    all_to_all x1, waiting for transfers between devices: 12.5 us -> 1.83 us  [shards(): r = lax.all_to_all(r, CUTS + (FAR,), 0, 0, tiled=True)]
    ppermute x1 -> x3, starting transfers between devices: 2.01 us -> 10.3 us  [the longest x1 4.82 us: shards(): x2 = lax.ppermute(x, 'yh', swap)]
    all_to_all x1, blocking collectives: 16.5 us -> 11.6 us  [shards(): p = lax.all_to_all(p, NEAR, 0, 0, tiled=True)]
    ppermute x1 -> x3, waiting for transfers between devices: 1.4 us -> 6.2 us  [the longest x1 5.08 us: shards(): x2 = lax.ppermute(x, 'yh', swap)]
    all_to_all x1, starting transfers between devices: 18.9 us -> 21.4 us  [shards(): r = lax.all_to_all(r, CUTS + (FAR,), 0, 0, tiled=True)]
    all_to_all x1, blocking collectives: 23.3 us -> 21.4 us  [shards(): p = lax.all_to_all(p, FAR, 0, 0, tiled=True)]
  transfers between devices with their start and end apart: 2 -> 4, of which waited for: 2 -> 3; matrix products, arithmetic and copies ran while one was open for 0% -> 0% of each run, Pallas kernels for 1% -> 1%
where the time goes in v7:
time: 102 us; the launch traced here: 100 us
  blocking collectives  54 us (53%)
  starting transfers between devices  31.7 us (31%)
  waiting for transfers between devices  8.04 us (8%)
  Pallas kernels  6.68 us (7%)
    all_to_all x1, blocking collectives, shards(): p = lax.all_to_all(p, FAR, 0, 0, tiled=True)  21.4 us
    all_to_all x1, starting transfers between devices, shards(): r = lax.all_to_all(r, CUTS + (FAR,), 0, 0, tiled=True)  21.4 us
    all_to_all x1, blocking collectives, shards(): x = lax.all_to_all(x, NEAR, 0, 0, tiled=True)  20.9 us
    all_to_all x1, blocking collectives, shards(): p = lax.all_to_all(p, NEAR, 0, 0, tiled=True)  11.6 us
    ppermute x1, waiting for transfers between devices, shards(): x2 = lax.ppermute(x, 'yh', swap)  5.08 us
    ppermute x1, starting transfers between devices, shards(): x2 = lax.ppermute(x, 'yh', swap)  4.82 us
    ppermute x1, starting transfers between devices, shards(): x3 = lax.ppermute(x2, 'core', swap)  2.92 us
    pallas_call x1, Pallas kernels, shards(): kernel_call(pack_kernel, (near, body + width, LANES), [ANY, VMEM], (0, 2...  2.77 us
  transfers between devices with their start and end apart: 4, of which 3 were waited for; matrix products, arithmetic and copies ran while one was open for 0% of the time, Pallas kernels for 1%

profile of v7, /device:TPU:1, one launch (start us, length us, event | category | flops | bytes accessed | tf_op | source)
XLA Modules:
  0.0 100.5 jit_solution(14678058895408742656)
XLA Ops:
  0.0 2.8 %pack.1 = f32[16,132,128]{2,1,0:T(8,128)} custom-call(f32[2,2,16,32,128]{4,3,2,1,0:T(8,128)} %bitcast.10, f32[2,2,4,512]{3,2,1,0:T(4,128)} %bitcast.11), custom_call_target="tpu_custom_call" | custom-call | bytes 2097152 | tf_op jit(solution)/shard_map/pack/pallas_call | solution.py:172
  2.8 20.9 %all_to_all.20.near_ref.left_ref = f32[16,132,128]{2,1,0:T(8,128)S(1)} all-to-all(f32[16,132,128]{2,1,0:T(8,128)} %pack.1), channel_id=1, replica_groups=mesh['yh'=2,'core'=2,'yl'=2,'x'=4,'za'=8,'zb'=2] {'yl','x','zb'}, dimensions={0} | all-to-all | bytes 2162688 | tf_op jit(solution)/shard_map/near_move/all_to_all | solution.py:189
  23.7 0.0 copy-start
  23.7 0.7 spread.1
  24.4 21.4 %all-to-all-start.1 = ((f32[32,16,128]{2,1,0:T(8,128)}), f32[32,16,128]{2,1,0:T(8,128)S(1)}, u32[]{:S(2)}, u32[]{:S(2)}) async-start(f32[32,16,128]{2,1,0:T(8,128)} %bitcast.3), calls=%async_computation.1 | async-start | bytes 524288 | tf_op jit(solution)/shard_map/right_move/all_to_all | solution.py:197
  45.9 0.0 copy-done
  45.9 1.4 %close.1.x0_ref = f32[64,1024]{1,0:T(8,128)S(1)} custom-call(s32[1]{0:T(128)} %bitcast.5.far_ref, f32[2,2,4,128]{3,2,1,0:T(4,128)S(1)} %bitcast.9, f32[16,132,128]{2,1,0:T(8,128)S(1)} %all_to_all.20.near_ref.left_ref), custom_call_target="tpu_custom_call" | custom-call | flops 4194304 | bytes 1572864 | tf_op jit(solution)/shard_map/close/pallas_call | solution.py:200
  47.3 4.8 %collective-permute-start.1 = (f32[64,1024]{1,0:T(8,128)S(1)}, f32[64,1024]{1,0:T(8,128)S(1)}, u32[]{:S(2)}, u32[]{:S(2)}) collective-permute-start(f32[64,1024]{1,0:T(8,128)S(1)} %close.1.x0_ref), channel_id=1, source_target_pairs={{0,256},{256,0},{1,257},{257,1},{2,258},{258,2},{3,259},{259,3},{4... | collective-permute-start | bytes 786440 | tf_op jit(solution)/shard_map/cuts_gather/ppermute | solution.py:209
  52.1 2.5 %collective-permute-start = (f32[64,1024]{1,0:T(8,128)S(1)}, f32[64,1024]{1,0:T(8,128)S(1)}, u32[]{:S(2)}, u32[]{:S(2)}) collective-permute-start(f32[64,1024]{1,0:T(8,128)S(1)} %close.1.x0_ref), channel_id=1, source_target_pairs={{0,128},{128,0},{1,129},{129,1},{2,130},{130,2},{3,131},{131,3},{4... | collective-permute-start | bytes 786440 | tf_op jit(solution)/shard_map/cuts_gather/ppermute | solution.py:210
  54.6 5.1 %collective-permute-done.1.x2_ref = f32[64,1024]{1,0:T(8,128)S(1)} collective-permute-done((f32[64,1024]{1,0:T(8,128)S(1)}, f32[64,1024]{1,0:T(8,128)S(1)}, u32[]{:S(2)}, u32[]{:S(2)}) %collective-permute-start.1) | collective-permute-done | bytes 262176 | tf_op jit(solution)/shard_map/cuts_gather/ppermute | solution.py:209
  59.7 2.9 %collective-permute-start.2 = (f32[64,1024]{1,0:T(8,128)S(1)}, f32[64,1024]{1,0:T(8,128)S(1)}, u32[]{:S(2)}, u32[]{:S(2)}) collective-permute-start(f32[64,1024]{1,0:T(8,128)S(1)} %collective-permute-done.1.x2_ref), channel_id=1, source_target_pairs={{0,128},{128,0},{1,129},{129,1},{2,130},{130,2},{3,131},{131,3},{4... | collective-permute-start | bytes 786440 | tf_op jit(solution)/shard_map/cuts_gather/ppermute | solution.py:211
  62.7 0.0 collective-permute-done.x1_ref
  62.7 1.1 %collective-permute-done.2.x3_ref = f32[64,1024]{1,0:T(8,128)S(1)} collective-permute-done((f32[64,1024]{1,0:T(8,128)S(1)}, f32[64,1024]{1,0:T(8,128)S(1)}, u32[]{:S(2)}, u32[]{:S(2)}) %collective-permute-start.2) | collective-permute-done | bytes 262176 | tf_op jit(solution)/shard_map/cuts_gather/ppermute | solution.py:211
  63.8 1.8 %all-to-all-done.1 = f32[32,16,128]{2,1,0:T(8,128)S(1)} async-done(((f32[32,16,128]{2,1,0:T(8,128)}), f32[32,16,128]{2,1,0:T(8,128)S(1)}, u32[]{:S(2)}, u32[]{:S(2)}) %all-to-all-start.1) | async-done | bytes 262176 | tf_op jit(solution)/shard_map/right_move/all_to_all | solution.py:197
  65.6 1.1 %join.1 = f32[16,8,8,128]{3,2,1,0:T(8,128)S(1)} custom-call(s32[1]{0:T(128)} %bitcast.cut_ref, f32[4,8,16,128]{3,2,1,0:T(8,128)S(1)} %bitcast.8, f32[64,1024]{1,0:T(8,128)S(1)} %close.1.x0_ref, f32[64,1024]{1,0:T(8,128)S(1)} %collective-permute-done.x1_ref, f32[64,1024]{1,0:T(8,128)S(1)} %collective-permute-done.1.x2_ref, ...), custom_call_target="tpu_custom_call" | custom-call | flops 134217728 | bytes 2097152 | tf_op jit(solution)/shard_map/join/pallas_call | solution.py:214
  66.8 11.6 %all_to_all.21.parts_ref = f32[16,8,8,128]{3,2,1,0:T(8,128)S(1)} all-to-all(f32[16,8,8,128]{3,2,1,0:T(8,128)S(1)} %join.1), channel_id=1, replica_groups=mesh['yh'=2,'core'=2,'yl'=2,'x'=4,'za'=8,'zb'=2] {'yl','x','zb'}, dimensions={0} | all-to-all | bytes 1048576 | tf_op jit(solution)/shard_map/sum_move/all_to_all | solution.py:224
  78.4 21.4 %all_to_all.22.parts_ref = f32[8,8,128]{2,1,0:T(8,128)S(1)} all-to-all(f32[8,8,128]{2,1,0:T(8,128)S(1)} %sum.1), channel_id=1, replica_groups=mesh['yh'=2,'core'=2,'yl'=2,'x'=4,'za'=8,'zb'=2] {'za'}, dimensions={0} | all-to-all | bytes 65536 | tf_op jit(solution)/shard_map/last_move/all_to_all | solution.py:234
  99.9 0.6 finish.1
  (1 shorter events, 0.0 us)
Async XLA Ops:
  23.7 22.2 %copy-start = (f32[2,2,128,4]{2,3,1,0:T(4,128)S(1)}, f32[2,2,128,4]{2,3,1,0:T(4,128)}, u32[]{:S(2)}) copy-start(f32[2,2,128,4]{2,3,1,0:T(4,128)} %param.5) | copy-start | bytes 24580
  24.4 41.2 %all-to-all-start.1 = ((f32[32,16,128]{2,1,0:T(8,128)}), f32[32,16,128]{2,1,0:T(8,128)S(1)}, u32[]{:S(2)}, u32[]{:S(2)}) async-start(f32[32,16,128]{2,1,0:T(8,128)} %bitcast.3), calls=%async_computation.1 | async-start | bytes 524288 | tf_op jit(solution)/shard_map/right_move/all_to_all | solution.py:197
  47.3 12.4 %collective-permute-start.1 = (f32[64,1024]{1,0:T(8,128)S(1)}, f32[64,1024]{1,0:T(8,128)S(1)}, u32[]{:S(2)}, u32[]{:S(2)}) collective-permute-start(f32[64,1024]{1,0:T(8,128)S(1)} %close.1.x0_ref), channel_id=1, source_target_pairs={{0,256},{256,0},{1,257},{257,1},{2,258},{258,2},{3,259},{259,3},{4... | collective-permute-start | bytes 786440 | tf_op jit(solution)/shard_map/cuts_gather/ppermute | solution.py:209
  52.1 10.6 %collective-permute-start = (f32[64,1024]{1,0:T(8,128)S(1)}, f32[64,1024]{1,0:T(8,128)S(1)}, u32[]{:S(2)}, u32[]{:S(2)}) collective-permute-start(f32[64,1024]{1,0:T(8,128)S(1)} %close.1.x0_ref), channel_id=1, source_target_pairs={{0,128},{128,0},{1,129},{129,1},{2,130},{130,2},{3,131},{131,3},{4... | collective-permute-start | bytes 786440 | tf_op jit(solution)/shard_map/cuts_gather/ppermute | solution.py:210
  59.7 4.1 %collective-permute-start.2 = (f32[64,1024]{1,0:T(8,128)S(1)}, f32[64,1024]{1,0:T(8,128)S(1)}, u32[]{:S(2)}, u32[]{:S(2)}) collective-permute-start(f32[64,1024]{1,0:T(8,128)S(1)} %collective-permute-done.1.x2_ref), channel_id=1, source_target_pairs={{0,128},{128,0},{1,129},{129,1},{2,130},{130,2},{3,131},{131,3},{4... | collective-permute-start | bytes 786440 | tf_op jit(solution)/shard_map/cuts_gather/ppermute | solution.py:211

commit v8 on v7

--- a/solution.py
+++ b/solution.py
@@ -16,6 +16,8 @@
 
 F32 = jnp.float32
 LANES = 128
+MID = 5
+LAST = 4
 SMEM = pl.BlockSpec(memory_space=pltpu.SMEM)
 VMEM = pl.BlockSpec(memory_space=pltpu.VMEM)
 ANY = pl.BlockSpec(memory_space=pl.ANY)
@@ -114,7 +116,8 @@
         for t in range(4):
             for q6 in range(2):
                 at = pl.ds(q6 * 8, 8)
-                low, high = right_ref[cut, 2 * t, at, :], right_ref[cut, 2 * t + 1, at, :]
+                low = right_ref[cut, (2 * t - MID) % 8, at, :]
+                high = right_ref[cut, (2 * t + 1 - MID) % 8, at, :]
                 to = (q6 * 8 + t * 2) * 8
                 lhs[pl.ds(to, 8), lanes] = jnp.where(first, low, pltpu.roll(high, 4, 0))
                 lhs[pl.ds(to + 8, 8), lanes] = jnp.where(first, pltpu.roll(low, 4, 0), high)
@@ -133,7 +136,7 @@
         total = parts_ref[0, j]
         for i in range(1, parts_ref.shape[0]):
             total = total + parts_ref[i, j]
-        out_ref[:, j, :] = total * scale
+        out_ref[:, j, :] = pltpu.roll(total * scale, (8 - LAST) % 8, 0)
 
 
 def finish_kernel(parts_ref, out_ref):
@@ -194,7 +197,8 @@
     )(x)
     with jax.named_scope("right_move"):
         r = r.reshape(cuts * 8, near * width // cuts, LANES)
-        r = lax.all_to_all(r, CUTS + (FAR,), 0, 0, tiled=True)
+        group = [c * 8 + (f + MID) % 8 for c in range(cuts) for f in range(8)]
+        r = lax.all_to_all(r, CUTS + (FAR,), 0, 0, tiled=True, axis_index_groups=[group])
         r = r.reshape(cuts, 8, near * width // cuts, LANES)
 
     x = kernel_call(
@@ -231,7 +235,8 @@
     )(p)
 
     with jax.named_scope("last_move"):
-        p = lax.all_to_all(p, FAR, 0, 0, tiled=True)
+        group = [(f + LAST) % 8 for f in range(8)]
+        p = lax.all_to_all(p, FAR, 0, 0, tiled=True, axis_index_groups=[group])
     p = kernel_call(finish_kernel, (outs, 2, rows), [VMEM], (2**14, 2**17), "finish")(p)
     return p.reshape(1, outs, 2, rows)
 

time: 102 us -> 93.7 us (0.919)
  blocking collectives: 54 us -> 46.7 us
  waiting for transfers between devices: 8.04 us -> 6.1 us
  starting transfers between devices: 31.7 us -> 32.8 us
    all_to_all x1, blocking collectives: 21.4 us -> 14.1 us  [shards(): p = lax.all_to_all(p, FAR, 0, 0, tiled=True, axis_index_groups=[group])]
    all_to_all x1, waiting for transfers between devices: 1.83 us -> 0.01 us  [shards(): lax.all_to_all(r, CUTS + (FAR,), 0, 0, tiled=True, axis_index_groups=[gro...]
    all_to_all x1, starting transfers between devices: 21.4 us -> 22.5 us  [shards(): lax.all_to_all(r, CUTS + (FAR,), 0, 0, tiled=True, axis_index_groups=[gro...]
  transfers between devices with their start and end apart: 4 -> 4, of which waited for: 3 -> 2; matrix products, arithmetic and copies ran while one was open for 0% -> 0% of each run, Pallas kernels for 1% -> 2%
where the time goes in v8:
time: 93.7 us; the launch traced here: 92.3 us
  blocking collectives  46.7 us (50%)
  starting transfers between devices  32.8 us (35%)
  Pallas kernels  6.68 us (7%)
  waiting for transfers between devices  6.1 us (7%)
    all_to_all x1, starting transfers between devices, shards(): lax.all_to_all(r, CUTS + (FAR,), 0, 0, tiled=True, axis_index_groups=[gro...  22.5 us
    all_to_all x1, blocking collectives, shards(): x = lax.all_to_all(x, NEAR, 0, 0, tiled=True)  20.9 us
    all_to_all x1, blocking collectives, shards(): p = lax.all_to_all(p, FAR, 0, 0, tiled=True, axis_index_groups=[group])  14.1 us
    all_to_all x1, blocking collectives, shards(): p = lax.all_to_all(p, NEAR, 0, 0, tiled=True)  11.6 us
    ppermute x1, waiting for transfers between devices, shards(): x2 = lax.ppermute(x, 'yh', swap)  4.97 us
    ppermute x1, starting transfers between devices, shards(): x2 = lax.ppermute(x, 'yh', swap)  4.63 us
    ppermute x1, starting transfers between devices, shards(): x3 = lax.ppermute(x2, 'core', swap)  3.1 us
    pallas_call x1, Pallas kernels, shards(): kernel_call(pack_kernel, (near, body + width, LANES), [ANY, VMEM], (0, 2...  2.77 us
  transfers between devices with their start and end apart: 4, of which 2 were waited for; matrix products, arithmetic and copies ran while one was open for 0% of the time, Pallas kernels for 2%

profile of v8, /device:TPU:1, one launch (start us, length us, event | category | flops | bytes accessed | tf_op | source)
XLA Modules:
  0.0 92.3 jit_solution(5981911736288672642)
XLA Ops:
  0.0 2.8 %pack.1 = f32[16,132,128]{2,1,0:T(8,128)} custom-call(f32[2,2,16,32,128]{4,3,2,1,0:T(8,128)} %bitcast.10, f32[2,2,4,512]{3,2,1,0:T(4,128)} %bitcast.11), custom_call_target="tpu_custom_call" | custom-call | bytes 2097152 | tf_op jit(solution)/shard_map/pack/pallas_call | solution.py:175
  2.8 20.9 %all_to_all.20.near_ref.left_ref = f32[16,132,128]{2,1,0:T(8,128)S(1)} all-to-all(f32[16,132,128]{2,1,0:T(8,128)} %pack.1), channel_id=1, replica_groups=mesh['yh'=2,'core'=2,'yl'=2,'x'=4,'za'=8,'zb'=2] {'yl','x','zb'}, dimensions={0} | all-to-all | bytes 2162688 | tf_op jit(solution)/shard_map/near_move/all_to_all | solution.py:192
  23.7 0.0 copy-start
  23.7 0.7 spread.1
  24.4 22.5 %all-to-all-start.1 = ((f32[32,16,128]{2,1,0:T(8,128)}), f32[32,16,128]{2,1,0:T(8,128)S(1)}, u32[]{:S(2)}, u32[]{:S(2)}) async-start(f32[32,16,128]{2,1,0:T(8,128)} %bitcast.3), calls=%async_computation.1 | async-start | bytes 524288 | tf_op jit(solution)/shard_map/right_move/all_to_all | solution.py:201
  47.0 0.0 copy-done
  47.0 1.4 %close.1.x0_ref = f32[64,1024]{1,0:T(8,128)S(1)} custom-call(s32[1]{0:T(128)} %bitcast.5.far_ref, f32[2,2,4,128]{3,2,1,0:T(4,128)S(1)} %bitcast.9, f32[16,132,128]{2,1,0:T(8,128)S(1)} %all_to_all.20.near_ref.left_ref), custom_call_target="tpu_custom_call" | custom-call | flops 4194304 | bytes 1572864 | tf_op jit(solution)/shard_map/close/pallas_call | solution.py:204
  48.4 4.6 %collective-permute-start.1 = (f32[64,1024]{1,0:T(8,128)S(1)}, f32[64,1024]{1,0:T(8,128)S(1)}, u32[]{:S(2)}, u32[]{:S(2)}) collective-permute-start(f32[64,1024]{1,0:T(8,128)S(1)} %close.1.x0_ref), channel_id=1, source_target_pairs={{0,256},{256,0},{1,257},{257,1},{2,258},{258,2},{3,259},{259,3},{4... | collective-permute-start | bytes 786440 | tf_op jit(solution)/shard_map/cuts_gather/ppermute | solution.py:213
  53.0 2.5 %collective-permute-start = (f32[64,1024]{1,0:T(8,128)S(1)}, f32[64,1024]{1,0:T(8,128)S(1)}, u32[]{:S(2)}, u32[]{:S(2)}) collective-permute-start(f32[64,1024]{1,0:T(8,128)S(1)} %close.1.x0_ref), channel_id=1, source_target_pairs={{0,128},{128,0},{1,129},{129,1},{2,130},{130,2},{3,131},{131,3},{4... | collective-permute-start | bytes 786440 | tf_op jit(solution)/shard_map/cuts_gather/ppermute | solution.py:214
  55.6 5.0 %collective-permute-done.1.x2_ref = f32[64,1024]{1,0:T(8,128)S(1)} collective-permute-done((f32[64,1024]{1,0:T(8,128)S(1)}, f32[64,1024]{1,0:T(8,128)S(1)}, u32[]{:S(2)}, u32[]{:S(2)}) %collective-permute-start.1) | collective-permute-done | bytes 262176 | tf_op jit(solution)/shard_map/cuts_gather/ppermute | solution.py:213
  60.6 3.1 %collective-permute-start.2 = (f32[64,1024]{1,0:T(8,128)S(1)}, f32[64,1024]{1,0:T(8,128)S(1)}, u32[]{:S(2)}, u32[]{:S(2)}) collective-permute-start(f32[64,1024]{1,0:T(8,128)S(1)} %collective-permute-done.1.x2_ref), channel_id=1, source_target_pairs={{0,128},{128,0},{1,129},{129,1},{2,130},{130,2},{3,131},{131,3},{4... | collective-permute-start | bytes 786440 | tf_op jit(solution)/shard_map/cuts_gather/ppermute | solution.py:215
  63.7 0.0 collective-permute-done.x1_ref
  63.7 1.1 %collective-permute-done.2.x3_ref = f32[64,1024]{1,0:T(8,128)S(1)} collective-permute-done((f32[64,1024]{1,0:T(8,128)S(1)}, f32[64,1024]{1,0:T(8,128)S(1)}, u32[]{:S(2)}, u32[]{:S(2)}) %collective-permute-start.2) | collective-permute-done | bytes 262176 | tf_op jit(solution)/shard_map/cuts_gather/ppermute | solution.py:215
  64.8 0.0 all-to-all-done.1
  64.8 1.1 %join.1 = f32[16,8,8,128]{3,2,1,0:T(8,128)S(1)} custom-call(s32[1]{0:T(128)} %bitcast.cut_ref, f32[4,8,16,128]{3,2,1,0:T(8,128)S(1)} %bitcast.8, f32[64,1024]{1,0:T(8,128)S(1)} %close.1.x0_ref, f32[64,1024]{1,0:T(8,128)S(1)} %collective-permute-done.x1_ref, f32[64,1024]{1,0:T(8,128)S(1)} %collective-permute-done.1.x2_ref, ...), custom_call_target="tpu_custom_call" | custom-call | flops 134217728 | bytes 2097152 | tf_op jit(solution)/shard_map/join/pallas_call | solution.py:218
  65.9 11.6 %all_to_all.21.parts_ref = f32[16,8,8,128]{3,2,1,0:T(8,128)S(1)} all-to-all(f32[16,8,8,128]{3,2,1,0:T(8,128)S(1)} %join.1), channel_id=1, replica_groups=mesh['yh'=2,'core'=2,'yl'=2,'x'=4,'za'=8,'zb'=2] {'yl','x','zb'}, dimensions={0} | all-to-all | bytes 1048576 | tf_op jit(solution)/shard_map/sum_move/all_to_all | solution.py:228
  77.6 0.1 sum.1
  77.6 14.1 %all_to_all.22.parts_ref = f32[8,8,128]{2,1,0:T(8,128)S(1)} all-to-all(f32[8,8,128]{2,1,0:T(8,128)S(1)} %sum.1), channel_id=1, replica_groups={{8,10,12,14,0,2,4,6},{9,11,13,15,1,3,5,7},{24,26,28,30,16,18,20,22},{25..., dimensions={0} | all-to-all | bytes 65536 | tf_op jit(solution)/shard_map/last_move/all_to_all | solution.py:239
  91.7 0.6 finish.1
Async XLA Ops:
  23.7 23.3 %copy-start = (f32[2,2,128,4]{2,3,1,0:T(4,128)S(1)}, f32[2,2,128,4]{2,3,1,0:T(4,128)}, u32[]{:S(2)}) copy-start(f32[2,2,128,4]{2,3,1,0:T(4,128)} %param.5) | copy-start | bytes 24580
  24.4 40.4 %all-to-all-start.1 = ((f32[32,16,128]{2,1,0:T(8,128)}), f32[32,16,128]{2,1,0:T(8,128)S(1)}, u32[]{:S(2)}, u32[]{:S(2)}) async-start(f32[32,16,128]{2,1,0:T(8,128)} %bitcast.3), calls=%async_computation.1 | async-start | bytes 524288 | tf_op jit(solution)/shard_map/right_move/all_to_all | solution.py:201
  48.4 12.1 %collective-permute-start.1 = (f32[64,1024]{1,0:T(8,128)S(1)}, f32[64,1024]{1,0:T(8,128)S(1)}, u32[]{:S(2)}, u32[]{:S(2)}) collective-permute-start(f32[64,1024]{1,0:T(8,128)S(1)} %close.1.x0_ref), channel_id=1, source_target_pairs={{0,256},{256,0},{1,257},{257,1},{2,258},{258,2},{3,259},{259,3},{4... | collective-permute-start | bytes 786440 | tf_op jit(solution)/shard_map/cuts_gather/ppermute | solution.py:213
  53.0 10.6 %collective-permute-start = (f32[64,1024]{1,0:T(8,128)S(1)}, f32[64,1024]{1,0:T(8,128)S(1)}, u32[]{:S(2)}, u32[]{:S(2)}) collective-permute-start(f32[64,1024]{1,0:T(8,128)S(1)} %close.1.x0_ref), channel_id=1, source_target_pairs={{0,128},{128,0},{1,129},{129,1},{2,130},{130,2},{3,131},{131,3},{4... | collective-permute-start | bytes 786440 | tf_op jit(solution)/shard_map/cuts_gather/ppermute | solution.py:214
  60.6 4.2 %collective-permute-start.2 = (f32[64,1024]{1,0:T(8,128)S(1)}, f32[64,1024]{1,0:T(8,128)S(1)}, u32[]{:S(2)}, u32[]{:S(2)}) collective-permute-start(f32[64,1024]{1,0:T(8,128)S(1)} %collective-permute-done.1.x2_ref), channel_id=1, source_target_pairs={{0,128},{128,0},{1,129},{129,1},{2,130},{130,2},{3,131},{131,3},{4... | collective-permute-start | bytes 786440 | tf_op jit(solution)/shard_map/cuts_gather/ppermute | solution.py:215

commit v9 on v8

--- a/solution.py
+++ b/solution.py
@@ -16,7 +16,7 @@
 
 F32 = jnp.float32
 LANES = 128
-MID = 5
+MID = 7
 LAST = 4
 SMEM = pl.BlockSpec(memory_space=pltpu.SMEM)
 VMEM = pl.BlockSpec(memory_space=pltpu.VMEM)
@@ -41,27 +41,33 @@
     return v
 
 
-def pack_kernel(left_ref, right_ref, out_ref, held, piece, into, out_of):
+def pack_kernel(left_ref, right_ref, out_ref, held, right, piece, into, out_of):
     slices, _, near, depth, _ = left_ref.shape
     each = 2 * slices
+    halves = [pl.ds(0, near // 2), pl.ds(near // 2, near // 2)]
+    parts = [(i, half) for half in halves for i in range(each)]
     copies = []
-    for i in range(each):
-        copies.append(pltpu.make_async_copy(left_ref.at[i // 2, i % 2], held.at[i], into.at[i]))
+    for n, (i, half) in enumerate(parts):
+        copies.append(pltpu.make_async_copy(left_ref.at[i // 2, i % 2, half], held.at[i, half], into.at[n]))
         copies[-1].start()
-    width = right_ref.shape[2]
+    given = pltpu.make_async_copy(right_ref, right, into.at[len(parts)])
+    given.start()
+    last = []
+    for n, (i, half) in enumerate(parts):
+        copies[n].wait()
+        to = out_ref.at[half, pl.ds(i * depth, depth), :]
+        last.append(pltpu.make_async_copy(held.at[i, half], to, out_of.at[n]))
+        last[-1].start()
+    given.wait()
+    width = right.shape[2]
     for t in range(near // each):
         lanes = pl.ds(t * LANES, LANES)
-        w = swap_blocks([right_ref[j % slices, j // slices, :, lanes] for j in range(each)])
+        w = swap_blocks([right[j % slices, j // slices, :, lanes] for j in range(each)])
         for g in range(each):
             piece[t * each + g] = w[g]
     to = out_ref.at[:, pl.ds(each * depth, width), :]
-    last = [pltpu.make_async_copy(piece, to, out_of.at[each])]
-    last[0].start()
-    for i in range(each):
-        copies[i].wait()
-        to = out_ref.at[:, pl.ds(i * depth, depth), :]
-        last.append(pltpu.make_async_copy(held.at[i], to, out_of.at[i]))
-        last[-1].start()
+    last.append(pltpu.make_async_copy(piece, to, out_of.at[len(parts)]))
+    last[-1].start()
     for copy in last:
         copy.wait()
 
@@ -175,14 +181,15 @@
     x = kernel_call(
         pack_kernel,
         (near, body + width, LANES),
-        [ANY, VMEM],
+        [ANY, ANY],
         (0, 2**21),
         "pack",
         [
             pltpu.VMEM((slices * 2, near, kk, rows), F32),
+            pltpu.VMEM((slices, 2, width, depth), F32),
             pltpu.VMEM((near, width, LANES), F32),
-            pltpu.SemaphoreType.DMA((slices * 2,)),
-            pltpu.SemaphoreType.DMA((slices * 2 + 1,)),
+            pltpu.SemaphoreType.DMA((slices * 4 + 1,)),
+            pltpu.SemaphoreType.DMA((slices * 4 + 1,)),
         ],
         60,
         ANY,

time: 93.7 us -> 95 us (1.014)
  waiting for transfers between devices: 6.1 us -> 9.56 us
    all_to_all x1, waiting for transfers between devices: 0.01 us -> 3.02 us  [shards(): lax.all_to_all(r, CUTS + (FAR,), 0, 0, tiled=True, axis_index_groups=[gro...]
  transfers between devices with their start and end apart: 4 -> 4, of which waited for: 2 -> 3; matrix products, arithmetic and copies ran while one was open for 0% -> 0% of each run, Pallas kernels for 2% -> 1%
where the time goes in v9:
time: 95 us; the launch traced here: 93.7 us
  blocking collectives  46.1 us (49%)
  starting transfers between devices  31.9 us (34%)
  waiting for transfers between devices  9.56 us (10%)
  Pallas kernels  6.12 us (6%)
    all_to_all x1, starting transfers between devices, shards(): lax.all_to_all(r, CUTS + (FAR,), 0, 0, tiled=True, axis_index_groups=[gro...  21.6 us
    all_to_all x1, blocking collectives, shards(): x = lax.all_to_all(x, NEAR, 0, 0, tiled=True)  20.9 us
    all_to_all x1, blocking collectives, shards(): p = lax.all_to_all(p, FAR, 0, 0, tiled=True, axis_index_groups=[group])  13.5 us
    all_to_all x1, blocking collectives, shards(): p = lax.all_to_all(p, NEAR, 0, 0, tiled=True)  11.7 us
    ppermute x1, waiting for transfers between devices, shards(): x2 = lax.ppermute(x, 'yh', swap)  5.42 us
    ppermute x1, starting transfers between devices, shards(): x2 = lax.ppermute(x, 'yh', swap)  4.61 us
    ppermute x1, starting transfers between devices, shards(): x3 = lax.ppermute(x2, 'core', swap)  3.1 us
    all_to_all x1, waiting for transfers between devices, shards(): lax.all_to_all(r, CUTS + (FAR,), 0, 0, tiled=True, axis_index_groups=[gro...  3.02 us
  transfers between devices with their start and end apart: 4, of which 3 were waited for; matrix products, arithmetic and copies ran while one was open for 0% of the time, Pallas kernels for 1%

profile of v9, /device:TPU:1, one launch (start us, length us, event | category | flops | bytes accessed | tf_op | source)
XLA Modules:
  0.0 93.7 jit_solution(3579183233811347393)
XLA Ops:
  0.0 2.2 %pack.1 = f32[16,132,128]{2,1,0:T(8,128)} custom-call(f32[2,2,16,32,128]{4,3,2,1,0:T(8,128)} %bitcast.10, f32[2,2,4,512]{3,2,1,0:T(4,128)} %bitcast.11), custom_call_target="tpu_custom_call" | custom-call | bytes 2097152 | tf_op jit(solution)/shard_map/pack/pallas_call | solution.py:181
  2.2 20.9 %all_to_all.20.near_ref.left_ref = f32[16,132,128]{2,1,0:T(8,128)S(1)} all-to-all(f32[16,132,128]{2,1,0:T(8,128)} %pack.1), channel_id=1, replica_groups=mesh['yh'=2,'core'=2,'yl'=2,'x'=4,'za'=8,'zb'=2] {'yl','x','zb'}, dimensions={0} | all-to-all | bytes 2162688 | tf_op jit(solution)/shard_map/near_move/all_to_all | solution.py:199
  23.1 0.0 copy-start
  23.1 0.7 spread.1
  23.9 21.6 %all-to-all-start.1 = ((f32[32,16,128]{2,1,0:T(8,128)}), f32[32,16,128]{2,1,0:T(8,128)S(1)}, u32[]{:S(2)}, u32[]{:S(2)}) async-start(f32[32,16,128]{2,1,0:T(8,128)} %bitcast.3), calls=%async_computation.1 | async-start | bytes 524288 | tf_op jit(solution)/shard_map/right_move/all_to_all | solution.py:208
  45.5 0.0 copy-done
  45.5 1.4 %close.1.x0_ref = f32[64,1024]{1,0:T(8,128)S(1)} custom-call(s32[1]{0:T(128)} %bitcast.5.far_ref, f32[2,2,4,128]{3,2,1,0:T(4,128)S(1)} %bitcast.9, f32[16,132,128]{2,1,0:T(8,128)S(1)} %all_to_all.20.near_ref.left_ref), custom_call_target="tpu_custom_call" | custom-call | flops 4194304 | bytes 1572864 | tf_op jit(solution)/shard_map/close/pallas_call | solution.py:211
  46.9 4.6 %collective-permute-start.1 = (f32[64,1024]{1,0:T(8,128)S(1)}, f32[64,1024]{1,0:T(8,128)S(1)}, u32[]{:S(2)}, u32[]{:S(2)}) collective-permute-start(f32[64,1024]{1,0:T(8,128)S(1)} %close.1.x0_ref), channel_id=1, source_target_pairs={{0,256},{256,0},{1,257},{257,1},{2,258},{258,2},{3,259},{259,3},{4... | collective-permute-start | bytes 786440 | tf_op jit(solution)/shard_map/cuts_gather/ppermute | solution.py:220
  51.5 2.5 %collective-permute-start = (f32[64,1024]{1,0:T(8,128)S(1)}, f32[64,1024]{1,0:T(8,128)S(1)}, u32[]{:S(2)}, u32[]{:S(2)}) collective-permute-start(f32[64,1024]{1,0:T(8,128)S(1)} %close.1.x0_ref), channel_id=1, source_target_pairs={{0,128},{128,0},{1,129},{129,1},{2,130},{130,2},{3,131},{131,3},{4... | collective-permute-start | bytes 786440 | tf_op jit(solution)/shard_map/cuts_gather/ppermute | solution.py:221
  54.1 5.4 %collective-permute-done.1.x2_ref = f32[64,1024]{1,0:T(8,128)S(1)} collective-permute-done((f32[64,1024]{1,0:T(8,128)S(1)}, f32[64,1024]{1,0:T(8,128)S(1)}, u32[]{:S(2)}, u32[]{:S(2)}) %collective-permute-start.1) | collective-permute-done | bytes 262176 | tf_op jit(solution)/shard_map/cuts_gather/ppermute | solution.py:220
  59.5 3.1 %collective-permute-start.2 = (f32[64,1024]{1,0:T(8,128)S(1)}, f32[64,1024]{1,0:T(8,128)S(1)}, u32[]{:S(2)}, u32[]{:S(2)}) collective-permute-start(f32[64,1024]{1,0:T(8,128)S(1)} %collective-permute-done.1.x2_ref), channel_id=1, source_target_pairs={{0,128},{128,0},{1,129},{129,1},{2,130},{130,2},{3,131},{131,3},{4... | collective-permute-start | bytes 786440 | tf_op jit(solution)/shard_map/cuts_gather/ppermute | solution.py:222
  62.6 0.0 collective-permute-done.x1_ref
  62.6 1.1 %collective-permute-done.2.x3_ref = f32[64,1024]{1,0:T(8,128)S(1)} collective-permute-done((f32[64,1024]{1,0:T(8,128)S(1)}, f32[64,1024]{1,0:T(8,128)S(1)}, u32[]{:S(2)}, u32[]{:S(2)}) %collective-permute-start.2) | collective-permute-done | bytes 262176 | tf_op jit(solution)/shard_map/cuts_gather/ppermute | solution.py:222
  63.8 3.0 %all-to-all-done.1 = f32[32,16,128]{2,1,0:T(8,128)S(1)} async-done(((f32[32,16,128]{2,1,0:T(8,128)}), f32[32,16,128]{2,1,0:T(8,128)S(1)}, u32[]{:S(2)}, u32[]{:S(2)}) %all-to-all-start.1) | async-done | bytes 262176 | tf_op jit(solution)/shard_map/right_move/all_to_all | solution.py:208
  66.8 1.1 %join.1 = f32[16,8,8,128]{3,2,1,0:T(8,128)S(1)} custom-call(s32[1]{0:T(128)} %bitcast.cut_ref, f32[4,8,16,128]{3,2,1,0:T(8,128)S(1)} %bitcast.8, f32[64,1024]{1,0:T(8,128)S(1)} %close.1.x0_ref, f32[64,1024]{1,0:T(8,128)S(1)} %collective-permute-done.x1_ref, f32[64,1024]{1,0:T(8,128)S(1)} %collective-permute-done.1.x2_ref, ...), custom_call_target="tpu_custom_call" | custom-call | flops 134217728 | bytes 2097152 | tf_op jit(solution)/shard_map/join/pallas_call | solution.py:225
  67.9 11.7 %all_to_all.21.parts_ref = f32[16,8,8,128]{3,2,1,0:T(8,128)S(1)} all-to-all(f32[16,8,8,128]{3,2,1,0:T(8,128)S(1)} %join.1), channel_id=1, replica_groups=mesh['yh'=2,'core'=2,'yl'=2,'x'=4,'za'=8,'zb'=2] {'yl','x','zb'}, dimensions={0} | all-to-all | bytes 1048576 | tf_op jit(solution)/shard_map/sum_move/all_to_all | solution.py:235
  79.6 0.1 sum.1
  79.6 13.5 %all_to_all.22.parts_ref = f32[8,8,128]{2,1,0:T(8,128)S(1)} all-to-all(f32[8,8,128]{2,1,0:T(8,128)S(1)} %sum.1), channel_id=1, replica_groups={{8,10,12,14,0,2,4,6},{9,11,13,15,1,3,5,7},{24,26,28,30,16,18,20,22},{25..., dimensions={0} | all-to-all | bytes 65536 | tf_op jit(solution)/shard_map/last_move/all_to_all | solution.py:246
  93.1 0.6 finish.1
Async XLA Ops:
  23.1 22.4 %copy-start = (f32[2,2,128,4]{2,3,1,0:T(4,128)S(1)}, f32[2,2,128,4]{2,3,1,0:T(4,128)}, u32[]{:S(2)}) copy-start(f32[2,2,128,4]{2,3,1,0:T(4,128)} %param.5) | copy-start | bytes 24580
  23.9 42.9 %all-to-all-start.1 = ((f32[32,16,128]{2,1,0:T(8,128)}), f32[32,16,128]{2,1,0:T(8,128)S(1)}, u32[]{:S(2)}, u32[]{:S(2)}) async-start(f32[32,16,128]{2,1,0:T(8,128)} %bitcast.3), calls=%async_computation.1 | async-start | bytes 524288 | tf_op jit(solution)/shard_map/right_move/all_to_all | solution.py:208
  46.9 12.6 %collective-permute-start.1 = (f32[64,1024]{1,0:T(8,128)S(1)}, f32[64,1024]{1,0:T(8,128)S(1)}, u32[]{:S(2)}, u32[]{:S(2)}) collective-permute-start(f32[64,1024]{1,0:T(8,128)S(1)} %close.1.x0_ref), channel_id=1, source_target_pairs={{0,256},{256,0},{1,257},{257,1},{2,258},{258,2},{3,259},{259,3},{4... | collective-permute-start | bytes 786440 | tf_op jit(solution)/shard_map/cuts_gather/ppermute | solution.py:220
  51.5 11.1 %collective-permute-start = (f32[64,1024]{1,0:T(8,128)S(1)}, f32[64,1024]{1,0:T(8,128)S(1)}, u32[]{:S(2)}, u32[]{:S(2)}) collective-permute-start(f32[64,1024]{1,0:T(8,128)S(1)} %close.1.x0_ref), channel_id=1, source_target_pairs={{0,128},{128,0},{1,129},{129,1},{2,130},{130,2},{3,131},{131,3},{4... | collective-permute-start | bytes 786440 | tf_op jit(solution)/shard_map/cuts_gather/ppermute | solution.py:221
  59.5 4.3 %collective-permute-start.2 = (f32[64,1024]{1,0:T(8,128)S(1)}, f32[64,1024]{1,0:T(8,128)S(1)}, u32[]{:S(2)}, u32[]{:S(2)}) collective-permute-start(f32[64,1024]{1,0:T(8,128)S(1)} %collective-permute-done.1.x2_ref), channel_id=1, source_target_pairs={{0,128},{128,0},{1,129},{129,1},{2,130},{130,2},{3,131},{131,3},{4... | collective-permute-start | bytes 786440 | tf_op jit(solution)/shard_map/cuts_gather/ppermute | solution.py:222

commit v10 on v9

--- a/solution.py
+++ b/solution.py
@@ -16,8 +16,9 @@
 
 F32 = jnp.float32
 LANES = 128
-MID = 7
+MID = 5
 LAST = 4
+ORDER = [yl * 8 + x * 2 + zb for x in (0, 2, 1, 3) for yl in range(2) for zb in range(2)]
 SMEM = pl.BlockSpec(memory_space=pltpu.SMEM)
 VMEM = pl.BlockSpec(memory_space=pltpu.VMEM)
 ANY = pl.BlockSpec(memory_space=pl.ANY)
@@ -79,7 +80,7 @@
         for q6 in range(2):
             for q0 in range(2):
                 for q2 in range(2):
-                    two = near_ref[q87 * 4 + q6 * 2 + q2, pl.ds(body + q0, 2, stride=2), :]
+                    two = near_ref[ORDER.index(q87 * 4 + q6 * 2 + q2), pl.ds(body + q0, 2, stride=2), :]
                     out_ref[q87, 0, pl.ds(q6 * 8 + q0 * 4 + q2 * 2, 2), :] = two
         for g in range(1, far):
             out_ref[q87, g] = out_ref[q87, 0]
@@ -94,7 +95,7 @@
     for s in range(slices):
         acc = [[None] * (depth // rows) for _ in range(2 * outs)]
         for h in range(heads):
-            head = (h // 2) * 16 + first + h % 2
+            head = (ORDER[h] // 2) * 16 + first + ORDER[h] % 2
             co = [coef_ref[s, j // outs, j % outs, head] for j in range(2 * outs)]
             for kb in range(depth // rows):
                 at = 2 * s * depth + kb * rows
@@ -196,7 +197,7 @@
     )(left_tensor.reshape(slices, 2, near, kk, rows), right_tensor.transpose(0, 1, 3, 2))
 
     with jax.named_scope("near_move"):
-        x = lax.all_to_all(x, NEAR, 0, 0, tiled=True)
+        x = lax.all_to_all(x, NEAR, 0, 0, tiled=True, axis_index_groups=[ORDER])
 
     cuts = 4
     r = kernel_call(

time: 95 us -> 93 us (0.979)
  waiting for transfers between devices: 9.56 us -> 6.2 us
    all_to_all x1, waiting for transfers between devices: 3.02 us -> 0.01 us  [shards(): lax.all_to_all(r, CUTS + (FAR,), 0, 0, tiled=True, axis_index_groups=[gro...]
  transfers between devices with their start and end apart: 4 -> 4, of which waited for: 3 -> 2; matrix products, arithmetic and copies ran while one was open for 0% -> 0% of each run, Pallas kernels for 1% -> 2%
where the time goes in v10:
time: 93 us; the launch traced here: 91.7 us
  blocking collectives  46.9 us (50%)
  starting transfers between devices  32.4 us (35%)
  waiting for transfers between devices  6.2 us (7%)
  Pallas kernels  6.12 us (7%)
    all_to_all x1, starting transfers between devices, shards(): lax.all_to_all(r, CUTS + (FAR,), 0, 0, tiled=True, axis_index_groups=[gro...  22.2 us
    all_to_all x1, blocking collectives, shards(): x = lax.all_to_all(x, NEAR, 0, 0, tiled=True, axis_index_groups=[ORDER])  21.2 us
    all_to_all x1, blocking collectives, shards(): p = lax.all_to_all(p, FAR, 0, 0, tiled=True, axis_index_groups=[group])  14.2 us
    all_to_all x1, blocking collectives, shards(): p = lax.all_to_all(p, NEAR, 0, 0, tiled=True)  11.5 us
    ppermute x1, waiting for transfers between devices, shards(): x2 = lax.ppermute(x, 'yh', swap)  5.07 us
    ppermute x1, starting transfers between devices, shards(): x2 = lax.ppermute(x, 'yh', swap)  4.63 us
    ppermute x1, starting transfers between devices, shards(): x3 = lax.ppermute(x2, 'core', swap)  3.03 us
    ppermute x1, starting transfers between devices, shards(): x1 = lax.ppermute(x, 'core', swap)  2.53 us
  transfers between devices with their start and end apart: 4, of which 2 were waited for; matrix products, arithmetic and copies ran while one was open for 0% of the time, Pallas kernels for 2%

profile of v10, /device:TPU:1, one launch (start us, length us, event | category | flops | bytes accessed | tf_op | source)
XLA Modules:
  0.0 91.7 jit_solution(2718051363179349228)
XLA Ops:
  0.0 2.2 %pack.1 = f32[16,132,128]{2,1,0:T(8,128)} custom-call(f32[2,2,16,32,128]{4,3,2,1,0:T(8,128)} %bitcast.10, f32[2,2,4,512]{3,2,1,0:T(4,128)} %bitcast.11), custom_call_target="tpu_custom_call" | custom-call | bytes 2097152 | tf_op jit(solution)/shard_map/pack/pallas_call | solution.py:182
  2.2 21.2 %all_to_all.20.near_ref.left_ref = f32[16,132,128]{2,1,0:T(8,128)S(1)} all-to-all(f32[16,132,128]{2,1,0:T(8,128)} %pack.1), channel_id=1, replica_groups={{0,1,64,65,32,33,96,97,16,17,80,81,48,49,112,113},{2,3,66,67,34,35,98,9..., dimensions={0} | all-to-all | bytes 2162688 | tf_op jit(solution)/shard_map/near_move/all_to_all | solution.py:200
  23.4 0.0 copy-start
  23.4 0.7 spread.1
  24.2 22.2 %all-to-all-start.1 = ((f32[32,16,128]{2,1,0:T(8,128)}), f32[32,16,128]{2,1,0:T(8,128)S(1)}, u32[]{:S(2)}, u32[]{:S(2)}) async-start(f32[32,16,128]{2,1,0:T(8,128)} %bitcast.3), calls=%async_computation.1 | async-start | bytes 524288 | tf_op jit(solution)/shard_map/right_move/all_to_all | solution.py:209
  46.4 0.0 copy-done
  46.4 1.4 %close.1.x0_ref = f32[64,1024]{1,0:T(8,128)S(1)} custom-call(s32[1]{0:T(128)} %bitcast.5.far_ref, f32[2,2,4,128]{3,2,1,0:T(4,128)S(1)} %bitcast.9, f32[16,132,128]{2,1,0:T(8,128)S(1)} %all_to_all.20.near_ref.left_ref), custom_call_target="tpu_custom_call" | custom-call | flops 4194304 | bytes 1572864 | tf_op jit(solution)/shard_map/close/pallas_call | solution.py:212
  47.8 4.6 %collective-permute-start.1 = (f32[64,1024]{1,0:T(8,128)S(1)}, f32[64,1024]{1,0:T(8,128)S(1)}, u32[]{:S(2)}, u32[]{:S(2)}) collective-permute-start(f32[64,1024]{1,0:T(8,128)S(1)} %close.1.x0_ref), channel_id=1, source_target_pairs={{0,256},{256,0},{1,257},{257,1},{2,258},{258,2},{3,259},{259,3},{4... | collective-permute-start | bytes 786440 | tf_op jit(solution)/shard_map/cuts_gather/ppermute | solution.py:221
  52.5 2.5 %collective-permute-start = (f32[64,1024]{1,0:T(8,128)S(1)}, f32[64,1024]{1,0:T(8,128)S(1)}, u32[]{:S(2)}, u32[]{:S(2)}) collective-permute-start(f32[64,1024]{1,0:T(8,128)S(1)} %close.1.x0_ref), channel_id=1, source_target_pairs={{0,128},{128,0},{1,129},{129,1},{2,130},{130,2},{3,131},{131,3},{4... | collective-permute-start | bytes 786440 | tf_op jit(solution)/shard_map/cuts_gather/ppermute | solution.py:222
  55.0 5.1 %collective-permute-done.1.x2_ref = f32[64,1024]{1,0:T(8,128)S(1)} collective-permute-done((f32[64,1024]{1,0:T(8,128)S(1)}, f32[64,1024]{1,0:T(8,128)S(1)}, u32[]{:S(2)}, u32[]{:S(2)}) %collective-permute-start.1) | collective-permute-done | bytes 262176 | tf_op jit(solution)/shard_map/cuts_gather/ppermute | solution.py:221
  60.1 3.0 %collective-permute-start.2 = (f32[64,1024]{1,0:T(8,128)S(1)}, f32[64,1024]{1,0:T(8,128)S(1)}, u32[]{:S(2)}, u32[]{:S(2)}) collective-permute-start(f32[64,1024]{1,0:T(8,128)S(1)} %collective-permute-done.1.x2_ref), channel_id=1, source_target_pairs={{0,128},{128,0},{1,129},{129,1},{2,130},{130,2},{3,131},{131,3},{4... | collective-permute-start | bytes 786440 | tf_op jit(solution)/shard_map/cuts_gather/ppermute | solution.py:223
  63.1 0.0 collective-permute-done.x1_ref
  63.1 1.1 %collective-permute-done.2.x3_ref = f32[64,1024]{1,0:T(8,128)S(1)} collective-permute-done((f32[64,1024]{1,0:T(8,128)S(1)}, f32[64,1024]{1,0:T(8,128)S(1)}, u32[]{:S(2)}, u32[]{:S(2)}) %collective-permute-start.2) | collective-permute-done | bytes 262176 | tf_op jit(solution)/shard_map/cuts_gather/ppermute | solution.py:223
  64.3 0.0 all-to-all-done.1
  64.3 1.1 %join.1 = f32[16,8,8,128]{3,2,1,0:T(8,128)S(1)} custom-call(s32[1]{0:T(128)} %bitcast.cut_ref, f32[4,8,16,128]{3,2,1,0:T(8,128)S(1)} %bitcast.8, f32[64,1024]{1,0:T(8,128)S(1)} %close.1.x0_ref, f32[64,1024]{1,0:T(8,128)S(1)} %collective-permute-done.x1_ref, f32[64,1024]{1,0:T(8,128)S(1)} %collective-permute-done.1.x2_ref, ...), custom_call_target="tpu_custom_call" | custom-call | flops 134217728 | bytes 2097152 | tf_op jit(solution)/shard_map/join/pallas_call | solution.py:226
  65.4 11.5 %all_to_all.21.parts_ref = f32[16,8,8,128]{3,2,1,0:T(8,128)S(1)} all-to-all(f32[16,8,8,128]{3,2,1,0:T(8,128)S(1)} %join.1), channel_id=1, replica_groups=mesh['yh'=2,'core'=2,'yl'=2,'x'=4,'za'=8,'zb'=2] {'yl','x','zb'}, dimensions={0} | all-to-all | bytes 1048576 | tf_op jit(solution)/shard_map/sum_move/all_to_all | solution.py:236
  76.9 0.1 sum.1
  76.9 14.2 %all_to_all.22.parts_ref = f32[8,8,128]{2,1,0:T(8,128)S(1)} all-to-all(f32[8,8,128]{2,1,0:T(8,128)S(1)} %sum.1), channel_id=1, replica_groups={{8,10,12,14,0,2,4,6},{9,11,13,15,1,3,5,7},{24,26,28,30,16,18,20,22},{25..., dimensions={0} | all-to-all | bytes 65536 | tf_op jit(solution)/shard_map/last_move/all_to_all | solution.py:247
  91.1 0.6 finish.1
Async XLA Ops:
  23.4 23.0 %copy-start = (f32[2,2,128,4]{2,3,1,0:T(4,128)S(1)}, f32[2,2,128,4]{2,3,1,0:T(4,128)}, u32[]{:S(2)}) copy-start(f32[2,2,128,4]{2,3,1,0:T(4,128)} %param.5) | copy-start | bytes 24580
  24.2 40.1 %all-to-all-start.1 = ((f32[32,16,128]{2,1,0:T(8,128)}), f32[32,16,128]{2,1,0:T(8,128)S(1)}, u32[]{:S(2)}, u32[]{:S(2)}) async-start(f32[32,16,128]{2,1,0:T(8,128)} %bitcast.3), calls=%async_computation.1 | async-start | bytes 524288 | tf_op jit(solution)/shard_map/right_move/all_to_all | solution.py:209
  47.8 12.2 %collective-permute-start.1 = (f32[64,1024]{1,0:T(8,128)S(1)}, f32[64,1024]{1,0:T(8,128)S(1)}, u32[]{:S(2)}, u32[]{:S(2)}) collective-permute-start(f32[64,1024]{1,0:T(8,128)S(1)} %close.1.x0_ref), channel_id=1, source_target_pairs={{0,256},{256,0},{1,257},{257,1},{2,258},{258,2},{3,259},{259,3},{4... | collective-permute-start | bytes 786440 | tf_op jit(solution)/shard_map/cuts_gather/ppermute | solution.py:221
  52.5 10.7 %collective-permute-start = (f32[64,1024]{1,0:T(8,128)S(1)}, f32[64,1024]{1,0:T(8,128)S(1)}, u32[]{:S(2)}, u32[]{:S(2)}) collective-permute-start(f32[64,1024]{1,0:T(8,128)S(1)} %close.1.x0_ref), channel_id=1, source_target_pairs={{0,128},{128,0},{1,129},{129,1},{2,130},{130,2},{3,131},{131,3},{4... | collective-permute-start | bytes 786440 | tf_op jit(solution)/shard_map/cuts_gather/ppermute | solution.py:222
  60.1 4.2 %collective-permute-start.2 = (f32[64,1024]{1,0:T(8,128)S(1)}, f32[64,1024]{1,0:T(8,128)S(1)}, u32[]{:S(2)}, u32[]{:S(2)}) collective-permute-start(f32[64,1024]{1,0:T(8,128)S(1)} %collective-permute-done.1.x2_ref), channel_id=1, source_target_pairs={{0,128},{128,0},{1,129},{129,1},{2,130},{130,2},{3,131},{131,3},{4... | collective-permute-start | bytes 786440 | tf_op jit(solution)/shard_map/cuts_gather/ppermute | solution.py:223

commit v11 on v6

--- a/solution.py
+++ b/solution.py
@@ -16,6 +16,9 @@
 
 F32 = jnp.float32
 LANES = 128
+MID = 5
+LAST = 4
+ORDER = [yl * 8 + x * 2 + zb for x in (0, 2, 1, 3) for yl in range(2) for zb in range(2)]
 SMEM = pl.BlockSpec(memory_space=pltpu.SMEM)
 VMEM = pl.BlockSpec(memory_space=pltpu.VMEM)
 ANY = pl.BlockSpec(memory_space=pl.ANY)
@@ -39,27 +42,33 @@
     return v
 
 
-def pack_kernel(left_ref, right_ref, out_ref, held, piece, into, out_of):
+def pack_kernel(left_ref, right_ref, out_ref, held, right, piece, into, out_of):
     slices, _, near, depth, _ = left_ref.shape
     each = 2 * slices
+    halves = [pl.ds(0, near // 2), pl.ds(near // 2, near // 2)]
+    parts = [(i, half) for half in halves for i in range(each)]
     copies = []
-    for i in range(each):
-        copies.append(pltpu.make_async_copy(left_ref.at[i // 2, i % 2], held.at[i], into.at[i]))
+    for n, (i, half) in enumerate(parts):
+        copies.append(pltpu.make_async_copy(left_ref.at[i // 2, i % 2, half], held.at[i, half], into.at[n]))
         copies[-1].start()
-    width = right_ref.shape[2]
+    given = pltpu.make_async_copy(right_ref, right, into.at[len(parts)])
+    given.start()
+    last = []
+    for n, (i, half) in enumerate(parts):
+        copies[n].wait()
+        to = out_ref.at[half, pl.ds(i * depth, depth), :]
+        last.append(pltpu.make_async_copy(held.at[i, half], to, out_of.at[n]))
+        last[-1].start()
+    given.wait()
+    width = right.shape[2]
     for t in range(near // each):
         lanes = pl.ds(t * LANES, LANES)
-        w = swap_blocks([right_ref[j % slices, j // slices, :, lanes] for j in range(each)])
+        w = swap_blocks([right[j % slices, j // slices, :, lanes] for j in range(each)])
         for g in range(each):
             piece[t * each + g] = w[g]
     to = out_ref.at[:, pl.ds(each * depth, width), :]
-    last = [pltpu.make_async_copy(piece, to, out_of.at[each])]
-    last[0].start()
-    for i in range(each):
-        copies[i].wait()
-        to = out_ref.at[:, pl.ds(i * depth, depth), :]
-        last.append(pltpu.make_async_copy(held.at[i], to, out_of.at[i]))
-        last[-1].start()
+    last.append(pltpu.make_async_copy(piece, to, out_of.at[len(parts)]))
+    last[-1].start()
     for copy in last:
         copy.wait()
 
@@ -72,7 +81,7 @@
             for q0 in range(2):
                 for q8 in range(2):
                     for q2 in range(2):
-                        two = near_ref[q8 * 8 + q7 * 4 + q6 * 2 + q2, pl.ds(body + q0, 2, stride=2), :]
+                        two = near_ref[ORDER.index(q8 * 8 + q7 * 4 + q6 * 2 + q2), pl.ds(body + q0, 2, stride=2), :]
                         out_ref[q7, 0, pl.ds(q6 * 16 + q0 * 8 + q8 * 4 + q2 * 2, 2), :] = two
     for q7 in range(2):
         for g in range(1, out_ref.shape[1]):
@@ -88,7 +97,7 @@
     for s in range(slices):
         acc = [[None] * (depth // rows) for _ in range(2 * outs)]
         for h in range(heads):
-            head = (h // 2) * 16 + first + h % 2
+            head = (ORDER[h] // 2) * 16 + first + ORDER[h] % 2
             co = [coef_ref[s, j // outs, j % outs, head] for j in range(2 * outs)]
             for kb in range(depth // rows):
                 at = 2 * s * depth + kb * rows
@@ -116,7 +125,8 @@
             for q6 in range(2):
                 for q0 in range(2):
                     at = pl.ds((q6 * 2 + q0) * 8, 8)
-                    low, high = right_ref[core, 2 * t, at, :], right_ref[core, 2 * t + 1, at, :]
+                    low = right_ref[core, (2 * t - MID) % 8, at, :]
+                    high = right_ref[core, (2 * t + 1 - MID) % 8, at, :]
                     to = (q6 * 8 + t * 2 + q0) * 16
                     lanes = pl.ds(i * LANES, LANES)
                     lhs[pl.ds(to, 8), lanes] = jnp.where(first, low, pltpu.roll(high, 4, 0))
@@ -124,10 +134,11 @@
         rhs[pl.ds(2 * i * depth, depth), :] = x_ref[...]
         rhs[pl.ds((2 * i + 1) * depth, depth), :half] = -x_ref[:, half:]
         rhs[pl.ds((2 * i + 1) * depth, depth), half:] = x_ref[:, :half]
-    for j in range(wide // LANES):
-        right = rhs[:, pl.ds(j * LANES, LANES)]
+    for j in range(0, wide // LANES, 2):
+        right = rhs[:, pl.ds(j * LANES, 2 * LANES)]
         out = jnp.dot(lhs[...], right, precision=lax.Precision.HIGHEST, preferred_element_type=F32)
-        out_ref[:, j, :, :] = out.reshape(16, 16, LANES)
+        out_ref[:, j, :, :] = out[:, :LANES].reshape(16, 16, LANES)
+        out_ref[:, j + 1, :, :] = out[:, LANES:].reshape(16, 16, LANES)
 
 
 def sum_kernel(scale, parts_ref, out_ref):
@@ -135,7 +146,9 @@
         total = parts_ref[0, j]
         for i in range(1, parts_ref.shape[0]):
             total = total + parts_ref[i, j]
-        out_ref[:, j, :] = total * scale
+        total = total * scale
+        for half in range(0, total.shape[0], 8):
+            out_ref[pl.ds(half, 8), j, :] = pltpu.roll(total[half : half + 8], (8 - LAST) % 8, 0)
 
 
 def finish_kernel(parts_ref, out_ref):
@@ -174,26 +187,28 @@
     x = kernel_call(
         pack_kernel,
         (near, body + width, LANES),
-        [ANY, VMEM],
+        [ANY, ANY],
         (0, 2**21),
         "pack",
         [
             pltpu.VMEM((slices * 2, near, kk, rows), F32),
+            pltpu.VMEM((slices, 2, width, depth), F32),
             pltpu.VMEM((near, width, LANES), F32),
-            pltpu.SemaphoreType.DMA((slices * 2,)),
-            pltpu.SemaphoreType.DMA((slices * 2 + 1,)),
+            pltpu.SemaphoreType.DMA((slices * 4 + 1,)),
+            pltpu.SemaphoreType.DMA((slices * 4 + 1,)),
         ],
         60,
         ANY,
     )(left_tensor.reshape(slices, 2, near, kk, rows), right_tensor.transpose(0, 1, 3, 2))
 
     with jax.named_scope("near_move"):
-        x = lax.all_to_all(x, NEAR, 0, 0, tiled=True)
+        x = lax.all_to_all(x, NEAR, 0, 0, tiled=True, axis_index_groups=[ORDER])
 
     r = kernel_call(spread_kernel, (2, 8, near * width // 2, LANES), [VMEM], (0, 2**18), "spread")(x)
     with jax.named_scope("right_move"):
         r = r.reshape(16, near * width // 2, LANES)
-        r = lax.all_to_all(r, ("core", FAR), 0, 0, tiled=True)
+        group = [c * 8 + (f + MID) % 8 for c in range(2) for f in range(8)]
+        r = lax.all_to_all(r, ("core", FAR), 0, 0, tiled=True, axis_index_groups=[group])
         r = r.reshape(2, 8, near * width // 2, LANES)
 
     x = kernel_call(
@@ -227,7 +242,8 @@
     )(p)
 
     with jax.named_scope("last_move"):
-        p = lax.all_to_all(p, ("yh", FAR), 0, 0, tiled=True)
+        group = [c * 8 + (f + LAST) % 8 for c in range(2) for f in range(8)]
+        p = lax.all_to_all(p, ("yh", FAR), 0, 0, tiled=True, axis_index_groups=[group])
     p = kernel_call(finish_kernel, (outs, 2, rows), [VMEM], (2**14, 2**17), "finish")(p)
     return p.reshape(1, outs, 2, rows)
 

time: 105 us -> 97.6 us (0.930)
  blocking collectives: 60.7 us -> 57 us
  waiting for transfers between devices: 13.9 us -> 10.9 us
  Pallas kernels: 7.41 us -> 6.08 us
  starting transfers between devices: 20.9 us -> 22 us
    all_to_all x2, blocking collectives: 44.2 us -> 40.1 us  [the longest x1 21.2 us: shards(): x = lax.all_to_all(x, NEAR, 0, 0, tiled=True, axis_index_groups=[ORDER])]
    all_to_all x1, waiting for transfers between devices: 12.5 us -> 9.78 us  [shards(): lax.all_to_all(r, ('core', FAR), 0, 0, tiled=True, axis_index_groups=[gro...]
where the time goes in v11:
time: 97.6 us; the launch traced here: 96.1 us
  blocking collectives  57 us (58%)
  starting transfers between devices  22 us (23%)
  waiting for transfers between devices  10.9 us (11%)
  Pallas kernels  6.08 us (6%)
    all_to_all x1, blocking collectives, shards(): x = lax.all_to_all(x, NEAR, 0, 0, tiled=True, axis_index_groups=[ORDER])  21.2 us
    all_to_all x1, starting transfers between devices, shards(): lax.all_to_all(r, ('core', FAR), 0, 0, tiled=True, axis_index_groups=[gro...  19.8 us
    all_to_all x1, blocking collectives, shards(): lax.all_to_all(p, ('yh', FAR), 0, 0, tiled=True, axis_index_groups=[group])  18.9 us
    all_to_all x1, blocking collectives, shards(): p = lax.all_to_all(p, NEAR, 0, 0, tiled=True)  16.9 us
    all_to_all x1, waiting for transfers between devices, shards(): lax.all_to_all(r, ('core', FAR), 0, 0, tiled=True, axis_index_groups=[gro...  9.78 us
    ppermute x1, starting transfers between devices, shards(): y = lax.ppermute(x, 'core', [(0, 1), (1, 0)])  2.27 us
    pallas_call x1, Pallas kernels, shards(): kernel_call(pack_kernel, (near, body + width, LANES), [ANY, ANY], (0, 2 *...  2.2 us
  transfers between devices with their start and end apart: 2, of which 2 were waited for; matrix products, arithmetic and copies ran while one was open for 0% of the time, Pallas kernels for 1%

profile of v11, /device:TPU:1, one launch (start us, length us, event | category | flops | bytes accessed | tf_op | source)
XLA Modules:
  0.0 96.1 jit_solution(93610321302008994)
XLA Ops:
  0.0 2.2 %pack.1 = f32[16,132,128]{2,1,0:T(8,128)} custom-call(f32[2,2,16,32,128]{4,3,2,1,0:T(8,128)} %bitcast.10, f32[2,2,4,512]{3,2,1,0:T(4,128)} %bitcast.11), custom_call_target="tpu_custom_call" | custom-call | bytes 2097152 | tf_op jit(solution)/shard_map/pack/pallas_call | solution.py:187
  2.2 21.2 %all_to_all.20.near_ref.left_ref = f32[16,132,128]{2,1,0:T(8,128)S(1)} all-to-all(f32[16,132,128]{2,1,0:T(8,128)} %pack.1), channel_id=1, replica_groups={{0,1,64,65,32,33,96,97,16,17,80,81,48,49,112,113},{2,3,66,67,34,35,98,9..., dimensions={0} | all-to-all | bytes 2162688 | tf_op jit(solution)/shard_map/near_move/all_to_all | solution.py:205
  23.4 0.0 copy-start
  23.4 0.7 spread.1
  24.2 19.8 %all-to-all-start.1 = ((f32[16,32,128]{2,1,0:T(8,128)}), f32[16,32,128]{2,1,0:T(8,128)S(1)}, u32[]{:S(2)}, u32[]{:S(2)}) async-start(f32[16,32,128]{2,1,0:T(8,128)} %bitcast.3), calls=%async_computation.1 | async-start | bytes 524288 | tf_op jit(solution)/shard_map/right_move/all_to_all | solution.py:211
  43.9 0.0 copy-done
  43.9 1.4 %close.1.mine_ref = f32[64,1024]{1,0:T(8,128)S(1)} custom-call(s32[1]{0:T(128)} %bitcast.5.far_ref, f32[2,2,4,128]{3,2,1,0:T(4,128)S(1)} %bitcast.9, f32[16,132,128]{2,1,0:T(8,128)S(1)} %all_to_all.20.near_ref.left_ref), custom_call_target="tpu_custom_call" | custom-call | flops 4194304 | bytes 1572864 | tf_op jit(solution)/shard_map/close/pallas_call | solution.py:214
  45.3 2.3 %collective-permute-start = (f32[64,1024]{1,0:T(8,128)S(1)}, f32[64,1024]{1,0:T(8,128)S(1)}, u32[]{:S(2)}, u32[]{:S(2)}) collective-permute-start(f32[64,1024]{1,0:T(8,128)S(1)} %close.1.mine_ref), channel_id=1, source_target_pairs={{0,128},{128,0},{1,129},{129,1},{2,130},{130,2},{3,131},{131,3},{4... | collective-permute-start | bytes 786440 | tf_op jit(solution)/shard_map/core_swap/ppermute | solution.py:222
  47.6 1.1 %collective-permute-done.other_ref = f32[64,1024]{1,0:T(8,128)S(1)} collective-permute-done((f32[64,1024]{1,0:T(8,128)S(1)}, f32[64,1024]{1,0:T(8,128)S(1)}, u32[]{:S(2)}, u32[]{:S(2)}) %collective-permute-start) | collective-permute-done | bytes 262176 | tf_op jit(solution)/shard_map/core_swap/ppermute | solution.py:222
  48.8 9.8 %all-to-all-done.1 = f32[16,32,128]{2,1,0:T(8,128)S(1)} async-done(((f32[16,32,128]{2,1,0:T(8,128)}), f32[16,32,128]{2,1,0:T(8,128)S(1)}, u32[]{:S(2)}, u32[]{:S(2)}) %all-to-all-start.1) | async-done | bytes 262176 | tf_op jit(solution)/shard_map/right_move/all_to_all | solution.py:211
  58.5 1.1 %join.1 = f32[16,8,16,128]{3,2,1,0:T(8,128)S(1)} custom-call(s32[1]{0:T(128)} %bitcast.core_ref, f32[2,8,32,128]{3,2,1,0:T(8,128)S(1)} %bitcast.8, f32[64,1024]{1,0:T(8,128)S(1)} %close.1.mine_ref, f32[64,1024]{1,0:T(8,128)S(1)} %collective-permute-done.other_ref), custom_call_target="tpu_custom_call" | custom-call | flops 134217728 | bytes 2097152 | tf_op jit(solution)/shard_map/join/pallas_call | solution.py:225
  59.6 16.9 %all_to_all.21.parts_ref = f32[16,8,16,128]{3,2,1,0:T(8,128)S(1)} all-to-all(f32[16,8,16,128]{3,2,1,0:T(8,128)S(1)} %join.1), channel_id=1, replica_groups=mesh['yh'=2,'core'=2,'yl'=2,'x'=4,'za'=8,'zb'=2] {'yl','x','zb'}, dimensions={0} | all-to-all | bytes 2097152 | tf_op jit(solution)/shard_map/sum_move/all_to_all | solution.py:235
  76.5 0.1 sum.1
  76.6 18.9 %all_to_all.22.parts_ref = f32[16,8,128]{2,1,0:T(8,128)S(1)} all-to-all(f32[16,8,128]{2,1,0:T(8,128)S(1)} %sum.1), channel_id=1, replica_groups={{8,10,12,14,0,2,4,6,264,266,268,270,256,258,260,262},{9,11,13,15,1,3,5,..., dimensions={0} | all-to-all | bytes 131072 | tf_op jit(solution)/shard_map/last_move/all_to_all | solution.py:246
  95.4 0.6 finish.1
Async XLA Ops:
  23.4 20.5 %copy-start = (f32[2,2,128,4]{2,3,1,0:T(4,128)S(1)}, f32[2,2,128,4]{2,3,1,0:T(4,128)}, u32[]{:S(2)}) copy-start(f32[2,2,128,4]{2,3,1,0:T(4,128)} %param.5) | copy-start | bytes 24580
  24.2 34.4 %all-to-all-start.1 = ((f32[16,32,128]{2,1,0:T(8,128)}), f32[16,32,128]{2,1,0:T(8,128)S(1)}, u32[]{:S(2)}, u32[]{:S(2)}) async-start(f32[16,32,128]{2,1,0:T(8,128)} %bitcast.3), calls=%async_computation.1 | async-start | bytes 524288 | tf_op jit(solution)/shard_map/right_move/all_to_all | solution.py:211
  45.3 3.4 %collective-permute-start = (f32[64,1024]{1,0:T(8,128)S(1)}, f32[64,1024]{1,0:T(8,128)S(1)}, u32[]{:S(2)}, u32[]{:S(2)}) collective-permute-start(f32[64,1024]{1,0:T(8,128)S(1)} %close.1.mine_ref), channel_id=1, source_target_pairs={{0,128},{128,0},{1,129},{129,1},{2,130},{130,2},{3,131},{131,3},{4... | collective-permute-start | bytes 786440 | tf_op jit(solution)/shard_map/core_swap/ppermute | solution.py:222

commit v12 on v10

--- a/solution.py
+++ b/solution.py
@@ -17,6 +17,7 @@
 F32 = jnp.float32
 LANES = 128
 MID = 5
+HALF = 2
 LAST = 4
 ORDER = [yl * 8 + x * 2 + zb for x in (0, 2, 1, 3) for yl in range(2) for zb in range(2)]
 SMEM = pl.BlockSpec(memory_space=pltpu.SMEM)
@@ -81,9 +82,9 @@
             for q0 in range(2):
                 for q2 in range(2):
                     two = near_ref[ORDER.index(q87 * 4 + q6 * 2 + q2), pl.ds(body + q0, 2, stride=2), :]
-                    out_ref[q87, 0, pl.ds(q6 * 8 + q0 * 4 + q2 * 2, 2), :] = two
+                    out_ref[q87 ^ HALF, 0, pl.ds(q6 * 8 + q0 * 4 + q2 * 2, 2), :] = two
         for g in range(1, far):
-            out_ref[q87, g] = out_ref[q87, 0]
+            out_ref[q87 ^ HALF, g] = out_ref[q87 ^ HALF, 0]
 
 
 def close_kernel(far_ref, coef_ref, left_ref, out_ref):
@@ -118,7 +119,7 @@
     half = wide // 2
     first = lax.broadcasted_iota(jnp.int32, (8, LANES), 0) < 4
     for i, x_ref in enumerate((x0_ref, x1_ref, x2_ref, x3_ref)):
-        cut = cut_ref[0] ^ i
+        cut = cut_ref[0] ^ (i ^ HALF)
         lanes = pl.ds(i * LANES, LANES)
         for t in range(4):
             for q6 in range(2):
@@ -205,7 +206,7 @@
     )(x)
     with jax.named_scope("right_move"):
         r = r.reshape(cuts * 8, near * width // cuts, LANES)
-        group = [c * 8 + (f + MID) % 8 for c in range(cuts) for f in range(8)]
+        group = [(c ^ HALF) * 8 + (f + MID) % 8 for c in range(cuts) for f in range(8)]
         r = lax.all_to_all(r, CUTS + (FAR,), 0, 0, tiled=True, axis_index_groups=[group])
         r = r.reshape(cuts, 8, near * width // cuts, LANES)
 

time: 93 us -> 92.7 us (level)
  waiting for transfers between devices: 6.2 us -> 8.52 us
  starting transfers between devices: 32.4 us -> 30.2 us
    ppermute x1, starting transfers between devices: 4.63 us -> 2.16 us  [shards(): x2 = lax.ppermute(x, 'yh', swap)]
    ppermute x1, waiting for transfers between devices: 5.07 us -> 7.39 us  [shards(): x2 = lax.ppermute(x, 'yh', swap)]
where the time goes in v12:
time: 92.7 us; the launch traced here: 91.4 us
  blocking collectives  46.4 us (50%)
  starting transfers between devices  30.2 us (33%)
  waiting for transfers between devices  8.52 us (9%)
  Pallas kernels  6.12 us (7%)
    all_to_all x1, starting transfers between devices, shards(): lax.all_to_all(r, CUTS + (FAR,), 0, 0, tiled=True, axis_index_groups=[gro...  22.3 us
    all_to_all x1, blocking collectives, shards(): x = lax.all_to_all(x, NEAR, 0, 0, tiled=True, axis_index_groups=[ORDER])  21.2 us
    all_to_all x1, blocking collectives, shards(): p = lax.all_to_all(p, FAR, 0, 0, tiled=True, axis_index_groups=[group])  13.5 us
    all_to_all x1, blocking collectives, shards(): p = lax.all_to_all(p, NEAR, 0, 0, tiled=True)  11.7 us
    ppermute x1, waiting for transfers between devices, shards(): x2 = lax.ppermute(x, 'yh', swap)  7.39 us
    ppermute x1, starting transfers between devices, shards(): x3 = lax.ppermute(x2, 'core', swap)  3.19 us
    ppermute x1, starting transfers between devices, shards(): x1 = lax.ppermute(x, 'core', swap)  2.55 us
    pallas_call x1, Pallas kernels, shards(): kernel_call(pack_kernel, (near, body + width, LANES), [ANY, ANY], (0, 2 *...  2.2 us
  transfers between devices with their start and end apart: 4, of which 2 were waited for; matrix products, arithmetic and copies ran while one was open for 0% of the time, Pallas kernels for 2%

profile of v12, /device:TPU:1, one launch (start us, length us, event | category | flops | bytes accessed | tf_op | source)
XLA Modules:
  0.0 91.4 jit_solution(16890125666768773668)
XLA Ops:
  0.0 2.2 %pack.1 = f32[16,132,128]{2,1,0:T(8,128)} custom-call(f32[2,2,16,32,128]{4,3,2,1,0:T(8,128)} %bitcast.10, f32[2,2,4,512]{3,2,1,0:T(4,128)} %bitcast.11), custom_call_target="tpu_custom_call" | custom-call | bytes 2097152 | tf_op jit(solution)/shard_map/pack/pallas_call | solution.py:183
  2.2 21.2 %all_to_all.20.near_ref.left_ref = f32[16,132,128]{2,1,0:T(8,128)S(1)} all-to-all(f32[16,132,128]{2,1,0:T(8,128)} %pack.1), channel_id=1, replica_groups={{0,1,64,65,32,33,96,97,16,17,80,81,48,49,112,113},{2,3,66,67,34,35,98,9..., dimensions={0} | all-to-all | bytes 2162688 | tf_op jit(solution)/shard_map/near_move/all_to_all | solution.py:201
  23.4 0.0 copy-start
  23.4 0.7 spread.1
  24.2 22.3 %all-to-all-start.1 = ((f32[32,16,128]{2,1,0:T(8,128)}), f32[32,16,128]{2,1,0:T(8,128)S(1)}, u32[]{:S(2)}, u32[]{:S(2)}) async-start(f32[32,16,128]{2,1,0:T(8,128)} %bitcast.3), calls=%async_computation.1 | async-start | bytes 524288 | tf_op jit(solution)/shard_map/right_move/all_to_all | solution.py:210
  46.5 0.0 copy-done
  46.5 1.4 %close.1.x0_ref = f32[64,1024]{1,0:T(8,128)S(1)} custom-call(s32[1]{0:T(128)} %bitcast.5.far_ref, f32[2,2,4,128]{3,2,1,0:T(4,128)S(1)} %bitcast.9, f32[16,132,128]{2,1,0:T(8,128)S(1)} %all_to_all.20.near_ref.left_ref), custom_call_target="tpu_custom_call" | custom-call | flops 4194304 | bytes 1572864 | tf_op jit(solution)/shard_map/close/pallas_call | solution.py:213
  47.9 2.2 %collective-permute-start.1 = (f32[64,1024]{1,0:T(8,128)S(1)}, f32[64,1024]{1,0:T(8,128)S(1)}, u32[]{:S(2)}, u32[]{:S(2)}) collective-permute-start(f32[64,1024]{1,0:T(8,128)S(1)} %close.1.x0_ref), channel_id=1, source_target_pairs={{0,256},{256,0},{1,257},{257,1},{2,258},{258,2},{3,259},{259,3},{4... | collective-permute-start | bytes 786440 | tf_op jit(solution)/shard_map/cuts_gather/ppermute | solution.py:222
  50.1 2.5 %collective-permute-start = (f32[64,1024]{1,0:T(8,128)S(1)}, f32[64,1024]{1,0:T(8,128)S(1)}, u32[]{:S(2)}, u32[]{:S(2)}) collective-permute-start(f32[64,1024]{1,0:T(8,128)S(1)} %close.1.x0_ref), channel_id=1, source_target_pairs={{0,128},{128,0},{1,129},{129,1},{2,130},{130,2},{3,131},{131,3},{4... | collective-permute-start | bytes 786440 | tf_op jit(solution)/shard_map/cuts_gather/ppermute | solution.py:223
  52.7 7.4 %collective-permute-done.1.x2_ref = f32[64,1024]{1,0:T(8,128)S(1)} collective-permute-done((f32[64,1024]{1,0:T(8,128)S(1)}, f32[64,1024]{1,0:T(8,128)S(1)}, u32[]{:S(2)}, u32[]{:S(2)}) %collective-permute-start.1) | collective-permute-done | bytes 262176 | tf_op jit(solution)/shard_map/cuts_gather/ppermute | solution.py:222
  60.1 3.2 %collective-permute-start.2 = (f32[64,1024]{1,0:T(8,128)S(1)}, f32[64,1024]{1,0:T(8,128)S(1)}, u32[]{:S(2)}, u32[]{:S(2)}) collective-permute-start(f32[64,1024]{1,0:T(8,128)S(1)} %collective-permute-done.1.x2_ref), channel_id=1, source_target_pairs={{0,128},{128,0},{1,129},{129,1},{2,130},{130,2},{3,131},{131,3},{4... | collective-permute-start | bytes 786440 | tf_op jit(solution)/shard_map/cuts_gather/ppermute | solution.py:224
  63.3 0.0 collective-permute-done.x1_ref
  63.3 1.1 %collective-permute-done.2.x3_ref = f32[64,1024]{1,0:T(8,128)S(1)} collective-permute-done((f32[64,1024]{1,0:T(8,128)S(1)}, f32[64,1024]{1,0:T(8,128)S(1)}, u32[]{:S(2)}, u32[]{:S(2)}) %collective-permute-start.2) | collective-permute-done | bytes 262176 | tf_op jit(solution)/shard_map/cuts_gather/ppermute | solution.py:224
  64.4 0.0 all-to-all-done.1
  64.4 1.1 %join.1 = f32[16,8,8,128]{3,2,1,0:T(8,128)S(1)} custom-call(s32[1]{0:T(128)} %bitcast.cut_ref, f32[4,8,16,128]{3,2,1,0:T(8,128)S(1)} %bitcast.8, f32[64,1024]{1,0:T(8,128)S(1)} %close.1.x0_ref, f32[64,1024]{1,0:T(8,128)S(1)} %collective-permute-done.x1_ref, f32[64,1024]{1,0:T(8,128)S(1)} %collective-permute-done.1.x2_ref, ...), custom_call_target="tpu_custom_call" | custom-call | flops 134217728 | bytes 2097152 | tf_op jit(solution)/shard_map/join/pallas_call | solution.py:227
  65.5 11.7 %all_to_all.21.parts_ref = f32[16,8,8,128]{3,2,1,0:T(8,128)S(1)} all-to-all(f32[16,8,8,128]{3,2,1,0:T(8,128)S(1)} %join.1), channel_id=1, replica_groups=mesh['yh'=2,'core'=2,'yl'=2,'x'=4,'za'=8,'zb'=2] {'yl','x','zb'}, dimensions={0} | all-to-all | bytes 1048576 | tf_op jit(solution)/shard_map/sum_move/all_to_all | solution.py:237
  77.2 0.1 sum.1
  77.3 13.5 %all_to_all.22.parts_ref = f32[8,8,128]{2,1,0:T(8,128)S(1)} all-to-all(f32[8,8,128]{2,1,0:T(8,128)S(1)} %sum.1), channel_id=1, replica_groups={{8,10,12,14,0,2,4,6},{9,11,13,15,1,3,5,7},{24,26,28,30,16,18,20,22},{25..., dimensions={0} | all-to-all | bytes 65536 | tf_op jit(solution)/shard_map/last_move/all_to_all | solution.py:248
  90.8 0.6 finish.1
Async XLA Ops:
  23.4 23.1 %copy-start = (f32[2,2,128,4]{2,3,1,0:T(4,128)S(1)}, f32[2,2,128,4]{2,3,1,0:T(4,128)}, u32[]{:S(2)}) copy-start(f32[2,2,128,4]{2,3,1,0:T(4,128)} %param.5) | copy-start | bytes 24580
  24.2 40.2 %all-to-all-start.1 = ((f32[32,16,128]{2,1,0:T(8,128)}), f32[32,16,128]{2,1,0:T(8,128)S(1)}, u32[]{:S(2)}, u32[]{:S(2)}) async-start(f32[32,16,128]{2,1,0:T(8,128)} %bitcast.3), calls=%async_computation.1 | async-start | bytes 524288 | tf_op jit(solution)/shard_map/right_move/all_to_all | solution.py:210
  47.9 12.1 %collective-permute-start.1 = (f32[64,1024]{1,0:T(8,128)S(1)}, f32[64,1024]{1,0:T(8,128)S(1)}, u32[]{:S(2)}, u32[]{:S(2)}) collective-permute-start(f32[64,1024]{1,0:T(8,128)S(1)} %close.1.x0_ref), channel_id=1, source_target_pairs={{0,256},{256,0},{1,257},{257,1},{2,258},{258,2},{3,259},{259,3},{4... | collective-permute-start | bytes 786440 | tf_op jit(solution)/shard_map/cuts_gather/ppermute | solution.py:222
  50.1 13.2 %collective-permute-start = (f32[64,1024]{1,0:T(8,128)S(1)}, f32[64,1024]{1,0:T(8,128)S(1)}, u32[]{:S(2)}, u32[]{:S(2)}) collective-permute-start(f32[64,1024]{1,0:T(8,128)S(1)} %close.1.x0_ref), channel_id=1, source_target_pairs={{0,128},{128,0},{1,129},{129,1},{2,130},{130,2},{3,131},{131,3},{4... | collective-permute-start | bytes 786440 | tf_op jit(solution)/shard_map/cuts_gather/ppermute | solution.py:223
  60.1 4.3 %collective-permute-start.2 = (f32[64,1024]{1,0:T(8,128)S(1)}, f32[64,1024]{1,0:T(8,128)S(1)}, u32[]{:S(2)}, u32[]{:S(2)}) collective-permute-start(f32[64,1024]{1,0:T(8,128)S(1)} %collective-permute-done.1.x2_ref), channel_id=1, source_target_pairs={{0,128},{128,0},{1,129},{129,1},{2,130},{130,2},{3,131},{131,3},{4... | collective-permute-start | bytes 786440 | tf_op jit(solution)/shard_map/cuts_gather/ppermute | solution.py:224

commit v13 on v12

--- a/solution.py
+++ b/solution.py
@@ -19,7 +19,7 @@
 MID = 5
 HALF = 2
 LAST = 4
-ORDER = [yl * 8 + x * 2 + zb for x in (0, 2, 1, 3) for yl in range(2) for zb in range(2)]
+ORDER = [yl * 8 + x * 2 + zb for x in (3, 1, 2, 0) for yl in (1, 0) for zb in range(2)]
 SMEM = pl.BlockSpec(memory_space=pltpu.SMEM)
 VMEM = pl.BlockSpec(memory_space=pltpu.VMEM)
 ANY = pl.BlockSpec(memory_space=pl.ANY)
@@ -74,7 +74,7 @@
         copy.wait()
 
 
-def spread_kernel(near_ref, out_ref):
+def spread_kernel(far_ref, near_ref, out_ref):
     cuts, far, width, _ = out_ref.shape
     body = near_ref.shape[1] - cuts * width // near_ref.shape[0]
     for q87 in range(cuts):
@@ -202,8 +202,8 @@
 
     cuts = 4
     r = kernel_call(
-        spread_kernel, (cuts, 8, near * width // cuts, LANES), [VMEM], (0, 2**18), "spread"
-    )(x)
+        spread_kernel, (cuts, 8, near * width // cuts, LANES), [SMEM, VMEM], (0, 2**18), "spread"
+    )(here, x)
     with jax.named_scope("right_move"):
         r = r.reshape(cuts * 8, near * width // cuts, LANES)
         group = [(c ^ HALF) * 8 + (f + MID) % 8 for c in range(cuts) for f in range(8)]

time: 92.7 us -> 92.9 us (level)
  the two profiles are of different devices: /device:TPU:1 before, /device:TPU:8 now
where the time goes in v13:
time: 92.9 us; the launch traced here: 92.5 us
  starting transfers between devices  35 us (38%)
  blocking collectives  29.8 us (32%)
  waiting for transfers between devices  21.5 us (23%)
  Pallas kernels  6.15 us (7%)
    all_to_all x1, starting transfers between devices, shards(): lax.all_to_all(r, CUTS + (FAR,), 0, 0, tiled=True, axis_index_groups=[gro...  18.9 us
    all_to_all x1, blocking collectives, shards(): p = lax.all_to_all(p, NEAR, 0, 0, tiled=True)  15.3 us
    all_to_all x1, blocking collectives, shards(): p = lax.all_to_all(p, FAR, 0, 0, tiled=True, axis_index_groups=[group])  14.5 us
    all_to_all x1, waiting for transfers between devices, shards(): x = lax.all_to_all(x, NEAR, 0, 0, tiled=True, axis_index_groups=[ORDER])  11.8 us
    all_to_all x1, starting transfers between devices, shards(): x = lax.all_to_all(x, NEAR, 0, 0, tiled=True, axis_index_groups=[ORDER])  9.8 us
    ppermute x1, waiting for transfers between devices, shards(): x2 = lax.ppermute(x, 'yh', swap)  8.16 us
    ppermute x1, starting transfers between devices, shards(): x2 = lax.ppermute(x, 'yh', swap)  2.46 us
    pallas_call x1, Pallas kernels, shards(): kernel_call(pack_kernel, (near, body + width, LANES), [ANY, ANY], (0, 2 *...  2.23 us
  transfers between devices with their start and end apart: 5, of which 3 were waited for; matrix products, arithmetic and copies ran while one was open for 0% of the time, Pallas kernels for 2%

profile of v13, /device:TPU:8, one launch (start us, length us, event | category | flops | bytes accessed | tf_op | source)
XLA Modules:
  0.0 92.5 jit_solution(887682317064777262)
XLA Ops:
  0.0 2.2 %pack.1 = f32[16,132,128]{2,1,0:T(8,128)} custom-call(f32[2,2,16,32,128]{4,3,2,1,0:T(8,128)} %bitcast.10, f32[2,2,4,512]{3,2,1,0:T(4,128)} %bitcast.11), custom_call_target="tpu_custom_call" | custom-call | bytes 2097152 | tf_op jit(solution)/shard_map/pack/pallas_call | solution.py:183
  2.2 9.8 %all-to-all-start = ((f32[16,132,128]{2,1,0:T(8,128)}), f32[16,132,128]{2,1,0:T(8,128)S(1)}, u32[]{:S(2)}, u32[]{:S(2)}) async-start(f32[16,132,128]{2,1,0:T(8,128)} %pack.1), calls=%async_computation | async-start | bytes 2228224 | tf_op jit(solution)/shard_map/near_move/all_to_all | solution.py:201
  12.0 0.0 copy-start
  12.0 11.8 %all-to-all-done.near_ref.left_ref = f32[16,132,128]{2,1,0:T(8,128)S(1)} async-done(((f32[16,132,128]{2,1,0:T(8,128)}), f32[16,132,128]{2,1,0:T(8,128)S(1)}, u32[]{:S(2)}, u32[]{:S(2)}) %all-to-all-start) | async-done | bytes 1081376 | tf_op jit(solution)/shard_map/near_move/all_to_all | solution.py:201
  23.9 0.7 spread.1
  24.6 18.9 %all-to-all-start.1 = ((f32[32,16,128]{2,1,0:T(8,128)}), f32[32,16,128]{2,1,0:T(8,128)S(1)}, u32[]{:S(2)}, u32[]{:S(2)}) async-start(f32[32,16,128]{2,1,0:T(8,128)} %bitcast.4), calls=%async_computation.1 | async-start | bytes 524288 | tf_op jit(solution)/shard_map/right_move/all_to_all | solution.py:210
  43.5 0.0 copy-done
  43.5 1.4 %close.1.x0_ref = f32[64,1024]{1,0:T(8,128)S(1)} custom-call(s32[1]{0:T(128)} %bitcast.1.far_ref, f32[2,2,4,128]{3,2,1,0:T(4,128)S(1)} %bitcast.9, f32[16,132,128]{2,1,0:T(8,128)S(1)} %all-to-all-done.near_ref.left_ref), custom_call_target="tpu_custom_call" | custom-call | flops 4194304 | bytes 1572864 | tf_op jit(solution)/shard_map/close/pallas_call | solution.py:213
  44.9 2.5 %collective-permute-start.1 = (f32[64,1024]{1,0:T(8,128)S(1)}, f32[64,1024]{1,0:T(8,128)S(1)}, u32[]{:S(2)}, u32[]{:S(2)}) collective-permute-start(f32[64,1024]{1,0:T(8,128)S(1)} %close.1.x0_ref), channel_id=1, source_target_pairs={{0,256},{256,0},{1,257},{257,1},{2,258},{258,2},{3,259},{259,3},{4... | collective-permute-start | bytes 786440 | tf_op jit(solution)/shard_map/cuts_gather/ppermute | solution.py:222
  47.4 1.9 %collective-permute-start = (f32[64,1024]{1,0:T(8,128)S(1)}, f32[64,1024]{1,0:T(8,128)S(1)}, u32[]{:S(2)}, u32[]{:S(2)}) collective-permute-start(f32[64,1024]{1,0:T(8,128)S(1)} %close.1.x0_ref), channel_id=1, source_target_pairs={{0,128},{128,0},{1,129},{129,1},{2,130},{130,2},{3,131},{131,3},{4... | collective-permute-start | bytes 786440 | tf_op jit(solution)/shard_map/cuts_gather/ppermute | solution.py:223
  49.3 8.2 %collective-permute-done.1.x2_ref = f32[64,1024]{1,0:T(8,128)S(1)} collective-permute-done((f32[64,1024]{1,0:T(8,128)S(1)}, f32[64,1024]{1,0:T(8,128)S(1)}, u32[]{:S(2)}, u32[]{:S(2)}) %collective-permute-start.1) | collective-permute-done | bytes 262176 | tf_op jit(solution)/shard_map/cuts_gather/ppermute | solution.py:222
  57.5 1.9 %collective-permute-start.2 = (f32[64,1024]{1,0:T(8,128)S(1)}, f32[64,1024]{1,0:T(8,128)S(1)}, u32[]{:S(2)}, u32[]{:S(2)}) collective-permute-start(f32[64,1024]{1,0:T(8,128)S(1)} %collective-permute-done.1.x2_ref), channel_id=1, source_target_pairs={{0,128},{128,0},{1,129},{129,1},{2,130},{130,2},{3,131},{131,3},{4... | collective-permute-start | bytes 786440 | tf_op jit(solution)/shard_map/cuts_gather/ppermute | solution.py:224
  59.4 0.0 collective-permute-done.x1_ref
  59.4 1.5 %collective-permute-done.2.x3_ref = f32[64,1024]{1,0:T(8,128)S(1)} collective-permute-done((f32[64,1024]{1,0:T(8,128)S(1)}, f32[64,1024]{1,0:T(8,128)S(1)}, u32[]{:S(2)}, u32[]{:S(2)}) %collective-permute-start.2) | collective-permute-done | bytes 262176 | tf_op jit(solution)/shard_map/cuts_gather/ppermute | solution.py:224
  60.9 0.0 all-to-all-done.1
  60.9 1.1 %join.1 = f32[16,8,8,128]{3,2,1,0:T(8,128)S(1)} custom-call(s32[1]{0:T(128)} %bitcast.cut_ref, f32[4,8,16,128]{3,2,1,0:T(8,128)S(1)} %bitcast.8, f32[64,1024]{1,0:T(8,128)S(1)} %close.1.x0_ref, f32[64,1024]{1,0:T(8,128)S(1)} %collective-permute-done.x1_ref, f32[64,1024]{1,0:T(8,128)S(1)} %collective-permute-done.1.x2_ref, ...), custom_call_target="tpu_custom_call" | custom-call | flops 134217728 | bytes 2097152 | tf_op jit(solution)/shard_map/join/pallas_call | solution.py:227
  62.0 15.3 %all_to_all.20.parts_ref = f32[16,8,8,128]{3,2,1,0:T(8,128)S(1)} all-to-all(f32[16,8,8,128]{3,2,1,0:T(8,128)S(1)} %join.1), channel_id=1, replica_groups=mesh['yh'=2,'core'=2,'yl'=2,'x'=4,'za'=8,'zb'=2] {'yl','x','zb'}, dimensions={0} | all-to-all | bytes 1048576 | tf_op jit(solution)/shard_map/sum_move/all_to_all | solution.py:237
  77.4 0.1 sum.1
  77.4 14.5 %all_to_all.21.parts_ref = f32[8,8,128]{2,1,0:T(8,128)S(1)} all-to-all(f32[8,8,128]{2,1,0:T(8,128)S(1)} %sum.1), channel_id=1, replica_groups={{8,10,12,14,0,2,4,6},{9,11,13,15,1,3,5,7},{24,26,28,30,16,18,20,22},{25..., dimensions={0} | all-to-all | bytes 65536 | tf_op jit(solution)/shard_map/last_move/all_to_all | solution.py:248
  91.9 0.6 finish.1
Async XLA Ops:
  2.2 21.6 %all-to-all-start = ((f32[16,132,128]{2,1,0:T(8,128)}), f32[16,132,128]{2,1,0:T(8,128)S(1)}, u32[]{:S(2)}, u32[]{:S(2)}) async-start(f32[16,132,128]{2,1,0:T(8,128)} %pack.1), calls=%async_computation | async-start | bytes 2228224 | tf_op jit(solution)/shard_map/near_move/all_to_all | solution.py:201
  12.0 31.4 %copy-start = (f32[2,2,128,4]{2,3,1,0:T(4,128)S(1)}, f32[2,2,128,4]{2,3,1,0:T(4,128)}, u32[]{:S(2)}) copy-start(f32[2,2,128,4]{2,3,1,0:T(4,128)} %param.5) | copy-start | bytes 24580
  24.6 36.3 %all-to-all-start.1 = ((f32[32,16,128]{2,1,0:T(8,128)}), f32[32,16,128]{2,1,0:T(8,128)S(1)}, u32[]{:S(2)}, u32[]{:S(2)}) async-start(f32[32,16,128]{2,1,0:T(8,128)} %bitcast.4), calls=%async_computation.1 | async-start | bytes 524288 | tf_op jit(solution)/shard_map/right_move/all_to_all | solution.py:210
  44.9 12.6 %collective-permute-start.1 = (f32[64,1024]{1,0:T(8,128)S(1)}, f32[64,1024]{1,0:T(8,128)S(1)}, u32[]{:S(2)}, u32[]{:S(2)}) collective-permute-start(f32[64,1024]{1,0:T(8,128)S(1)} %close.1.x0_ref), channel_id=1, source_target_pairs={{0,256},{256,0},{1,257},{257,1},{2,258},{258,2},{3,259},{259,3},{4... | collective-permute-start | bytes 786440 | tf_op jit(solution)/shard_map/cuts_gather/ppermute | solution.py:222
  47.4 12.0 %collective-permute-start = (f32[64,1024]{1,0:T(8,128)S(1)}, f32[64,1024]{1,0:T(8,128)S(1)}, u32[]{:S(2)}, u32[]{:S(2)}) collective-permute-start(f32[64,1024]{1,0:T(8,128)S(1)} %close.1.x0_ref), channel_id=1, source_target_pairs={{0,128},{128,0},{1,129},{129,1},{2,130},{130,2},{3,131},{131,3},{4... | collective-permute-start | bytes 786440 | tf_op jit(solution)/shard_map/cuts_gather/ppermute | solution.py:223
  57.5 3.4 %collective-permute-start.2 = (f32[64,1024]{1,0:T(8,128)S(1)}, f32[64,1024]{1,0:T(8,128)S(1)}, u32[]{:S(2)}, u32[]{:S(2)}) collective-permute-start(f32[64,1024]{1,0:T(8,128)S(1)} %collective-permute-done.1.x2_ref), channel_id=1, source_target_pairs={{0,128},{128,0},{1,129},{129,1},{2,130},{130,2},{3,131},{131,3},{4... | collective-permute-start | bytes 786440 | tf_op jit(solution)/shard_map/cuts_gather/ppermute | solution.py:224

commit v14 on v13

--- a/solution.py
+++ b/solution.py
@@ -16,7 +16,7 @@
 
 F32 = jnp.float32
 LANES = 128
-MID = 5
+MID = 6
 HALF = 2
 LAST = 4
 ORDER = [yl * 8 + x * 2 + zb for x in (3, 1, 2, 0) for yl in (1, 0) for zb in range(2)]
@@ -87,38 +87,39 @@
             out_ref[q87 ^ HALF, g] = out_ref[q87 ^ HALF, 0]
 
 
-def close_kernel(far_ref, coef_ref, left_ref, out_ref):
+def close_kernel(s, far_ref, coef_ref, left_ref, out_ref):
     heads = left_ref.shape[0]
-    slices, _, outs, _ = coef_ref.shape
-    depth = out_ref.shape[0] // slices
+    outs = coef_ref.shape[2]
+    depth = out_ref.shape[0]
     first = far_ref[0] * 2
     rows = 8
-    for s in range(slices):
-        acc = [[None] * (depth // rows) for _ in range(2 * outs)]
-        for h in range(heads):
-            head = (ORDER[h] // 2) * 16 + first + ORDER[h] % 2
-            co = [coef_ref[s, j // outs, j % outs, head] for j in range(2 * outs)]
-            for kb in range(depth // rows):
-                at = 2 * s * depth + kb * rows
-                re = left_ref[h, pl.ds(at, rows), :]
-                im = left_ref[h, pl.ds(at + depth, rows), :]
-                for o in range(outs):
-                    cre, cim = co[o], co[outs + o]
-                    new_re = cre * re - cim * im
-                    new_im = cre * im + cim * re
-                    if h:
-                        new_re, new_im = acc[o][kb] + new_re, acc[outs + o][kb] + new_im
-                    acc[o][kb], acc[outs + o][kb] = new_re, new_im
+    acc = [[None] * (depth // rows) for _ in range(2 * outs)]
+    for h in range(heads):
+        head = (ORDER[h] // 2) * 16 + first + ORDER[h] % 2
+        co = [coef_ref[s, j // outs, j % outs, head] for j in range(2 * outs)]
         for kb in range(depth // rows):
-            for j in range(2 * outs):
-                out_ref[pl.ds(s * depth + kb * rows, rows), pl.ds(j * LANES, LANES)] = acc[j][kb]
-
-
-def join_kernel(cut_ref, right_ref, x0_ref, x1_ref, x2_ref, x3_ref, out_ref, lhs, rhs):
-    depth, wide = x0_ref.shape
+            at = 2 * s * depth + kb * rows
+            re = left_ref[h, pl.ds(at, rows), :]
+            im = left_ref[h, pl.ds(at + depth, rows), :]
+            for o in range(outs):
+                cre, cim = co[o], co[outs + o]
+                new_re = cre * re - cim * im
+                new_im = cre * im + cim * re
+                if h:
+                    new_re, new_im = acc[o][kb] + new_re, acc[outs + o][kb] + new_im
+                acc[o][kb], acc[outs + o][kb] = new_re, new_im
+    for kb in range(depth // rows):
+        for j in range(2 * outs):
+            out_ref[pl.ds(kb * rows, rows), pl.ds(j * LANES, LANES)] = acc[j][kb]
+
+
+def join_kernel(cut_ref, right_ref, *refs):
+    *x_refs, out_ref, lhs, rhs = refs
+    depth, wide = x_refs[0].shape
+    slices = len(x_refs) // 4
     half = wide // 2
     first = lax.broadcasted_iota(jnp.int32, (8, LANES), 0) < 4
-    for i, x_ref in enumerate((x0_ref, x1_ref, x2_ref, x3_ref)):
+    for i in range(4):
         cut = cut_ref[0] ^ (i ^ HALF)
         lanes = pl.ds(i * LANES, LANES)
         for t in range(4):
@@ -129,9 +130,13 @@
                 to = (q6 * 8 + t * 2) * 8
                 lhs[pl.ds(to, 8), lanes] = jnp.where(first, low, pltpu.roll(high, 4, 0))
                 lhs[pl.ds(to + 8, 8), lanes] = jnp.where(first, pltpu.roll(low, 4, 0), high)
-        rhs[pl.ds(2 * i * depth, depth), :] = x_ref[...]
-        rhs[pl.ds((2 * i + 1) * depth, depth), :half] = -x_ref[:, half:]
-        rhs[pl.ds((2 * i + 1) * depth, depth), half:] = x_ref[:, :half]
+        for s in range(slices):
+            x_ref = x_refs[i * slices + s]
+            re = pl.ds((2 * i * slices + s) * depth, depth)
+            im = pl.ds(((2 * i + 1) * slices + s) * depth, depth)
+            rhs[re, :] = x_ref[...]
+            rhs[im, :half] = -x_ref[:, half:]
+            rhs[im, half:] = x_ref[:, :half]
     for j in range(0, wide // LANES, 2):
         right = rhs[:, pl.ds(j * LANES, 2 * LANES)]
         out = jnp.dot(lhs[...], right, precision=lax.Precision.HIGHEST, preferred_element_type=F32)
@@ -210,28 +215,32 @@
         r = lax.all_to_all(r, CUTS + (FAR,), 0, 0, tiled=True, axis_index_groups=[group])
         r = r.reshape(cuts, 8, near * width // cuts, LANES)
 
-    x = kernel_call(
-        close_kernel,
-        (slices * kk, 2 * outs * rows),
-        [SMEM, SMEM, VMEM],
-        (2**22, 6 * 2**18),
-        "close",
-    )(here, closing_tensor.transpose(0, 1, 3, 2), x)
     swap = [(0, 1), (1, 0)]
-    with jax.named_scope("cuts_gather"):
-        x2 = lax.ppermute(x, "yh", swap)
-        x1 = lax.ppermute(x, "core", swap)
-        x3 = lax.ppermute(x2, "core", swap)
+    pieces = [[], [], [], []]
+    for i in range(slices):
+        x0 = kernel_call(
+            functools.partial(close_kernel, i),
+            (kk, 2 * outs * rows),
+            [SMEM, SMEM, VMEM],
+            (2**21, 3 * 2**18),
+            "close",
+        )(here, closing_tensor.transpose(0, 1, 3, 2), x)
+        with jax.named_scope("cuts_gather"):
+            x2 = lax.ppermute(x0, "yh", swap)
+            x1 = lax.ppermute(x0, "core", swap)
+            x3 = lax.ppermute(x2, "core", swap)
+        for piece, given in zip(pieces, (x0, x1, x2, x3)):
+            piece.append(given)
 
     wide = 2 * outs * rows
     p = kernel_call(
         join_kernel,
         (near, 2 * outs, 8, rows),
-        [SMEM] + [VMEM] * 5,
+        [SMEM] + [VMEM] * (1 + 4 * slices),
         (2**27, 2**21),
         "join",
         [pltpu.VMEM((128, cuts * LANES), F32), pltpu.VMEM((2 * cuts * slices * kk, wide), F32)],
-    )(lax.axis_index(CUTS).reshape(1), r, x, x1, x2, x3)
+    )(lax.axis_index(CUTS).reshape(1), r, *sum(pieces, []))
 
     with jax.named_scope("sum_move"):
         p = lax.all_to_all(p, NEAR, 0, 0, tiled=True)

time: 92.9 us -> 93 us (level)
  the two profiles are of different devices: /device:TPU:8 before, /device:TPU:1 now
where the time goes in v14:
time: 93 us; the launch traced here: 91.7 us
  starting transfers between devices  46.4 us (50%)
  blocking collectives  26.8 us (29%)
  waiting for transfers between devices  11.6 us (12%)
  Pallas kernels  6.8 us (7%)
    all_to_all x1, starting transfers between devices, shards(): lax.all_to_all(r, CUTS + (FAR,), 0, 0, tiled=True, axis_index_groups=[gro...  22.4 us
    all_to_all x1, blocking collectives, shards(): p = lax.all_to_all(p, FAR, 0, 0, tiled=True, axis_index_groups=[group])  13.5 us
    all_to_all x1, blocking collectives, shards(): p = lax.all_to_all(p, NEAR, 0, 0, tiled=True)  13.2 us
    all_to_all x1, waiting for transfers between devices, shards(): x = lax.all_to_all(x, NEAR, 0, 0, tiled=True, axis_index_groups=[ORDER])  10.3 us
    all_to_all x1, starting transfers between devices, shards(): x = lax.all_to_all(x, NEAR, 0, 0, tiled=True, axis_index_groups=[ORDER])  8.11 us
    ppermute x2, starting transfers between devices, shards(): x2 = lax.ppermute(x0, 'yh', swap)  6.79 us
    ppermute x2, starting transfers between devices, shards(): x1 = lax.ppermute(x0, 'core', swap)  4.73 us
    ppermute x2, starting transfers between devices, shards(): x3 = lax.ppermute(x2, 'core', swap)  4.33 us
  transfers between devices with their start and end apart: 8, of which 2 were waited for; matrix products, arithmetic and copies ran while one was open for 0% of the time, Pallas kernels for 2%

profile of v14, /device:TPU:1, one launch (start us, length us, event | category | flops | bytes accessed | tf_op | source)
XLA Modules:
  0.0 91.7 jit_solution(5513008788860466677)
XLA Ops:
  0.0 2.2 %pack.1 = f32[16,132,128]{2,1,0:T(8,128)} custom-call(f32[2,2,16,32,128]{4,3,2,1,0:T(8,128)} %bitcast.11, f32[2,2,4,512]{3,2,1,0:T(4,128)} %bitcast.12), custom_call_target="tpu_custom_call" | custom-call | bytes 2097152 | tf_op jit(solution)/shard_map/pack/pallas_call | solution.py:188
  2.2 8.1 %all-to-all-start = ((f32[16,132,128]{2,1,0:T(8,128)}), f32[16,132,128]{2,1,0:T(8,128)S(1)}, u32[]{:S(2)}, u32[]{:S(2)}) async-start(f32[16,132,128]{2,1,0:T(8,128)} %pack.1), calls=%async_computation | async-start | bytes 2228224 | tf_op jit(solution)/shard_map/near_move/all_to_all | solution.py:206
  10.3 0.0 copy-start
  10.3 10.3 %all-to-all-done.near_ref.left_ref = f32[16,132,128]{2,1,0:T(8,128)S(1)} async-done(((f32[16,132,128]{2,1,0:T(8,128)}), f32[16,132,128]{2,1,0:T(8,128)S(1)}, u32[]{:S(2)}, u32[]{:S(2)}) %all-to-all-start) | async-done | bytes 1081376 | tf_op jit(solution)/shard_map/near_move/all_to_all | solution.py:206
  20.6 0.7 spread.1
  21.4 22.4 %all-to-all-start.1 = ((f32[32,16,128]{2,1,0:T(8,128)}), f32[32,16,128]{2,1,0:T(8,128)S(1)}, u32[]{:S(2)}, u32[]{:S(2)}) async-start(f32[32,16,128]{2,1,0:T(8,128)} %bitcast.4), calls=%async_computation.1 | async-start | bytes 524288 | tf_op jit(solution)/shard_map/right_move/all_to_all | solution.py:215
  43.8 0.0 copy-done
  43.8 1.0 %close.2.refs_0_ = f32[32,1024]{1,0:T(8,128)S(1)} custom-call(s32[1]{0:T(128)} %bitcast.1.far_ref, f32[2,2,4,128]{3,2,1,0:T(4,128)S(1)} %bitcast.9, f32[16,132,128]{2,1,0:T(8,128)S(1)} %all-to-all-done.near_ref.left_ref), custom_call_target="tpu_custom_call" | custom-call | flops 2097152 | bytes 786432 | tf_op jit(solution)/shard_map/close/pallas_call | solution.py:221
  44.8 2.2 %collective-permute-start.2 = (f32[32,1024]{1,0:T(8,128)S(1)}, f32[32,1024]{1,0:T(8,128)S(1)}, u32[]{:S(2)}, u32[]{:S(2)}) collective-permute-start(f32[32,1024]{1,0:T(8,128)S(1)} %close.2.refs_0_), channel_id=1, source_target_pairs={{0,256},{256,0},{1,257},{257,1},{2,258},{258,2},{3,259},{259,3},{4... | collective-permute-start | bytes 393224 | tf_op jit(solution)/shard_map/cuts_gather/ppermute | solution.py:229
  47.0 1.1 %close.3.refs_1_ = f32[32,1024]{1,0:T(8,128)S(1)} custom-call(s32[1]{0:T(128)} %bitcast.1.far_ref, f32[2,2,4,128]{3,2,1,0:T(4,128)S(1)} %bitcast.10, f32[16,132,128]{2,1,0:T(8,128)S(1)} %all-to-all-done.near_ref.left_ref), custom_call_target="tpu_custom_call" | custom-call | flops 2097152 | bytes 786432 | tf_op jit(solution)/shard_map/close/pallas_call | solution.py:221
  48.1 4.6 %collective-permute-start.3 = (f32[32,1024]{1,0:T(8,128)S(1)}, f32[32,1024]{1,0:T(8,128)S(1)}, u32[]{:S(2)}, u32[]{:S(2)}) collective-permute-start(f32[32,1024]{1,0:T(8,128)S(1)} %close.3.refs_1_), channel_id=1, source_target_pairs={{0,256},{256,0},{1,257},{257,1},{2,258},{258,2},{3,259},{259,3},{4... | collective-permute-start | bytes 393224 | tf_op jit(solution)/shard_map/cuts_gather/ppermute | solution.py:229
  52.7 2.8 %collective-permute-start = (f32[32,1024]{1,0:T(8,128)S(1)}, f32[32,1024]{1,0:T(8,128)S(1)}, u32[]{:S(2)}, u32[]{:S(2)}) collective-permute-start(f32[32,1024]{1,0:T(8,128)S(1)} %close.2.refs_0_), channel_id=1, source_target_pairs={{0,128},{128,0},{1,129},{129,1},{2,130},{130,2},{3,131},{131,3},{4... | collective-permute-start | bytes 393224 | tf_op jit(solution)/shard_map/cuts_gather/ppermute | solution.py:230
  55.5 1.9 %collective-permute-start.1 = (f32[32,1024]{1,0:T(8,128)S(1)}, f32[32,1024]{1,0:T(8,128)S(1)}, u32[]{:S(2)}, u32[]{:S(2)}) collective-permute-start(f32[32,1024]{1,0:T(8,128)S(1)} %close.3.refs_1_), channel_id=1, source_target_pairs={{0,128},{128,0},{1,129},{129,1},{2,130},{130,2},{3,131},{131,3},{4... | collective-permute-start | bytes 393224 | tf_op jit(solution)/shard_map/cuts_gather/ppermute | solution.py:230
  57.4 0.0 collective-permute-done.2.refs_4_
  57.5 2.4 %collective-permute-start.4 = (f32[32,1024]{1,0:T(8,128)S(1)}, f32[32,1024]{1,0:T(8,128)S(1)}, u32[]{:S(2)}, u32[]{:S(2)}) collective-permute-start(f32[32,1024]{1,0:T(8,128)S(1)} %collective-permute-done.2.refs_4_), channel_id=1, source_target_pairs={{0,128},{128,0},{1,129},{129,1},{2,130},{130,2},{3,131},{131,3},{4... | collective-permute-start | bytes 393224 | tf_op jit(solution)/shard_map/cuts_gather/ppermute | solution.py:231
  59.9 0.0 collective-permute-done.3.refs_5_
  59.9 1.9 %collective-permute-start.5 = (f32[32,1024]{1,0:T(8,128)S(1)}, f32[32,1024]{1,0:T(8,128)S(1)}, u32[]{:S(2)}, u32[]{:S(2)}) collective-permute-start(f32[32,1024]{1,0:T(8,128)S(1)} %collective-permute-done.3.refs_5_), channel_id=1, source_target_pairs={{0,128},{128,0},{1,129},{129,1},{2,130},{130,2},{3,131},{131,3},{4... | collective-permute-start | bytes 393224 | tf_op jit(solution)/shard_map/cuts_gather/ppermute | solution.py:231
  61.8 0.0 collective-permute-done.refs_2_
  61.8 0.0 collective-permute-done.1.refs_3_
  61.8 0.0 collective-permute-done.4.refs_6_
  61.8 1.3 %collective-permute-done.5.refs_7_ = f32[32,1024]{1,0:T(8,128)S(1)} collective-permute-done((f32[32,1024]{1,0:T(8,128)S(1)}, f32[32,1024]{1,0:T(8,128)S(1)}, u32[]{:S(2)}, u32[]{:S(2)}) %collective-permute-start.5) | collective-permute-done | bytes 131104 | tf_op jit(solution)/shard_map/cuts_gather/ppermute | solution.py:231
  63.1 0.0 all-to-all-done.1
  63.1 1.1 %join.1 = f32[16,8,8,128]{3,2,1,0:T(8,128)S(1)} custom-call(s32[1]{0:T(128)} %bitcast.cut_ref, f32[4,8,16,128]{3,2,1,0:T(8,128)S(1)} %bitcast.8, f32[32,1024]{1,0:T(8,128)S(1)} %close.2.refs_0_, f32[32,1024]{1,0:T(8,128)S(1)} %close.3.refs_1_, f32[32,1024]{1,0:T(8,128)S(1)} %collective-permute-done.refs_2_, f32[32,1024]{1,0:T(8,128)S(1)} %collective-permute-done.1.refs_3_, ...), custom_call_target="tpu_custom_call" | custom-call | flops 134217728 | bytes 2097152 | tf_op jit(solution)/shard_map/join/pallas_call | solution.py:236
  64.3 13.2 %all_to_all.20.parts_ref = f32[16,8,8,128]{3,2,1,0:T(8,128)S(1)} all-to-all(f32[16,8,8,128]{3,2,1,0:T(8,128)S(1)} %join.1), channel_id=1, replica_groups=mesh['yh'=2,'core'=2,'yl'=2,'x'=4,'za'=8,'zb'=2] {'yl','x','zb'}, dimensions={0} | all-to-all | bytes 1048576 | tf_op jit(solution)/shard_map/sum_move/all_to_all | solution.py:246
  77.5 0.1 sum.1
  77.5 13.5 %all_to_all.21.parts_ref = f32[8,8,128]{2,1,0:T(8,128)S(1)} all-to-all(f32[8,8,128]{2,1,0:T(8,128)S(1)} %sum.1), channel_id=1, replica_groups={{8,10,12,14,0,2,4,6},{9,11,13,15,1,3,5,7},{24,26,28,30,16,18,20,22},{25..., dimensions={0} | all-to-all | bytes 65536 | tf_op jit(solution)/shard_map/last_move/all_to_all | solution.py:257
  91.1 0.6 finish.1
Async XLA Ops:
  2.2 18.4 %all-to-all-start = ((f32[16,132,128]{2,1,0:T(8,128)}), f32[16,132,128]{2,1,0:T(8,128)S(1)}, u32[]{:S(2)}, u32[]{:S(2)}) async-start(f32[16,132,128]{2,1,0:T(8,128)} %pack.1), calls=%async_computation | async-start | bytes 2228224 | tf_op jit(solution)/shard_map/near_move/all_to_all | solution.py:206
  10.3 33.5 %copy-start = (f32[2,2,128,4]{2,3,1,0:T(4,128)S(1)}, f32[2,2,128,4]{2,3,1,0:T(4,128)}, u32[]{:S(2)}) copy-start(f32[2,2,128,4]{2,3,1,0:T(4,128)} %param.5) | copy-start | bytes 24580
  21.4 41.8 %all-to-all-start.1 = ((f32[32,16,128]{2,1,0:T(8,128)}), f32[32,16,128]{2,1,0:T(8,128)S(1)}, u32[]{:S(2)}, u32[]{:S(2)}) async-start(f32[32,16,128]{2,1,0:T(8,128)} %bitcast.4), calls=%async_computation.1 | async-start | bytes 524288 | tf_op jit(solution)/shard_map/right_move/all_to_all | solution.py:215
  44.8 12.6 %collective-permute-start.2 = (f32[32,1024]{1,0:T(8,128)S(1)}, f32[32,1024]{1,0:T(8,128)S(1)}, u32[]{:S(2)}, u32[]{:S(2)}) collective-permute-start(f32[32,1024]{1,0:T(8,128)S(1)} %close.2.refs_0_), channel_id=1, source_target_pairs={{0,256},{256,0},{1,257},{257,1},{2,258},{258,2},{3,259},{259,3},{4... | collective-permute-start | bytes 393224 | tf_op jit(solution)/shard_map/cuts_gather/ppermute | solution.py:229
  48.1 11.8 %collective-permute-start.3 = (f32[32,1024]{1,0:T(8,128)S(1)}, f32[32,1024]{1,0:T(8,128)S(1)}, u32[]{:S(2)}, u32[]{:S(2)}) collective-permute-start(f32[32,1024]{1,0:T(8,128)S(1)} %close.3.refs_1_), channel_id=1, source_target_pairs={{0,256},{256,0},{1,257},{257,1},{2,258},{258,2},{3,259},{259,3},{4... | collective-permute-start | bytes 393224 | tf_op jit(solution)/shard_map/cuts_gather/ppermute | solution.py:229
  52.7 9.1 %collective-permute-start = (f32[32,1024]{1,0:T(8,128)S(1)}, f32[32,1024]{1,0:T(8,128)S(1)}, u32[]{:S(2)}, u32[]{:S(2)}) collective-permute-start(f32[32,1024]{1,0:T(8,128)S(1)} %close.2.refs_0_), channel_id=1, source_target_pairs={{0,128},{128,0},{1,129},{129,1},{2,130},{130,2},{3,131},{131,3},{4... | collective-permute-start | bytes 393224 | tf_op jit(solution)/shard_map/cuts_gather/ppermute | solution.py:230
  55.5 6.3 %collective-permute-start.1 = (f32[32,1024]{1,0:T(8,128)S(1)}, f32[32,1024]{1,0:T(8,128)S(1)}, u32[]{:S(2)}, u32[]{:S(2)}) collective-permute-start(f32[32,1024]{1,0:T(8,128)S(1)} %close.3.refs_1_), channel_id=1, source_target_pairs={{0,128},{128,0},{1,129},{129,1},{2,130},{130,2},{3,131},{131,3},{4... | collective-permute-start | bytes 393224 | tf_op jit(solution)/shard_map/cuts_gather/ppermute | solution.py:230
  57.5 4.4 %collective-permute-start.4 = (f32[32,1024]{1,0:T(8,128)S(1)}, f32[32,1024]{1,0:T(8,128)S(1)}, u32[]{:S(2)}, u32[]{:S(2)}) collective-permute-start(f32[32,1024]{1,0:T(8,128)S(1)} %collective-permute-done.2.refs_4_), channel_id=1, source_target_pairs={{0,128},{128,0},{1,129},{129,1},{2,130},{130,2},{3,131},{131,3},{4... | collective-permute-start | bytes 393224 | tf_op jit(solution)/shard_map/cuts_gather/ppermute | solution.py:231
  59.9 3.2 %collective-permute-start.5 = (f32[32,1024]{1,0:T(8,128)S(1)}, f32[32,1024]{1,0:T(8,128)S(1)}, u32[]{:S(2)}, u32[]{:S(2)}) collective-permute-start(f32[32,1024]{1,0:T(8,128)S(1)} %collective-permute-done.3.refs_5_), channel_id=1, source_target_pairs={{0,128},{128,0},{1,129},{129,1},{2,130},{130,2},{3,131},{131,3},{4... | collective-permute-start | bytes 393224 | tf_op jit(solution)/shard_map/cuts_gather/ppermute | solution.py:231

commit v15 on v13

--- a/solution.py
+++ b/solution.py
@@ -16,7 +16,7 @@
 
 F32 = jnp.float32
 LANES = 128
-MID = 5
+MID = 6
 HALF = 2
 LAST = 4
 ORDER = [yl * 8 + x * 2 + zb for x in (3, 1, 2, 0) for yl in (1, 0) for zb in range(2)]
@@ -87,13 +87,13 @@
             out_ref[q87 ^ HALF, g] = out_ref[q87 ^ HALF, 0]
 
 
-def close_kernel(far_ref, coef_ref, left_ref, out_ref):
+def close_kernel(far_ref, coef_ref, left_ref, out_ref, *piece_refs):
     heads = left_ref.shape[0]
-    slices, _, outs, _ = coef_ref.shape
-    depth = out_ref.shape[0] // slices
+    outs = coef_ref.shape[2]
     first = far_ref[0] * 2
     rows = 8
-    for s in range(slices):
+    for s, piece_ref in enumerate(piece_refs):
+        depth = piece_ref.shape[0]
         acc = [[None] * (depth // rows) for _ in range(2 * outs)]
         for h in range(heads):
             head = (ORDER[h] // 2) * 16 + first + ORDER[h] % 2
@@ -111,14 +111,19 @@
                     acc[o][kb], acc[outs + o][kb] = new_re, new_im
         for kb in range(depth // rows):
             for j in range(2 * outs):
-                out_ref[pl.ds(s * depth + kb * rows, rows), pl.ds(j * LANES, LANES)] = acc[j][kb]
-
-
-def join_kernel(cut_ref, right_ref, x0_ref, x1_ref, x2_ref, x3_ref, out_ref, lhs, rhs):
-    depth, wide = x0_ref.shape
+                lanes = pl.ds(j * LANES, LANES)
+                piece_ref[pl.ds(kb * rows, rows), lanes] = acc[j][kb]
+                out_ref[pl.ds(s * depth + kb * rows, rows), lanes] = acc[j][kb]
+
+
+def join_kernel(cut_ref, right_ref, *refs):
+    *x_refs, out_ref, lhs, rhs = refs
+    depth, wide = x_refs[2].shape
+    slices = len(x_refs) // 2 - 1
+    x_refs = [x.at[pl.ds(s * depth, depth), :] for x in x_refs[:2] for s in range(slices)] + x_refs[2:]
     half = wide // 2
     first = lax.broadcasted_iota(jnp.int32, (8, LANES), 0) < 4
-    for i, x_ref in enumerate((x0_ref, x1_ref, x2_ref, x3_ref)):
+    for i in range(4):
         cut = cut_ref[0] ^ (i ^ HALF)
         lanes = pl.ds(i * LANES, LANES)
         for t in range(4):
@@ -129,9 +134,13 @@
                 to = (q6 * 8 + t * 2) * 8
                 lhs[pl.ds(to, 8), lanes] = jnp.where(first, low, pltpu.roll(high, 4, 0))
                 lhs[pl.ds(to + 8, 8), lanes] = jnp.where(first, pltpu.roll(low, 4, 0), high)
-        rhs[pl.ds(2 * i * depth, depth), :] = x_ref[...]
-        rhs[pl.ds((2 * i + 1) * depth, depth), :half] = -x_ref[:, half:]
-        rhs[pl.ds((2 * i + 1) * depth, depth), half:] = x_ref[:, :half]
+        for s in range(slices):
+            x_ref = x_refs[i * slices + s]
+            re = pl.ds((2 * i * slices + s) * depth, depth)
+            im = pl.ds(((2 * i + 1) * slices + s) * depth, depth)
+            rhs[re, :] = x_ref[...]
+            rhs[im, :half] = -x_ref[:, half:]
+            rhs[im, half:] = x_ref[:, :half]
     for j in range(0, wide // LANES, 2):
         right = rhs[:, pl.ds(j * LANES, 2 * LANES)]
         out = jnp.dot(lhs[...], right, precision=lax.Precision.HIGHEST, preferred_element_type=F32)
@@ -161,7 +170,7 @@
     flops, size = cost
     return pl.pallas_call(
         body,
-        out_shape=jax.ShapeDtypeStruct(shape, F32),
+        out_shape=jax.tree.map(lambda n: jax.ShapeDtypeStruct(n, F32), shape, is_leaf=lambda n: isinstance(n, tuple)),
         in_specs=specs,
         out_specs=to,
         scratch_shapes=scratch,
@@ -210,28 +219,29 @@
         r = lax.all_to_all(r, CUTS + (FAR,), 0, 0, tiled=True, axis_index_groups=[group])
         r = r.reshape(cuts, 8, near * width // cuts, LANES)
 
-    x = kernel_call(
+    swap = [(0, 1), (1, 0)]
+    wide = 2 * outs * rows
+    x0, *pieces = kernel_call(
         close_kernel,
-        (slices * kk, 2 * outs * rows),
+        [(slices * kk, wide)] + [(kk, wide)] * slices,
         [SMEM, SMEM, VMEM],
         (2**22, 6 * 2**18),
         "close",
+        to=[VMEM] * (1 + slices),
     )(here, closing_tensor.transpose(0, 1, 3, 2), x)
-    swap = [(0, 1), (1, 0)]
     with jax.named_scope("cuts_gather"):
-        x2 = lax.ppermute(x, "yh", swap)
-        x1 = lax.ppermute(x, "core", swap)
-        x3 = lax.ppermute(x2, "core", swap)
-
-    wide = 2 * outs * rows
+        x2 = [lax.ppermute(piece, "yh", swap) for piece in pieces]
+        x1 = lax.ppermute(x0, "core", swap)
+        x3 = [lax.ppermute(piece, "core", swap) for piece in x2]
+
     p = kernel_call(
         join_kernel,
         (near, 2 * outs, 8, rows),
-        [SMEM] + [VMEM] * 5,
+        [SMEM] + [VMEM] * (3 + 2 * slices),
         (2**27, 2**21),
         "join",
         [pltpu.VMEM((128, cuts * LANES), F32), pltpu.VMEM((2 * cuts * slices * kk, wide), F32)],
-    )(lax.axis_index(CUTS).reshape(1), r, x, x1, x2, x3)
+    )(lax.axis_index(CUTS).reshape(1), r, x0, x1, *x2, *x3)
 
     with jax.named_scope("sum_move"):
         p = lax.all_to_all(p, NEAR, 0, 0, tiled=True)

time: 92.9 us -> 91.9 us (0.989)
  the two profiles are of different devices: /device:TPU:8 before, /device:TPU:1 now
where the time goes in v15:
time: 91.9 us; the launch traced here: 90.4 us
  starting transfers between devices  45.6 us (50%)
  blocking collectives  27.3 us (30%)
  waiting for transfers between devices  11.2 us (12%)
  Pallas kernels  6.14 us (7%)
    all_to_all x1, starting transfers between devices, shards(): lax.all_to_all(r, CUTS + (FAR,), 0, 0, tiled=True, axis_index_groups=[gro...  22.4 us
    all_to_all x1, blocking collectives, shards(): p = lax.all_to_all(p, FAR, 0, 0, tiled=True, axis_index_groups=[group])  13.8 us
    all_to_all x1, blocking collectives, shards(): p = lax.all_to_all(p, NEAR, 0, 0, tiled=True)  13.4 us
    all_to_all x1, waiting for transfers between devices, shards(): x = lax.all_to_all(x, NEAR, 0, 0, tiled=True, axis_index_groups=[ORDER])  10.3 us
    all_to_all x1, starting transfers between devices, shards(): x = lax.all_to_all(x, NEAR, 0, 0, tiled=True, axis_index_groups=[ORDER])  8.11 us
    ppermute x2, starting transfers between devices, shards(): x2 = [lax.ppermute(piece, 'yh', swap) for piece in pieces]  6.79 us
    ppermute x2, starting transfers between devices, shards(): x3 = [lax.ppermute(piece, 'core', swap) for piece in x2]  5.49 us
    ppermute x1, starting transfers between devices, shards(): x1 = lax.ppermute(x0, 'core', swap)  2.81 us
  transfers between devices with their start and end apart: 7, of which 2 were waited for; matrix products, arithmetic and copies ran while one was open for 0% of the time, Pallas kernels for 2%

profile of v15, /device:TPU:1, one launch (start us, length us, event | category | flops | bytes accessed | tf_op | source)
XLA Modules:
  0.0 90.4 jit_solution(18330155089587613117)
XLA Ops:
  0.0 2.2 %pack.1 = f32[16,132,128]{2,1,0:T(8,128)} custom-call(f32[2,2,16,32,128]{4,3,2,1,0:T(8,128)} %bitcast.10, f32[2,2,4,512]{3,2,1,0:T(4,128)} %bitcast.11), custom_call_target="tpu_custom_call" | custom-call | bytes 2097152 | tf_op jit(solution)/shard_map/pack/pallas_call | solution.py:192
  2.2 8.1 %all-to-all-start = ((f32[16,132,128]{2,1,0:T(8,128)}), f32[16,132,128]{2,1,0:T(8,128)S(1)}, u32[]{:S(2)}, u32[]{:S(2)}) async-start(f32[16,132,128]{2,1,0:T(8,128)} %pack.1), calls=%async_computation | async-start | bytes 2228224 | tf_op jit(solution)/shard_map/near_move/all_to_all | solution.py:210
  10.3 0.0 copy-start
  10.3 10.3 %all-to-all-done.near_ref.left_ref = f32[16,132,128]{2,1,0:T(8,128)S(1)} async-done(((f32[16,132,128]{2,1,0:T(8,128)}), f32[16,132,128]{2,1,0:T(8,128)S(1)}, u32[]{:S(2)}, u32[]{:S(2)}) %all-to-all-start) | async-done | bytes 1081376 | tf_op jit(solution)/shard_map/near_move/all_to_all | solution.py:210
  20.6 0.7 spread.1
  21.4 22.4 %all-to-all-start.1 = ((f32[32,16,128]{2,1,0:T(8,128)}), f32[32,16,128]{2,1,0:T(8,128)S(1)}, u32[]{:S(2)}, u32[]{:S(2)}) async-start(f32[32,16,128]{2,1,0:T(8,128)} %bitcast.4), calls=%async_computation.1 | async-start | bytes 524288 | tf_op jit(solution)/shard_map/right_move/all_to_all | solution.py:219
  43.8 0.0 copy-done
  43.8 1.4 %close.1 = (f32[64,1024]{1,0:T(8,128)S(1)}, f32[32,1024]{1,0:T(8,128)S(1)}, f32[32,1024]{1,0:T(8,128)S(1)}) custom-call(s32[1]{0:T(128)} %bitcast.1.far_ref, f32[2,2,4,128]{3,2,1,0:T(4,128)S(1)} %bitcast.9, f32[16,132,128]{2,1,0:T(8,128)S(1)} %all-to-all-done.near_ref.left_ref), custom_call_target="tpu_custom_call" | custom-call | flops 4194304 | bytes 1572864 | tf_op jit(solution)/shard_map/close/pallas_call | solution.py:224
  45.2 2.2 %collective-permute-start.1 = (f32[32,1024]{1,0:T(8,128)S(1)}, f32[32,1024]{1,0:T(8,128)S(1)}, u32[]{:S(2)}, u32[]{:S(2)}) collective-permute-start(f32[32,1024]{1,0:T(8,128)S(1)} %get-tuple-element.9), channel_id=1, source_target_pairs={{0,256},{256,0},{1,257},{257,1},{2,258},{258,2},{3,259},{259,3},{4... | collective-permute-start | bytes 393224 | tf_op jit(solution)/shard_map/cuts_gather/ppermute | solution.py:233
  47.4 4.6 %collective-permute-start.2 = (f32[32,1024]{1,0:T(8,128)S(1)}, f32[32,1024]{1,0:T(8,128)S(1)}, u32[]{:S(2)}, u32[]{:S(2)}) collective-permute-start(f32[32,1024]{1,0:T(8,128)S(1)} %get-tuple-element.10), channel_id=1, source_target_pairs={{0,256},{256,0},{1,257},{257,1},{2,258},{258,2},{3,259},{259,3},{4... | collective-permute-start | bytes 393224 | tf_op jit(solution)/shard_map/cuts_gather/ppermute | solution.py:233
  52.0 2.8 %collective-permute-start = (f32[64,1024]{1,0:T(8,128)S(1)}, f32[64,1024]{1,0:T(8,128)S(1)}, u32[]{:S(2)}, u32[]{:S(2)}) collective-permute-start(f32[64,1024]{1,0:T(8,128)S(1)} %get-tuple-element.8.refs_0_), channel_id=1, source_target_pairs={{0,128},{128,0},{1,129},{129,1},{2,130},{130,2},{3,131},{131,3},{4... | collective-permute-start | bytes 786440 | tf_op jit(solution)/shard_map/cuts_gather/ppermute | solution.py:234
  54.9 0.0 collective-permute-done.1.refs_2_
  54.9 3.0 %collective-permute-start.3 = (f32[32,1024]{1,0:T(8,128)S(1)}, f32[32,1024]{1,0:T(8,128)S(1)}, u32[]{:S(2)}, u32[]{:S(2)}) collective-permute-start(f32[32,1024]{1,0:T(8,128)S(1)} %collective-permute-done.1.refs_2_), channel_id=1, source_target_pairs={{0,128},{128,0},{1,129},{129,1},{2,130},{130,2},{3,131},{131,3},{4... | collective-permute-start | bytes 393224 | tf_op jit(solution)/shard_map/cuts_gather/ppermute | solution.py:235
  57.9 0.0 collective-permute-done.2.refs_3_
  57.9 2.5 %collective-permute-start.4 = (f32[32,1024]{1,0:T(8,128)S(1)}, f32[32,1024]{1,0:T(8,128)S(1)}, u32[]{:S(2)}, u32[]{:S(2)}) collective-permute-start(f32[32,1024]{1,0:T(8,128)S(1)} %collective-permute-done.2.refs_3_), channel_id=1, source_target_pairs={{0,128},{128,0},{1,129},{129,1},{2,130},{130,2},{3,131},{131,3},{4... | collective-permute-start | bytes 393224 | tf_op jit(solution)/shard_map/cuts_gather/ppermute | solution.py:235
  60.4 0.0 collective-permute-done.3.refs_4_
  60.4 0.9 %collective-permute-done.4.refs_5_ = f32[32,1024]{1,0:T(8,128)S(1)} collective-permute-done((f32[32,1024]{1,0:T(8,128)S(1)}, f32[32,1024]{1,0:T(8,128)S(1)}, u32[]{:S(2)}, u32[]{:S(2)}) %collective-permute-start.4) | collective-permute-done | bytes 131104 | tf_op jit(solution)/shard_map/cuts_gather/ppermute | solution.py:235
  61.3 0.0 collective-permute-done.refs_1_
  61.4 0.0 all-to-all-done.1
  61.4 1.1 %join.1 = f32[16,8,8,128]{3,2,1,0:T(8,128)S(1)} custom-call(s32[1]{0:T(128)} %bitcast.cut_ref, f32[4,8,16,128]{3,2,1,0:T(8,128)S(1)} %bitcast.8, f32[64,1024]{1,0:T(8,128)S(1)} %get-tuple-element.8.refs_0_, f32[64,1024]{1,0:T(8,128)S(1)} %collective-permute-done.refs_1_, f32[32,1024]{1,0:T(8,128)S(1)} %collective-permute-done.1.refs_2_, ...), custom_call_target="tpu_custom_call" | custom-call | flops 134217728 | bytes 2097152 | tf_op jit(solution)/shard_map/join/pallas_call | solution.py:237
  62.5 13.4 %all_to_all.20.parts_ref = f32[16,8,8,128]{3,2,1,0:T(8,128)S(1)} all-to-all(f32[16,8,8,128]{3,2,1,0:T(8,128)S(1)} %join.1), channel_id=1, replica_groups=mesh['yh'=2,'core'=2,'yl'=2,'x'=4,'za'=8,'zb'=2] {'yl','x','zb'}, dimensions={0} | all-to-all | bytes 1048576 | tf_op jit(solution)/shard_map/sum_move/all_to_all | solution.py:247
  75.9 0.1 sum.1
  76.0 13.8 %all_to_all.21.parts_ref = f32[8,8,128]{2,1,0:T(8,128)S(1)} all-to-all(f32[8,8,128]{2,1,0:T(8,128)S(1)} %sum.1), channel_id=1, replica_groups={{8,10,12,14,0,2,4,6},{9,11,13,15,1,3,5,7},{24,26,28,30,16,18,20,22},{25..., dimensions={0} | all-to-all | bytes 65536 | tf_op jit(solution)/shard_map/last_move/all_to_all | solution.py:258
  89.8 0.6 finish.1
Async XLA Ops:
  2.2 18.4 %all-to-all-start = ((f32[16,132,128]{2,1,0:T(8,128)}), f32[16,132,128]{2,1,0:T(8,128)S(1)}, u32[]{:S(2)}, u32[]{:S(2)}) async-start(f32[16,132,128]{2,1,0:T(8,128)} %pack.1), calls=%async_computation | async-start | bytes 2228224 | tf_op jit(solution)/shard_map/near_move/all_to_all | solution.py:210
  10.3 33.5 %copy-start = (f32[2,2,128,4]{2,3,1,0:T(4,128)S(1)}, f32[2,2,128,4]{2,3,1,0:T(4,128)}, u32[]{:S(2)}) copy-start(f32[2,2,128,4]{2,3,1,0:T(4,128)} %param.5) | copy-start | bytes 24580
  21.4 40.0 %all-to-all-start.1 = ((f32[32,16,128]{2,1,0:T(8,128)}), f32[32,16,128]{2,1,0:T(8,128)S(1)}, u32[]{:S(2)}, u32[]{:S(2)}) async-start(f32[32,16,128]{2,1,0:T(8,128)} %bitcast.4), calls=%async_computation.1 | async-start | bytes 524288 | tf_op jit(solution)/shard_map/right_move/all_to_all | solution.py:219
  45.2 9.6 %collective-permute-start.1 = (f32[32,1024]{1,0:T(8,128)S(1)}, f32[32,1024]{1,0:T(8,128)S(1)}, u32[]{:S(2)}, u32[]{:S(2)}) collective-permute-start(f32[32,1024]{1,0:T(8,128)S(1)} %get-tuple-element.9), channel_id=1, source_target_pairs={{0,256},{256,0},{1,257},{257,1},{2,258},{258,2},{3,259},{259,3},{4... | collective-permute-start | bytes 393224 | tf_op jit(solution)/shard_map/cuts_gather/ppermute | solution.py:233
  47.4 10.5 %collective-permute-start.2 = (f32[32,1024]{1,0:T(8,128)S(1)}, f32[32,1024]{1,0:T(8,128)S(1)}, u32[]{:S(2)}, u32[]{:S(2)}) collective-permute-start(f32[32,1024]{1,0:T(8,128)S(1)} %get-tuple-element.10), channel_id=1, source_target_pairs={{0,256},{256,0},{1,257},{257,1},{2,258},{258,2},{3,259},{259,3},{4... | collective-permute-start | bytes 393224 | tf_op jit(solution)/shard_map/cuts_gather/ppermute | solution.py:233
  52.0 9.3 %collective-permute-start = (f32[64,1024]{1,0:T(8,128)S(1)}, f32[64,1024]{1,0:T(8,128)S(1)}, u32[]{:S(2)}, u32[]{:S(2)}) collective-permute-start(f32[64,1024]{1,0:T(8,128)S(1)} %get-tuple-element.8.refs_0_), channel_id=1, source_target_pairs={{0,128},{128,0},{1,129},{129,1},{2,130},{130,2},{3,131},{131,3},{4... | collective-permute-start | bytes 786440 | tf_op jit(solution)/shard_map/cuts_gather/ppermute | solution.py:234
  54.9 5.5 %collective-permute-start.3 = (f32[32,1024]{1,0:T(8,128)S(1)}, f32[32,1024]{1,0:T(8,128)S(1)}, u32[]{:S(2)}, u32[]{:S(2)}) collective-permute-start(f32[32,1024]{1,0:T(8,128)S(1)} %collective-permute-done.1.refs_2_), channel_id=1, source_target_pairs={{0,128},{128,0},{1,129},{129,1},{2,130},{130,2},{3,131},{131,3},{4... | collective-permute-start | bytes 393224 | tf_op jit(solution)/shard_map/cuts_gather/ppermute | solution.py:235
  57.9 3.4 %collective-permute-start.4 = (f32[32,1024]{1,0:T(8,128)S(1)}, f32[32,1024]{1,0:T(8,128)S(1)}, u32[]{:S(2)}, u32[]{:S(2)}) collective-permute-start(f32[32,1024]{1,0:T(8,128)S(1)} %collective-permute-done.2.refs_3_), channel_id=1, source_target_pairs={{0,128},{128,0},{1,129},{129,1},{2,130},{130,2},{3,131},{131,3},{4... | collective-permute-start | bytes 393224 | tf_op jit(solution)/shard_map/cuts_gather/ppermute | solution.py:235

commit v16 on v15

--- a/solution.py
+++ b/solution.py
@@ -230,8 +230,10 @@
         to=[VMEM] * (1 + slices),
     )(here, closing_tensor.transpose(0, 1, 3, 2), x)
     with jax.named_scope("cuts_gather"):
-        x2 = [lax.ppermute(piece, "yh", swap) for piece in pieces]
+        x2 = [lax.ppermute(pieces[0], "yh", swap)]
         x1 = lax.ppermute(x0, "core", swap)
+        *pieces, x1 = lax.optimization_barrier((*pieces, x1))
+        x2 += [lax.ppermute(piece, "yh", swap) for piece in pieces[1:]]
         x3 = [lax.ppermute(piece, "core", swap) for piece in x2]
 
     p = kernel_call(

time: 91.9 us -> 93.6 us (1.018)
  waiting for transfers between devices: 11.2 us -> 13 us
    ppermute x2, waiting for transfers between devices: 0.01 us -> 1.74 us  [the longest x1 1.73 us: shards(): x2 = [lax.ppermute(pieces[0], 'yh', swap)]]
  transfers between devices with their start and end apart: 7 -> 7, of which waited for: 2 -> 3; matrix products, arithmetic and copies ran while one was open for 0% -> 0% of each run, Pallas kernels for 2% -> 2%
where the time goes in v16:
time: 93.6 us; the launch traced here: 92 us
  starting transfers between devices  45.7 us (49%)
  blocking collectives  27.1 us (29%)
  waiting for transfers between devices  13 us (14%)
  Pallas kernels  6.14 us (7%)
    all_to_all x1, starting transfers between devices, shards(): lax.all_to_all(r, CUTS + (FAR,), 0, 0, tiled=True, axis_index_groups=[gro...  22.4 us
    all_to_all x1, blocking collectives, shards(): p = lax.all_to_all(p, FAR, 0, 0, tiled=True, axis_index_groups=[group])  13.9 us
    all_to_all x1, blocking collectives, shards(): p = lax.all_to_all(p, NEAR, 0, 0, tiled=True)  13.2 us
    all_to_all x1, waiting for transfers between devices, shards(): x = lax.all_to_all(x, NEAR, 0, 0, tiled=True, axis_index_groups=[ORDER])  10.3 us
    all_to_all x1, starting transfers between devices, shards(): x = lax.all_to_all(x, NEAR, 0, 0, tiled=True, axis_index_groups=[ORDER])  8.11 us
    ppermute x2, starting transfers between devices, shards(): x3 = [lax.ppermute(piece, 'core', swap) for piece in x2]  6.1 us
    ppermute x1, starting transfers between devices, shards(): x2 += [lax.ppermute(piece, 'yh', swap) for piece in pieces[1:]]  4.6 us
    ppermute x1, starting transfers between devices, shards(): x1 = lax.ppermute(x0, 'core', swap)  2.25 us
  transfers between devices with their start and end apart: 7, of which 3 were waited for; matrix products, arithmetic and copies ran while one was open for 0% of the time, Pallas kernels for 2%

profile of v16, /device:TPU:1, one launch (start us, length us, event | category | flops | bytes accessed | tf_op | source)
XLA Modules:
  0.0 92.0 jit_solution(16853537809935538769)
XLA Ops:
  0.0 2.2 %pack.1 = f32[16,132,128]{2,1,0:T(8,128)} custom-call(f32[2,2,16,32,128]{4,3,2,1,0:T(8,128)} %bitcast.10, f32[2,2,4,512]{3,2,1,0:T(4,128)} %bitcast.11), custom_call_target="tpu_custom_call" | custom-call | bytes 2097152 | tf_op jit(solution)/shard_map/pack/pallas_call | solution.py:192
  2.2 8.1 %all-to-all-start = ((f32[16,132,128]{2,1,0:T(8,128)}), f32[16,132,128]{2,1,0:T(8,128)S(1)}, u32[]{:S(2)}, u32[]{:S(2)}) async-start(f32[16,132,128]{2,1,0:T(8,128)} %pack.1), calls=%async_computation | async-start | bytes 2228224 | tf_op jit(solution)/shard_map/near_move/all_to_all | solution.py:210
  10.3 0.0 copy-start
  10.3 10.3 %all-to-all-done.near_ref.left_ref = f32[16,132,128]{2,1,0:T(8,128)S(1)} async-done(((f32[16,132,128]{2,1,0:T(8,128)}), f32[16,132,128]{2,1,0:T(8,128)S(1)}, u32[]{:S(2)}, u32[]{:S(2)}) %all-to-all-start) | async-done | bytes 1081376 | tf_op jit(solution)/shard_map/near_move/all_to_all | solution.py:210
  20.6 0.7 spread.1
  21.4 22.4 %all-to-all-start.1 = ((f32[32,16,128]{2,1,0:T(8,128)}), f32[32,16,128]{2,1,0:T(8,128)S(1)}, u32[]{:S(2)}, u32[]{:S(2)}) async-start(f32[32,16,128]{2,1,0:T(8,128)} %bitcast.4), calls=%async_computation.1 | async-start | bytes 524288 | tf_op jit(solution)/shard_map/right_move/all_to_all | solution.py:219
  43.8 0.0 copy-done
  43.8 1.4 %close.1 = (f32[64,1024]{1,0:T(8,128)S(1)}, f32[32,1024]{1,0:T(8,128)S(1)}, f32[32,1024]{1,0:T(8,128)S(1)}) custom-call(s32[1]{0:T(128)} %bitcast.1.far_ref, f32[2,2,4,128]{3,2,1,0:T(4,128)S(1)} %bitcast.9, f32[16,132,128]{2,1,0:T(8,128)S(1)} %all-to-all-done.near_ref.left_ref), custom_call_target="tpu_custom_call" | custom-call | flops 4194304 | bytes 1572864 | tf_op jit(solution)/shard_map/close/pallas_call | solution.py:224
  45.2 2.3 %collective-permute-start = (f32[64,1024]{1,0:T(8,128)S(1)}, f32[64,1024]{1,0:T(8,128)S(1)}, u32[]{:S(2)}, u32[]{:S(2)}) collective-permute-start(f32[64,1024]{1,0:T(8,128)S(1)} %get-tuple-element.10.refs_0_), channel_id=1, source_target_pairs={{0,128},{128,0},{1,129},{129,1},{2,130},{130,2},{3,131},{131,3},{4... | collective-permute-start | bytes 786440 | tf_op jit(solution)/shard_map/cuts_gather/ppermute | solution.py:234
  47.5 2.2 %collective-permute-start.1 = (f32[32,1024]{1,0:T(8,128)S(1)}, f32[32,1024]{1,0:T(8,128)S(1)}, u32[]{:S(2)}, u32[]{:S(2)}) collective-permute-start(f32[32,1024]{1,0:T(8,128)S(1)} %get-tuple-element.11), channel_id=1, source_target_pairs={{0,256},{256,0},{1,257},{257,1},{2,258},{258,2},{3,259},{259,3},{4... | collective-permute-start | bytes 393224 | tf_op jit(solution)/shard_map/cuts_gather/ppermute | solution.py:233
  49.7 0.0 collective-permute-done.refs_1_
  49.7 4.6 %collective-permute-start.2 = (f32[32,1024]{1,0:T(8,128)S(1)}, f32[32,1024]{1,0:T(8,128)S(1)}, u32[]{:S(2)}, u32[]{:S(2)}) collective-permute-start(f32[32,1024]{1,0:T(8,128)S(1)} %get-tuple-element.14), channel_id=1, source_target_pairs={{0,256},{256,0},{1,257},{257,1},{2,258},{258,2},{3,259},{259,3},{4... | collective-permute-start | bytes 393224 | tf_op jit(solution)/shard_map/cuts_gather/ppermute | solution.py:236
  54.3 1.7 %collective-permute-done.1.refs_2_ = f32[32,1024]{1,0:T(8,128)S(1)} collective-permute-done((f32[32,1024]{1,0:T(8,128)S(1)}, f32[32,1024]{1,0:T(8,128)S(1)}, u32[]{:S(2)}, u32[]{:S(2)}) %collective-permute-start.1) | collective-permute-done | bytes 131104 | tf_op jit(solution)/shard_map/cuts_gather/ppermute | solution.py:233
  56.0 3.6 %collective-permute-start.3 = (f32[32,1024]{1,0:T(8,128)S(1)}, f32[32,1024]{1,0:T(8,128)S(1)}, u32[]{:S(2)}, u32[]{:S(2)}) collective-permute-start(f32[32,1024]{1,0:T(8,128)S(1)} %collective-permute-done.1.refs_2_), channel_id=1, source_target_pairs={{0,128},{128,0},{1,129},{129,1},{2,130},{130,2},{3,131},{131,3},{4... | collective-permute-start | bytes 393224 | tf_op jit(solution)/shard_map/cuts_gather/ppermute | solution.py:237
  59.6 0.0 collective-permute-done.2.refs_3_
  59.7 2.5 %collective-permute-start.4 = (f32[32,1024]{1,0:T(8,128)S(1)}, f32[32,1024]{1,0:T(8,128)S(1)}, u32[]{:S(2)}, u32[]{:S(2)}) collective-permute-start(f32[32,1024]{1,0:T(8,128)S(1)} %collective-permute-done.2.refs_3_), channel_id=1, source_target_pairs={{0,128},{128,0},{1,129},{129,1},{2,130},{130,2},{3,131},{131,3},{4... | collective-permute-start | bytes 393224 | tf_op jit(solution)/shard_map/cuts_gather/ppermute | solution.py:237
  62.2 0.0 collective-permute-done.3.refs_4_
  62.2 0.9 %collective-permute-done.4.refs_5_ = f32[32,1024]{1,0:T(8,128)S(1)} collective-permute-done((f32[32,1024]{1,0:T(8,128)S(1)}, f32[32,1024]{1,0:T(8,128)S(1)}, u32[]{:S(2)}, u32[]{:S(2)}) %collective-permute-start.4) | collective-permute-done | bytes 131104 | tf_op jit(solution)/shard_map/cuts_gather/ppermute | solution.py:237
  63.1 0.0 all-to-all-done.1
  63.1 1.1 %join.1 = f32[16,8,8,128]{3,2,1,0:T(8,128)S(1)} custom-call(s32[1]{0:T(128)} %bitcast.cut_ref, f32[4,8,16,128]{3,2,1,0:T(8,128)S(1)} %bitcast.8, f32[64,1024]{1,0:T(8,128)S(1)} %get-tuple-element.10.refs_0_, f32[64,1024]{1,0:T(8,128)S(1)} %collective-permute-done.refs_1_, f32[32,1024]{1,0:T(8,128)S(1)} %collective-permute-done.1.refs_2_, ...), custom_call_target="tpu_custom_call" | custom-call | flops 134217728 | bytes 2097152 | tf_op jit(solution)/shard_map/join/pallas_call | solution.py:239
  64.3 13.2 %all_to_all.20.parts_ref = f32[16,8,8,128]{3,2,1,0:T(8,128)S(1)} all-to-all(f32[16,8,8,128]{3,2,1,0:T(8,128)S(1)} %join.1), channel_id=1, replica_groups=mesh['yh'=2,'core'=2,'yl'=2,'x'=4,'za'=8,'zb'=2] {'yl','x','zb'}, dimensions={0} | all-to-all | bytes 1048576 | tf_op jit(solution)/shard_map/sum_move/all_to_all | solution.py:249
  77.5 0.1 sum.1
  77.5 13.9 %all_to_all.21.parts_ref = f32[8,8,128]{2,1,0:T(8,128)S(1)} all-to-all(f32[8,8,128]{2,1,0:T(8,128)S(1)} %sum.1), channel_id=1, replica_groups={{8,10,12,14,0,2,4,6},{9,11,13,15,1,3,5,7},{24,26,28,30,16,18,20,22},{25..., dimensions={0} | all-to-all | bytes 65536 | tf_op jit(solution)/shard_map/last_move/all_to_all | solution.py:260
  91.4 0.6 finish.1
Async XLA Ops:
  2.2 18.4 %all-to-all-start = ((f32[16,132,128]{2,1,0:T(8,128)}), f32[16,132,128]{2,1,0:T(8,128)S(1)}, u32[]{:S(2)}, u32[]{:S(2)}) async-start(f32[16,132,128]{2,1,0:T(8,128)} %pack.1), calls=%async_computation | async-start | bytes 2228224 | tf_op jit(solution)/shard_map/near_move/all_to_all | solution.py:210
  10.3 33.5 %copy-start = (f32[2,2,128,4]{2,3,1,0:T(4,128)S(1)}, f32[2,2,128,4]{2,3,1,0:T(4,128)}, u32[]{:S(2)}) copy-start(f32[2,2,128,4]{2,3,1,0:T(4,128)} %param.5) | copy-start | bytes 24580
  21.4 41.8 %all-to-all-start.1 = ((f32[32,16,128]{2,1,0:T(8,128)}), f32[32,16,128]{2,1,0:T(8,128)S(1)}, u32[]{:S(2)}, u32[]{:S(2)}) async-start(f32[32,16,128]{2,1,0:T(8,128)} %bitcast.4), calls=%async_computation.1 | async-start | bytes 524288 | tf_op jit(solution)/shard_map/right_move/all_to_all | solution.py:219
  45.2 4.5 %collective-permute-start = (f32[64,1024]{1,0:T(8,128)S(1)}, f32[64,1024]{1,0:T(8,128)S(1)}, u32[]{:S(2)}, u32[]{:S(2)}) collective-permute-start(f32[64,1024]{1,0:T(8,128)S(1)} %get-tuple-element.10.refs_0_), channel_id=1, source_target_pairs={{0,128},{128,0},{1,129},{129,1},{2,130},{130,2},{3,131},{131,3},{4... | collective-permute-start | bytes 786440 | tf_op jit(solution)/shard_map/cuts_gather/ppermute | solution.py:234
  47.5 8.5 %collective-permute-start.1 = (f32[32,1024]{1,0:T(8,128)S(1)}, f32[32,1024]{1,0:T(8,128)S(1)}, u32[]{:S(2)}, u32[]{:S(2)}) collective-permute-start(f32[32,1024]{1,0:T(8,128)S(1)} %get-tuple-element.11), channel_id=1, source_target_pairs={{0,256},{256,0},{1,257},{257,1},{2,258},{258,2},{3,259},{259,3},{4... | collective-permute-start | bytes 393224 | tf_op jit(solution)/shard_map/cuts_gather/ppermute | solution.py:233
  49.7 9.9 %collective-permute-start.2 = (f32[32,1024]{1,0:T(8,128)S(1)}, f32[32,1024]{1,0:T(8,128)S(1)}, u32[]{:S(2)}, u32[]{:S(2)}) collective-permute-start(f32[32,1024]{1,0:T(8,128)S(1)} %get-tuple-element.14), channel_id=1, source_target_pairs={{0,256},{256,0},{1,257},{257,1},{2,258},{258,2},{3,259},{259,3},{4... | collective-permute-start | bytes 393224 | tf_op jit(solution)/shard_map/cuts_gather/ppermute | solution.py:236
  56.0 6.1 %collective-permute-start.3 = (f32[32,1024]{1,0:T(8,128)S(1)}, f32[32,1024]{1,0:T(8,128)S(1)}, u32[]{:S(2)}, u32[]{:S(2)}) collective-permute-start(f32[32,1024]{1,0:T(8,128)S(1)} %collective-permute-done.1.refs_2_), channel_id=1, source_target_pairs={{0,128},{128,0},{1,129},{129,1},{2,130},{130,2},{3,131},{131,3},{4... | collective-permute-start | bytes 393224 | tf_op jit(solution)/shard_map/cuts_gather/ppermute | solution.py:237
  59.7 3.5 %collective-permute-start.4 = (f32[32,1024]{1,0:T(8,128)S(1)}, f32[32,1024]{1,0:T(8,128)S(1)}, u32[]{:S(2)}, u32[]{:S(2)}) collective-permute-start(f32[32,1024]{1,0:T(8,128)S(1)} %collective-permute-done.2.refs_3_), channel_id=1, source_target_pairs={{0,128},{128,0},{1,129},{129,1},{2,130},{130,2},{3,131},{131,3},{4... | collective-permute-start | bytes 393224 | tf_op jit(solution)/shard_map/cuts_gather/ppermute | solution.py:237

commit v17 on v15

--- a/solution.py
+++ b/solution.py
@@ -74,7 +74,7 @@
         copy.wait()
 
 
-def spread_kernel(far_ref, near_ref, out_ref):
+def spread_kernel(coef_ref, near_ref, out_ref):
     cuts, far, width, _ = out_ref.shape
     body = near_ref.shape[1] - cuts * width // near_ref.shape[0]
     for q87 in range(cuts):
@@ -87,17 +87,27 @@
             out_ref[q87 ^ HALF, g] = out_ref[q87 ^ HALF, 0]
 
 
-def close_kernel(far_ref, coef_ref, left_ref, out_ref, *piece_refs):
+def coef_kernel(far_ref, closing_ref, out_ref):
+    slices, heads, each, _ = out_ref.shape
+    first = far_ref[0] * 2
+    lane = lax.broadcasted_iota(jnp.int32, (each, LANES), 1)
+    for s in range(slices):
+        rows = closing_ref[pl.ds(s * each, each), :]
+        for h in range(heads):
+            head = (ORDER[h] // 2) * 16 + first + ORDER[h] % 2
+            one = jnp.sum(jnp.where(lane == head, rows, 0.0), axis=1, keepdims=True)
+            out_ref[s, h] = jnp.broadcast_to(one, (each, LANES))
+
+
+def close_kernel(coef_ref, left_ref, out_ref, *piece_refs):
     heads = left_ref.shape[0]
-    outs = coef_ref.shape[2]
-    first = far_ref[0] * 2
+    outs = coef_ref.shape[2] // 2
     rows = 8
     for s, piece_ref in enumerate(piece_refs):
         depth = piece_ref.shape[0]
         acc = [[None] * (depth // rows) for _ in range(2 * outs)]
         for h in range(heads):
-            head = (ORDER[h] // 2) * 16 + first + ORDER[h] % 2
-            co = [coef_ref[s, j // outs, j % outs, head] for j in range(2 * outs)]
+            co = [jnp.broadcast_to(coef_ref[s, h, pl.ds(j, 1), :], (rows, LANES)) for j in range(2 * outs)]
             for kb in range(depth // rows):
                 at = 2 * s * depth + kb * rows
                 re = left_ref[h, pl.ds(at, rows), :]
@@ -209,10 +219,15 @@
     with jax.named_scope("near_move"):
         x = lax.all_to_all(x, NEAR, 0, 0, tiled=True, axis_index_groups=[ORDER])
 
+    heads = closing_tensor.shape[2]
+    co = kernel_call(
+        coef_kernel, (slices, near, 2 * outs, LANES), [SMEM, VMEM], (2**18, 2**18), "coef"
+    )(here, closing_tensor.transpose(0, 1, 3, 2).reshape(slices * 2 * outs, heads))
+
     cuts = 4
     r = kernel_call(
-        spread_kernel, (cuts, 8, near * width // cuts, LANES), [SMEM, VMEM], (0, 2**18), "spread"
-    )(here, x)
+        spread_kernel, (cuts, 8, near * width // cuts, LANES), [ANY, VMEM], (0, 2**18), "spread"
+    )(co, x)
     with jax.named_scope("right_move"):
         r = r.reshape(cuts * 8, near * width // cuts, LANES)
         group = [(c ^ HALF) * 8 + (f + MID) % 8 for c in range(cuts) for f in range(8)]
@@ -224,11 +239,11 @@
     x0, *pieces = kernel_call(
         close_kernel,
         [(slices * kk, wide)] + [(kk, wide)] * slices,
-        [SMEM, SMEM, VMEM],
+        [VMEM, VMEM],
         (2**22, 6 * 2**18),
         "close",
         to=[VMEM] * (1 + slices),
-    )(here, closing_tensor.transpose(0, 1, 3, 2), x)
+    )(co, x)
     with jax.named_scope("cuts_gather"):
         x2 = [lax.ppermute(piece, "yh", swap) for piece in pieces]
         x1 = lax.ppermute(x0, "core", swap)

time: 91.9 us -> 91.3 us (level)
  transfers between devices with their start and end apart: 7 -> 7, of which waited for: 2 -> 3; matrix products, arithmetic and copies ran while one was open for 0% -> 0% of each run, Pallas kernels for 2% -> 1%
where the time goes in v17:
time: 91.3 us; the launch traced here: 89.7 us
  starting transfers between devices  45.9 us (50%)
  blocking collectives  26.7 us (29%)
  waiting for transfers between devices  11.5 us (13%)
  Pallas kernels  5.45 us (6%)
    all_to_all x1, starting transfers between devices, shards(): lax.all_to_all(r, CUTS + (FAR,), 0, 0, tiled=True, axis_index_groups=[gro...  22.4 us
    all_to_all x1, blocking collectives, shards(): p = lax.all_to_all(p, FAR, 0, 0, tiled=True, axis_index_groups=[group])  13.9 us
    all_to_all x1, blocking collectives, shards(): p = lax.all_to_all(p, NEAR, 0, 0, tiled=True)  12.8 us
    all_to_all x1, waiting for transfers between devices, shards(): x = lax.all_to_all(x, NEAR, 0, 0, tiled=True, axis_index_groups=[ORDER])  10.2 us
    all_to_all x1, starting transfers between devices, shards(): x = lax.all_to_all(x, NEAR, 0, 0, tiled=True, axis_index_groups=[ORDER])  8.11 us
    ppermute x2, starting transfers between devices, shards(): x2 = [lax.ppermute(piece, 'yh', swap) for piece in pieces]  6.79 us
    ppermute x2, starting transfers between devices, shards(): x3 = [lax.ppermute(piece, 'core', swap) for piece in x2]  5.75 us
    ppermute x1, starting transfers between devices, shards(): x1 = lax.ppermute(x0, 'core', swap)  2.81 us
  transfers between devices with their start and end apart: 7, of which 3 were waited for; matrix products, arithmetic and copies ran while one was open for 0% of the time, Pallas kernels for 1%

profile of v17, /device:TPU:1, one launch (start us, length us, event | category | flops | bytes accessed | tf_op | source)
XLA Modules:
  0.0 89.7 jit_solution(17579584878794685480)
XLA Ops:
  0.0 2.2 %pack.1 = f32[16,132,128]{2,1,0:T(8,128)} custom-call(f32[2,2,16,32,128]{4,3,2,1,0:T(8,128)} %bitcast.12, f32[2,2,4,512]{3,2,1,0:T(4,128)} %bitcast.13), custom_call_target="tpu_custom_call" | custom-call | bytes 2097152 | tf_op jit(solution)/shard_map/pack/pallas_call | solution.py:202
  2.2 0.0 copy-start
  2.2 8.1 %all-to-all-start = ((f32[16,132,128]{2,1,0:T(8,128)}), f32[16,132,128]{2,1,0:T(8,128)S(1)}, u32[]{:S(2)}, u32[]{:S(2)}) async-start(f32[16,132,128]{2,1,0:T(8,128)} %pack.1), calls=%async_computation | async-start | bytes 2228224 | tf_op jit(solution)/shard_map/near_move/all_to_all | solution.py:220
  10.3 0.0 copy-done
  10.3 0.1 coef.1.coef_ref
  10.4 10.2 %all-to-all-done.near_ref.left_ref = f32[16,132,128]{2,1,0:T(8,128)S(1)} async-done(((f32[16,132,128]{2,1,0:T(8,128)}), f32[16,132,128]{2,1,0:T(8,128)S(1)}, u32[]{:S(2)}, u32[]{:S(2)}) %all-to-all-start) | async-done | bytes 1081376 | tf_op jit(solution)/shard_map/near_move/all_to_all | solution.py:220
  20.6 0.7 spread.1
  21.4 22.4 %all-to-all-start.1 = ((f32[32,16,128]{2,1,0:T(8,128)}), f32[32,16,128]{2,1,0:T(8,128)S(1)}, u32[]{:S(2)}, u32[]{:S(2)}) async-start(f32[32,16,128]{2,1,0:T(8,128)} %bitcast.6), calls=%async_computation.1 | async-start | bytes 524288 | tf_op jit(solution)/shard_map/right_move/all_to_all | solution.py:234
  43.8 0.6 close.1
  44.4 2.2 %collective-permute-start.1 = (f32[32,1024]{1,0:T(8,128)S(1)}, f32[32,1024]{1,0:T(8,128)S(1)}, u32[]{:S(2)}, u32[]{:S(2)}) collective-permute-start(f32[32,1024]{1,0:T(8,128)S(1)} %get-tuple-element.9), channel_id=1, source_target_pairs={{0,256},{256,0},{1,257},{257,1},{2,258},{258,2},{3,259},{259,3},{4... | collective-permute-start | bytes 393224 | tf_op jit(solution)/shard_map/cuts_gather/ppermute | solution.py:248
  46.6 4.6 %collective-permute-start.2 = (f32[32,1024]{1,0:T(8,128)S(1)}, f32[32,1024]{1,0:T(8,128)S(1)}, u32[]{:S(2)}, u32[]{:S(2)}) collective-permute-start(f32[32,1024]{1,0:T(8,128)S(1)} %get-tuple-element.10), channel_id=1, source_target_pairs={{0,256},{256,0},{1,257},{257,1},{2,258},{258,2},{3,259},{259,3},{4... | collective-permute-start | bytes 393224 | tf_op jit(solution)/shard_map/cuts_gather/ppermute | solution.py:248
  51.3 2.8 %collective-permute-start = (f32[64,1024]{1,0:T(8,128)S(1)}, f32[64,1024]{1,0:T(8,128)S(1)}, u32[]{:S(2)}, u32[]{:S(2)}) collective-permute-start(f32[64,1024]{1,0:T(8,128)S(1)} %get-tuple-element.8.refs_0_), channel_id=1, source_target_pairs={{0,128},{128,0},{1,129},{129,1},{2,130},{130,2},{3,131},{131,3},{4... | collective-permute-start | bytes 786440 | tf_op jit(solution)/shard_map/cuts_gather/ppermute | solution.py:249
  54.1 0.0 collective-permute-done.1.refs_2_
  54.1 3.1 %collective-permute-start.3 = (f32[32,1024]{1,0:T(8,128)S(1)}, f32[32,1024]{1,0:T(8,128)S(1)}, u32[]{:S(2)}, u32[]{:S(2)}) collective-permute-start(f32[32,1024]{1,0:T(8,128)S(1)} %collective-permute-done.1.refs_2_), channel_id=1, source_target_pairs={{0,128},{128,0},{1,129},{129,1},{2,130},{130,2},{3,131},{131,3},{4... | collective-permute-start | bytes 393224 | tf_op jit(solution)/shard_map/cuts_gather/ppermute | solution.py:250
  57.1 0.0 collective-permute-done.2.refs_3_
  57.2 2.7 %collective-permute-start.4 = (f32[32,1024]{1,0:T(8,128)S(1)}, f32[32,1024]{1,0:T(8,128)S(1)}, u32[]{:S(2)}, u32[]{:S(2)}) collective-permute-start(f32[32,1024]{1,0:T(8,128)S(1)} %collective-permute-done.2.refs_3_), channel_id=1, source_target_pairs={{0,128},{128,0},{1,129},{129,1},{2,130},{130,2},{3,131},{131,3},{4... | collective-permute-start | bytes 393224 | tf_op jit(solution)/shard_map/cuts_gather/ppermute | solution.py:250
  59.9 0.0 collective-permute-done.3.refs_4_
  59.9 0.9 %collective-permute-done.4.refs_5_ = f32[32,1024]{1,0:T(8,128)S(1)} collective-permute-done((f32[32,1024]{1,0:T(8,128)S(1)}, f32[32,1024]{1,0:T(8,128)S(1)}, u32[]{:S(2)}, u32[]{:S(2)}) %collective-permute-start.4) | collective-permute-done | bytes 131104 | tf_op jit(solution)/shard_map/cuts_gather/ppermute | solution.py:250
  60.8 0.0 collective-permute-done.refs_1_
  60.8 0.3 all-to-all-done.1
  61.2 1.1 %join.1 = f32[16,8,8,128]{3,2,1,0:T(8,128)S(1)} custom-call(s32[1]{0:T(128)} %bitcast.cut_ref, f32[4,8,16,128]{3,2,1,0:T(8,128)S(1)} %bitcast.10, f32[64,1024]{1,0:T(8,128)S(1)} %get-tuple-element.8.refs_0_, f32[64,1024]{1,0:T(8,128)S(1)} %collective-permute-done.refs_1_, f32[32,1024]{1,0:T(8,128)S(1)} %collective-permute-done.1.refs_2_, ...), custom_call_target="tpu_custom_call" | custom-call | flops 134217728 | bytes 2097152 | tf_op jit(solution)/shard_map/join/pallas_call | solution.py:252
  62.3 12.8 %all_to_all.20.parts_ref = f32[16,8,8,128]{3,2,1,0:T(8,128)S(1)} all-to-all(f32[16,8,8,128]{3,2,1,0:T(8,128)S(1)} %join.1), channel_id=1, replica_groups=mesh['yh'=2,'core'=2,'yl'=2,'x'=4,'za'=8,'zb'=2] {'yl','x','zb'}, dimensions={0} | all-to-all | bytes 1048576 | tf_op jit(solution)/shard_map/sum_move/all_to_all | solution.py:262
  75.1 0.1 sum.1
  75.2 13.9 %all_to_all.21.parts_ref = f32[8,8,128]{2,1,0:T(8,128)S(1)} all-to-all(f32[8,8,128]{2,1,0:T(8,128)S(1)} %sum.1), channel_id=1, replica_groups={{8,10,12,14,0,2,4,6},{9,11,13,15,1,3,5,7},{24,26,28,30,16,18,20,22},{25..., dimensions={0} | all-to-all | bytes 65536 | tf_op jit(solution)/shard_map/last_move/all_to_all | solution.py:273
  89.1 0.6 finish.1
Async XLA Ops:
  2.2 8.1 %copy-start = (f32[2,2,128,4]{2,3,1,0:T(4,128)S(1)}, f32[2,2,128,4]{2,3,1,0:T(4,128)}, u32[]{:S(2)}) copy-start(f32[2,2,128,4]{2,3,1,0:T(4,128)} %param.5) | copy-start | bytes 24580
  2.2 18.4 %all-to-all-start = ((f32[16,132,128]{2,1,0:T(8,128)}), f32[16,132,128]{2,1,0:T(8,128)S(1)}, u32[]{:S(2)}, u32[]{:S(2)}) async-start(f32[16,132,128]{2,1,0:T(8,128)} %pack.1), calls=%async_computation | async-start | bytes 2228224 | tf_op jit(solution)/shard_map/near_move/all_to_all | solution.py:220
  21.4 39.8 %all-to-all-start.1 = ((f32[32,16,128]{2,1,0:T(8,128)}), f32[32,16,128]{2,1,0:T(8,128)S(1)}, u32[]{:S(2)}, u32[]{:S(2)}) async-start(f32[32,16,128]{2,1,0:T(8,128)} %bitcast.6), calls=%async_computation.1 | async-start | bytes 524288 | tf_op jit(solution)/shard_map/right_move/all_to_all | solution.py:234
  44.4 9.6 %collective-permute-start.1 = (f32[32,1024]{1,0:T(8,128)S(1)}, f32[32,1024]{1,0:T(8,128)S(1)}, u32[]{:S(2)}, u32[]{:S(2)}) collective-permute-start(f32[32,1024]{1,0:T(8,128)S(1)} %get-tuple-element.9), channel_id=1, source_target_pairs={{0,256},{256,0},{1,257},{257,1},{2,258},{258,2},{3,259},{259,3},{4... | collective-permute-start | bytes 393224 | tf_op jit(solution)/shard_map/cuts_gather/ppermute | solution.py:248
  46.6 10.5 %collective-permute-start.2 = (f32[32,1024]{1,0:T(8,128)S(1)}, f32[32,1024]{1,0:T(8,128)S(1)}, u32[]{:S(2)}, u32[]{:S(2)}) collective-permute-start(f32[32,1024]{1,0:T(8,128)S(1)} %get-tuple-element.10), channel_id=1, source_target_pairs={{0,256},{256,0},{1,257},{257,1},{2,258},{258,2},{3,259},{259,3},{4... | collective-permute-start | bytes 393224 | tf_op jit(solution)/shard_map/cuts_gather/ppermute | solution.py:248
  51.3 9.6 %collective-permute-start = (f32[64,1024]{1,0:T(8,128)S(1)}, f32[64,1024]{1,0:T(8,128)S(1)}, u32[]{:S(2)}, u32[]{:S(2)}) collective-permute-start(f32[64,1024]{1,0:T(8,128)S(1)} %get-tuple-element.8.refs_0_), channel_id=1, source_target_pairs={{0,128},{128,0},{1,129},{129,1},{2,130},{130,2},{3,131},{131,3},{4... | collective-permute-start | bytes 786440 | tf_op jit(solution)/shard_map/cuts_gather/ppermute | solution.py:249
  54.1 5.8 %collective-permute-start.3 = (f32[32,1024]{1,0:T(8,128)S(1)}, f32[32,1024]{1,0:T(8,128)S(1)}, u32[]{:S(2)}, u32[]{:S(2)}) collective-permute-start(f32[32,1024]{1,0:T(8,128)S(1)} %collective-permute-done.1.refs_2_), channel_id=1, source_target_pairs={{0,128},{128,0},{1,129},{129,1},{2,130},{130,2},{3,131},{131,3},{4... | collective-permute-start | bytes 393224 | tf_op jit(solution)/shard_map/cuts_gather/ppermute | solution.py:250
  57.2 3.7 %collective-permute-start.4 = (f32[32,1024]{1,0:T(8,128)S(1)}, f32[32,1024]{1,0:T(8,128)S(1)}, u32[]{:S(2)}, u32[]{:S(2)}) collective-permute-start(f32[32,1024]{1,0:T(8,128)S(1)} %collective-permute-done.2.refs_3_), channel_id=1, source_target_pairs={{0,128},{128,0},{1,129},{129,1},{2,130},{130,2},{3,131},{131,3},{4... | collective-permute-start | bytes 393224 | tf_op jit(solution)/shard_map/cuts_gather/ppermute | solution.py:250

commit v18 on v17

--- a/solution.py
+++ b/solution.py
@@ -158,7 +158,7 @@
         out_ref[:, j + 1, :, :] = out[:, LANES:].reshape(16, 8, LANES)
 
 
-def sum_kernel(scale, parts_ref, out_ref):
+def sum_kernel(scale, tie_ref, parts_ref, out_ref):
     for j in range(parts_ref.shape[1]):
         total = parts_ref[0, j]
         for i in range(1, parts_ref.shape[0]):
@@ -166,7 +166,7 @@
         out_ref[:, j, :] = pltpu.roll(total * scale, (8 - LAST) % 8, 0)
 
 
-def finish_kernel(parts_ref, out_ref):
+def finish_kernel(tie_ref, parts_ref, out_ref):
     total = parts_ref[0]
     for i in range(1, parts_ref.shape[0]):
         total = total + parts_ref[i]
@@ -259,19 +259,21 @@
     )(lax.axis_index(CUTS).reshape(1), r, x0, x1, *x2, *x3)
 
     with jax.named_scope("sum_move"):
+        tie = p[:1, :1]
         p = lax.all_to_all(p, NEAR, 0, 0, tiled=True)
     p = kernel_call(
         functools.partial(sum_kernel, (slices * cuts) ** -0.5),
         (8, 2 * outs, rows),
-        [VMEM],
+        [ANY, VMEM],
         (2**18, 2**20),
         "sum",
-    )(p)
+    )(tie, p)
 
     with jax.named_scope("last_move"):
+        tie = p[:1]
         group = [(f + LAST) % 8 for f in range(8)]
         p = lax.all_to_all(p, FAR, 0, 0, tiled=True, axis_index_groups=[group])
-    p = kernel_call(finish_kernel, (outs, 2, rows), [VMEM], (2**14, 2**17), "finish")(p)
+    p = kernel_call(finish_kernel, (outs, 2, rows), [ANY, VMEM], (2**14, 2**17), "finish")(tie, p)
     return p.reshape(1, outs, 2, rows)
 
 

time: 91.3 us -> 93.2 us (1.021)
  blocking collectives: 26.7 us -> 0 us
  starting transfers between devices: 45.9 us -> 62 us
  waiting for transfers between devices: 11.5 us -> 21.1 us
  Pallas kernels: 5.45 us -> 6.85 us
  local copies, waits for them, and re-layouts: 0.01 us -> 1.4 us
    all_to_all x2 -> x0, blocking collectives: 26.7 us -> none  [the longest x1 13.9 us: shards(): p = lax.all_to_all(p, FAR, 0, 0, tiled=True, axis_index_groups=[group])]
    all_to_all x0 -> x2, starting transfers between devices: none -> 16.1 us  [the longest x1 11.8 us: shards(): p = lax.all_to_all(p, FAR, 0, 0, tiled=True, axis_index_groups=[group])]
    all_to_all x0 -> x2, waiting for transfers between devices: none -> 9.63 us  [the longest x1 8.05 us: shards(): p = lax.all_to_all(p, NEAR, 0, 0, tiled=True)]
    slice x0 -> x2, local copies, waits for them, and re-layouts: none -> 1.4 us  [the longest x1 0.71 us: shards(): tie = p[:1]]
  transfers between devices with their start and end apart: 7 -> 9, of which waited for: 3 -> 5; matrix products, arithmetic and copies ran while one was open for 0% -> 2% of each run, Pallas kernels for 1% -> 1%
where the time goes in v18:
time: 93.2 us; the launch traced here: 91.5 us
  starting transfers between devices  62 us (67%)
  waiting for transfers between devices  21.1 us (23%)
  Pallas kernels  6.85 us (7%)
  local copies, waits for them, and re-layouts  1.4 us (2%)
    all_to_all x1, starting transfers between devices, shards(): lax.all_to_all(r, CUTS + (FAR,), 0, 0, tiled=True, axis_index_groups=[gro...  22.4 us
    all_to_all x1, starting transfers between devices, shards(): p = lax.all_to_all(p, FAR, 0, 0, tiled=True, axis_index_groups=[group])  11.8 us
    all_to_all x1, waiting for transfers between devices, shards(): x = lax.all_to_all(x, NEAR, 0, 0, tiled=True, axis_index_groups=[ORDER])  10.2 us
    all_to_all x1, starting transfers between devices, shards(): x = lax.all_to_all(x, NEAR, 0, 0, tiled=True, axis_index_groups=[ORDER])  8.11 us
    all_to_all x1, waiting for transfers between devices, shards(): p = lax.all_to_all(p, NEAR, 0, 0, tiled=True)  8.05 us
    ppermute x2, starting transfers between devices, shards(): x2 = [lax.ppermute(piece, 'yh', swap) for piece in pieces]  6.79 us
    ppermute x2, starting transfers between devices, shards(): x3 = [lax.ppermute(piece, 'core', swap) for piece in x2]  5.75 us
    all_to_all x1, starting transfers between devices, shards(): p = lax.all_to_all(p, NEAR, 0, 0, tiled=True)  4.3 us
  transfers between devices with their start and end apart: 9, of which 5 were waited for; matrix products, arithmetic and copies ran while one was open for 2% of the time, Pallas kernels for 1%

profile of v18, /device:TPU:1, one launch (start us, length us, event | category | flops | bytes accessed | tf_op | source)
XLA Modules:
  0.0 91.5 jit_solution(12368495317921509125)
XLA Ops:
  0.0 2.2 %pack.1 = f32[16,132,128]{2,1,0:T(8,128)} custom-call(f32[2,2,16,32,128]{4,3,2,1,0:T(8,128)} %bitcast.12, f32[2,2,4,512]{3,2,1,0:T(4,128)} %bitcast.13), custom_call_target="tpu_custom_call" | custom-call | bytes 2097152 | tf_op jit(solution)/shard_map/pack/pallas_call | solution.py:202
  2.2 0.0 copy-start
  2.2 8.1 %all-to-all-start = ((f32[16,132,128]{2,1,0:T(8,128)}), f32[16,132,128]{2,1,0:T(8,128)S(1)}, u32[]{:S(2)}, u32[]{:S(2)}) async-start(f32[16,132,128]{2,1,0:T(8,128)} %pack.1), calls=%async_computation | async-start | bytes 2228224 | tf_op jit(solution)/shard_map/near_move/all_to_all | solution.py:220
  10.3 0.0 copy-done
  10.3 0.1 coef.1.coef_ref
  10.4 10.2 %all-to-all-done.near_ref.left_ref = f32[16,132,128]{2,1,0:T(8,128)S(1)} async-done(((f32[16,132,128]{2,1,0:T(8,128)}), f32[16,132,128]{2,1,0:T(8,128)S(1)}, u32[]{:S(2)}, u32[]{:S(2)}) %all-to-all-start) | async-done | bytes 1081376 | tf_op jit(solution)/shard_map/near_move/all_to_all | solution.py:220
  20.6 0.7 spread.1
  21.4 22.4 %all-to-all-start.1 = ((f32[32,16,128]{2,1,0:T(8,128)}), f32[32,16,128]{2,1,0:T(8,128)S(1)}, u32[]{:S(2)}, u32[]{:S(2)}) async-start(f32[32,16,128]{2,1,0:T(8,128)} %bitcast.6), calls=%async_computation.1 | async-start | bytes 524288 | tf_op jit(solution)/shard_map/right_move/all_to_all | solution.py:234
  43.8 0.6 close.1
  44.4 2.2 %collective-permute-start.1 = (f32[32,1024]{1,0:T(8,128)S(1)}, f32[32,1024]{1,0:T(8,128)S(1)}, u32[]{:S(2)}, u32[]{:S(2)}) collective-permute-start(f32[32,1024]{1,0:T(8,128)S(1)} %get-tuple-element.9), channel_id=1, source_target_pairs={{0,256},{256,0},{1,257},{257,1},{2,258},{258,2},{3,259},{259,3},{4... | collective-permute-start | bytes 393224 | tf_op jit(solution)/shard_map/cuts_gather/ppermute | solution.py:248
  46.6 4.6 %collective-permute-start.2 = (f32[32,1024]{1,0:T(8,128)S(1)}, f32[32,1024]{1,0:T(8,128)S(1)}, u32[]{:S(2)}, u32[]{:S(2)}) collective-permute-start(f32[32,1024]{1,0:T(8,128)S(1)} %get-tuple-element.10), channel_id=1, source_target_pairs={{0,256},{256,0},{1,257},{257,1},{2,258},{258,2},{3,259},{259,3},{4... | collective-permute-start | bytes 393224 | tf_op jit(solution)/shard_map/cuts_gather/ppermute | solution.py:248
  51.2 2.8 %collective-permute-start = (f32[64,1024]{1,0:T(8,128)S(1)}, f32[64,1024]{1,0:T(8,128)S(1)}, u32[]{:S(2)}, u32[]{:S(2)}) collective-permute-start(f32[64,1024]{1,0:T(8,128)S(1)} %get-tuple-element.8.refs_0_), channel_id=1, source_target_pairs={{0,128},{128,0},{1,129},{129,1},{2,130},{130,2},{3,131},{131,3},{4... | collective-permute-start | bytes 786440 | tf_op jit(solution)/shard_map/cuts_gather/ppermute | solution.py:249
  54.1 0.0 collective-permute-done.1.refs_2_
  54.1 3.1 %collective-permute-start.3 = (f32[32,1024]{1,0:T(8,128)S(1)}, f32[32,1024]{1,0:T(8,128)S(1)}, u32[]{:S(2)}, u32[]{:S(2)}) collective-permute-start(f32[32,1024]{1,0:T(8,128)S(1)} %collective-permute-done.1.refs_2_), channel_id=1, source_target_pairs={{0,128},{128,0},{1,129},{129,1},{2,130},{130,2},{3,131},{131,3},{4... | collective-permute-start | bytes 393224 | tf_op jit(solution)/shard_map/cuts_gather/ppermute | solution.py:250
  57.1 0.0 collective-permute-done.2.refs_3_
  57.2 2.7 %collective-permute-start.4 = (f32[32,1024]{1,0:T(8,128)S(1)}, f32[32,1024]{1,0:T(8,128)S(1)}, u32[]{:S(2)}, u32[]{:S(2)}) collective-permute-start(f32[32,1024]{1,0:T(8,128)S(1)} %collective-permute-done.2.refs_3_), channel_id=1, source_target_pairs={{0,128},{128,0},{1,129},{129,1},{2,130},{130,2},{3,131},{131,3},{4... | collective-permute-start | bytes 393224 | tf_op jit(solution)/shard_map/cuts_gather/ppermute | solution.py:250
  59.9 0.0 collective-permute-done.3.refs_4_
  59.9 0.9 %collective-permute-done.4.refs_5_ = f32[32,1024]{1,0:T(8,128)S(1)} collective-permute-done((f32[32,1024]{1,0:T(8,128)S(1)}, f32[32,1024]{1,0:T(8,128)S(1)}, u32[]{:S(2)}, u32[]{:S(2)}) %collective-permute-start.4) | collective-permute-done | bytes 131104 | tf_op jit(solution)/shard_map/cuts_gather/ppermute | solution.py:250
  60.8 0.0 collective-permute-done.refs_1_
  60.8 0.3 all-to-all-done.1
  61.2 1.9 %join.1 = f32[16,8,8,128]{3,2,1,0:T(8,128)} custom-call(s32[1]{0:T(128)} %bitcast.cut_ref, f32[4,8,16,128]{3,2,1,0:T(8,128)S(1)} %bitcast.10, f32[64,1024]{1,0:T(8,128)S(1)} %get-tuple-element.8.refs_0_, f32[64,1024]{1,0:T(8,128)S(1)} %collective-permute-done.refs_1_, f32[32,1024]{1,0:T(8,128)S(1)} %collective-permute-done.1.refs_2_, ...), custom_call_target="tpu_custom_call" | custom-call | flops 134217728 | bytes 2097152 | tf_op jit(solution)/shard_map/join/pallas_call | solution.py:252
  63.1 4.3 %all-to-all-start.2 = ((f32[16,8,8,128]{3,2,1,0:T(8,128)}), f32[16,8,8,128]{3,2,1,0:T(8,128)S(1)}, u32[]{:S(2)}, u32[]{:S(2)}) async-start(f32[16,8,8,128]{3,2,1,0:T(8,128)} %join.1), calls=%async_computation.2 | async-start | bytes 1048576 | tf_op jit(solution)/shard_map/sum_move/all_to_all | solution.py:263
  67.4 0.7 slice.8.tie_ref
  68.1 8.0 %all-to-all-done.2.parts_ref = f32[16,8,8,128]{3,2,1,0:T(8,128)S(1)} async-done(((f32[16,8,8,128]{3,2,1,0:T(8,128)}), f32[16,8,8,128]{3,2,1,0:T(8,128)S(1)}, u32[]{:S(2)}, u32[]{:S(2)}) %all-to-all-start.2) | async-done | bytes 524320 | tf_op jit(solution)/shard_map/sum_move/all_to_all | solution.py:263
  76.1 0.7 sum.1
  76.8 11.8 %all-to-all-start.3 = ((f32[8,8,128]{2,1,0:T(8,128)}), f32[8,8,128]{2,1,0:T(8,128)S(1)}, u32[]{:S(2)}, u32[]{:S(2)}) async-start(f32[8,8,128]{2,1,0:T(8,128)} %sum.1), calls=%async_computation.3 | async-start | bytes 65536 | tf_op jit(solution)/shard_map/last_move/all_to_all | solution.py:275
  88.6 0.7 slice.9.tie_ref
  89.3 1.6 %all-to-all-done.3.parts_ref = f32[8,8,128]{2,1,0:T(8,128)S(1)} async-done(((f32[8,8,128]{2,1,0:T(8,128)}), f32[8,8,128]{2,1,0:T(8,128)S(1)}, u32[]{:S(2)}, u32[]{:S(2)}) %all-to-all-start.3) | async-done | bytes 32800 | tf_op jit(solution)/shard_map/last_move/all_to_all | solution.py:275
  90.9 0.6 finish.1
Async XLA Ops:
  2.2 8.1 %copy-start = (f32[2,2,128,4]{2,3,1,0:T(4,128)S(1)}, f32[2,2,128,4]{2,3,1,0:T(4,128)}, u32[]{:S(2)}) copy-start(f32[2,2,128,4]{2,3,1,0:T(4,128)} %param.5) | copy-start | bytes 24580
  2.2 18.4 %all-to-all-start = ((f32[16,132,128]{2,1,0:T(8,128)}), f32[16,132,128]{2,1,0:T(8,128)S(1)}, u32[]{:S(2)}, u32[]{:S(2)}) async-start(f32[16,132,128]{2,1,0:T(8,128)} %pack.1), calls=%async_computation | async-start | bytes 2228224 | tf_op jit(solution)/shard_map/near_move/all_to_all | solution.py:220
  21.4 39.8 %all-to-all-start.1 = ((f32[32,16,128]{2,1,0:T(8,128)}), f32[32,16,128]{2,1,0:T(8,128)S(1)}, u32[]{:S(2)}, u32[]{:S(2)}) async-start(f32[32,16,128]{2,1,0:T(8,128)} %bitcast.6), calls=%async_computation.1 | async-start | bytes 524288 | tf_op jit(solution)/shard_map/right_move/all_to_all | solution.py:234
  44.4 9.6 %collective-permute-start.1 = (f32[32,1024]{1,0:T(8,128)S(1)}, f32[32,1024]{1,0:T(8,128)S(1)}, u32[]{:S(2)}, u32[]{:S(2)}) collective-permute-start(f32[32,1024]{1,0:T(8,128)S(1)} %get-tuple-element.9), channel_id=1, source_target_pairs={{0,256},{256,0},{1,257},{257,1},{2,258},{258,2},{3,259},{259,3},{4... | collective-permute-start | bytes 393224 | tf_op jit(solution)/shard_map/cuts_gather/ppermute | solution.py:248
  46.6 10.5 %collective-permute-start.2 = (f32[32,1024]{1,0:T(8,128)S(1)}, f32[32,1024]{1,0:T(8,128)S(1)}, u32[]{:S(2)}, u32[]{:S(2)}) collective-permute-start(f32[32,1024]{1,0:T(8,128)S(1)} %get-tuple-element.10), channel_id=1, source_target_pairs={{0,256},{256,0},{1,257},{257,1},{2,258},{258,2},{3,259},{259,3},{4... | collective-permute-start | bytes 393224 | tf_op jit(solution)/shard_map/cuts_gather/ppermute | solution.py:248
  51.2 9.6 %collective-permute-start = (f32[64,1024]{1,0:T(8,128)S(1)}, f32[64,1024]{1,0:T(8,128)S(1)}, u32[]{:S(2)}, u32[]{:S(2)}) collective-permute-start(f32[64,1024]{1,0:T(8,128)S(1)} %get-tuple-element.8.refs_0_), channel_id=1, source_target_pairs={{0,128},{128,0},{1,129},{129,1},{2,130},{130,2},{3,131},{131,3},{4... | collective-permute-start | bytes 786440 | tf_op jit(solution)/shard_map/cuts_gather/ppermute | solution.py:249
  54.1 5.8 %collective-permute-start.3 = (f32[32,1024]{1,0:T(8,128)S(1)}, f32[32,1024]{1,0:T(8,128)S(1)}, u32[]{:S(2)}, u32[]{:S(2)}) collective-permute-start(f32[32,1024]{1,0:T(8,128)S(1)} %collective-permute-done.1.refs_2_), channel_id=1, source_target_pairs={{0,128},{128,0},{1,129},{129,1},{2,130},{130,2},{3,131},{131,3},{4... | collective-permute-start | bytes 393224 | tf_op jit(solution)/shard_map/cuts_gather/ppermute | solution.py:250
  57.2 3.7 %collective-permute-start.4 = (f32[32,1024]{1,0:T(8,128)S(1)}, f32[32,1024]{1,0:T(8,128)S(1)}, u32[]{:S(2)}, u32[]{:S(2)}) collective-permute-start(f32[32,1024]{1,0:T(8,128)S(1)} %collective-permute-done.2.refs_3_), channel_id=1, source_target_pairs={{0,128},{128,0},{1,129},{129,1},{2,130},{130,2},{3,131},{131,3},{4... | collective-permute-start | bytes 393224 | tf_op jit(solution)/shard_map/cuts_gather/ppermute | solution.py:250
  63.1 13.0 %all-to-all-start.2 = ((f32[16,8,8,128]{3,2,1,0:T(8,128)}), f32[16,8,8,128]{3,2,1,0:T(8,128)S(1)}, u32[]{:S(2)}, u32[]{:S(2)}) async-start(f32[16,8,8,128]{3,2,1,0:T(8,128)} %join.1), calls=%async_computation.2 | async-start | bytes 1048576 | tf_op jit(solution)/shard_map/sum_move/all_to_all | solution.py:263
  76.8 14.1 %all-to-all-start.3 = ((f32[8,8,128]{2,1,0:T(8,128)}), f32[8,8,128]{2,1,0:T(8,128)S(1)}, u32[]{:S(2)}, u32[]{:S(2)}) async-start(f32[8,8,128]{2,1,0:T(8,128)} %sum.1), calls=%async_computation.3 | async-start | bytes 65536 | tf_op jit(solution)/shard_map/last_move/all_to_all | solution.py:275

commit v19 on v17

--- a/solution.py
+++ b/solution.py
@@ -16,7 +16,7 @@
 
 F32 = jnp.float32
 LANES = 128
-MID = 6
+MID = 5
 HALF = 2
 LAST = 4
 ORDER = [yl * 8 + x * 2 + zb for x in (3, 1, 2, 0) for yl in (1, 0) for zb in range(2)]

time: 91.3 us -> 92.3 us (1.011)
    all_to_all x1, starting transfers between devices: 22.4 us -> 23.4 us  [shards(): lax.all_to_all(r, CUTS + (FAR,), 0, 0, tiled=True, axis_index_groups=[gro...]
  transfers between devices with their start and end apart: 7 -> 7, of which waited for: 3 -> 2; matrix products, arithmetic and copies ran while one was open for 0% -> 0% of each run, Pallas kernels for 1% -> 1%
where the time goes in v19:
time: 92.3 us; the launch traced here: 90.7 us
  starting transfers between devices  46.8 us (51%)
  blocking collectives  27.2 us (29%)
  waiting for transfers between devices  11.1 us (12%)
  Pallas kernels  5.45 us (6%)
    all_to_all x1, starting transfers between devices, shards(): lax.all_to_all(r, CUTS + (FAR,), 0, 0, tiled=True, axis_index_groups=[gro...  23.4 us
    all_to_all x1, blocking collectives, shards(): p = lax.all_to_all(p, NEAR, 0, 0, tiled=True)  13.7 us
    all_to_all x1, blocking collectives, shards(): p = lax.all_to_all(p, FAR, 0, 0, tiled=True, axis_index_groups=[group])  13.6 us
    all_to_all x1, waiting for transfers between devices, shards(): x = lax.all_to_all(x, NEAR, 0, 0, tiled=True, axis_index_groups=[ORDER])  10.2 us
    all_to_all x1, starting transfers between devices, shards(): x = lax.all_to_all(x, NEAR, 0, 0, tiled=True, axis_index_groups=[ORDER])  8.11 us
    ppermute x2, starting transfers between devices, shards(): x2 = [lax.ppermute(piece, 'yh', swap) for piece in pieces]  6.79 us
    ppermute x2, starting transfers between devices, shards(): x3 = [lax.ppermute(piece, 'core', swap) for piece in x2]  5.68 us
    ppermute x1, starting transfers between devices, shards(): x1 = lax.ppermute(x0, 'core', swap)  2.81 us
  transfers between devices with their start and end apart: 7, of which 2 were waited for; matrix products, arithmetic and copies ran while one was open for 0% of the time, Pallas kernels for 1%

profile of v19, /device:TPU:1, one launch (start us, length us, event | category | flops | bytes accessed | tf_op | source)
XLA Modules:
  0.0 90.7 jit_solution(8480611930307097717)
XLA Ops:
  0.0 2.2 %pack.1 = f32[16,132,128]{2,1,0:T(8,128)} custom-call(f32[2,2,16,32,128]{4,3,2,1,0:T(8,128)} %bitcast.12, f32[2,2,4,512]{3,2,1,0:T(4,128)} %bitcast.13), custom_call_target="tpu_custom_call" | custom-call | bytes 2097152 | tf_op jit(solution)/shard_map/pack/pallas_call | solution.py:202
  2.2 0.0 copy-start
  2.2 8.1 %all-to-all-start = ((f32[16,132,128]{2,1,0:T(8,128)}), f32[16,132,128]{2,1,0:T(8,128)S(1)}, u32[]{:S(2)}, u32[]{:S(2)}) async-start(f32[16,132,128]{2,1,0:T(8,128)} %pack.1), calls=%async_computation | async-start | bytes 2228224 | tf_op jit(solution)/shard_map/near_move/all_to_all | solution.py:220
  10.3 0.0 copy-done
  10.3 0.1 coef.1.coef_ref
  10.4 10.2 %all-to-all-done.near_ref.left_ref = f32[16,132,128]{2,1,0:T(8,128)S(1)} async-done(((f32[16,132,128]{2,1,0:T(8,128)}), f32[16,132,128]{2,1,0:T(8,128)S(1)}, u32[]{:S(2)}, u32[]{:S(2)}) %all-to-all-start) | async-done | bytes 1081376 | tf_op jit(solution)/shard_map/near_move/all_to_all | solution.py:220
  20.6 0.7 spread.1
  21.4 23.4 %all-to-all-start.1 = ((f32[32,16,128]{2,1,0:T(8,128)}), f32[32,16,128]{2,1,0:T(8,128)S(1)}, u32[]{:S(2)}, u32[]{:S(2)}) async-start(f32[32,16,128]{2,1,0:T(8,128)} %bitcast.6), calls=%async_computation.1 | async-start | bytes 524288 | tf_op jit(solution)/shard_map/right_move/all_to_all | solution.py:234
  44.8 0.6 close.1
  45.4 2.2 %collective-permute-start.1 = (f32[32,1024]{1,0:T(8,128)S(1)}, f32[32,1024]{1,0:T(8,128)S(1)}, u32[]{:S(2)}, u32[]{:S(2)}) collective-permute-start(f32[32,1024]{1,0:T(8,128)S(1)} %get-tuple-element.9), channel_id=1, source_target_pairs={{0,256},{256,0},{1,257},{257,1},{2,258},{258,2},{3,259},{259,3},{4... | collective-permute-start | bytes 393224 | tf_op jit(solution)/shard_map/cuts_gather/ppermute | solution.py:248
  47.6 4.6 %collective-permute-start.2 = (f32[32,1024]{1,0:T(8,128)S(1)}, f32[32,1024]{1,0:T(8,128)S(1)}, u32[]{:S(2)}, u32[]{:S(2)}) collective-permute-start(f32[32,1024]{1,0:T(8,128)S(1)} %get-tuple-element.10), channel_id=1, source_target_pairs={{0,256},{256,0},{1,257},{257,1},{2,258},{258,2},{3,259},{259,3},{4... | collective-permute-start | bytes 393224 | tf_op jit(solution)/shard_map/cuts_gather/ppermute | solution.py:248
  52.2 2.8 %collective-permute-start = (f32[64,1024]{1,0:T(8,128)S(1)}, f32[64,1024]{1,0:T(8,128)S(1)}, u32[]{:S(2)}, u32[]{:S(2)}) collective-permute-start(f32[64,1024]{1,0:T(8,128)S(1)} %get-tuple-element.8.refs_0_), channel_id=1, source_target_pairs={{0,128},{128,0},{1,129},{129,1},{2,130},{130,2},{3,131},{131,3},{4... | collective-permute-start | bytes 786440 | tf_op jit(solution)/shard_map/cuts_gather/ppermute | solution.py:249
  55.0 0.0 collective-permute-done.1.refs_2_
  55.0 3.1 %collective-permute-start.3 = (f32[32,1024]{1,0:T(8,128)S(1)}, f32[32,1024]{1,0:T(8,128)S(1)}, u32[]{:S(2)}, u32[]{:S(2)}) collective-permute-start(f32[32,1024]{1,0:T(8,128)S(1)} %collective-permute-done.1.refs_2_), channel_id=1, source_target_pairs={{0,128},{128,0},{1,129},{129,1},{2,130},{130,2},{3,131},{131,3},{4... | collective-permute-start | bytes 393224 | tf_op jit(solution)/shard_map/cuts_gather/ppermute | solution.py:250
  58.1 0.0 collective-permute-done.2.refs_3_
  58.1 2.6 %collective-permute-start.4 = (f32[32,1024]{1,0:T(8,128)S(1)}, f32[32,1024]{1,0:T(8,128)S(1)}, u32[]{:S(2)}, u32[]{:S(2)}) collective-permute-start(f32[32,1024]{1,0:T(8,128)S(1)} %collective-permute-done.2.refs_3_), channel_id=1, source_target_pairs={{0,128},{128,0},{1,129},{129,1},{2,130},{130,2},{3,131},{131,3},{4... | collective-permute-start | bytes 393224 | tf_op jit(solution)/shard_map/cuts_gather/ppermute | solution.py:250
  60.7 0.0 collective-permute-done.3.refs_4_
  60.7 0.9 %collective-permute-done.4.refs_5_ = f32[32,1024]{1,0:T(8,128)S(1)} collective-permute-done((f32[32,1024]{1,0:T(8,128)S(1)}, f32[32,1024]{1,0:T(8,128)S(1)}, u32[]{:S(2)}, u32[]{:S(2)}) %collective-permute-start.4) | collective-permute-done | bytes 131104 | tf_op jit(solution)/shard_map/cuts_gather/ppermute | solution.py:250
  61.7 0.0 collective-permute-done.refs_1_
  61.7 0.0 all-to-all-done.1
  61.7 1.1 %join.1 = f32[16,8,8,128]{3,2,1,0:T(8,128)S(1)} custom-call(s32[1]{0:T(128)} %bitcast.cut_ref, f32[4,8,16,128]{3,2,1,0:T(8,128)S(1)} %bitcast.10, f32[64,1024]{1,0:T(8,128)S(1)} %get-tuple-element.8.refs_0_, f32[64,1024]{1,0:T(8,128)S(1)} %collective-permute-done.refs_1_, f32[32,1024]{1,0:T(8,128)S(1)} %collective-permute-done.1.refs_2_, ...), custom_call_target="tpu_custom_call" | custom-call | flops 134217728 | bytes 2097152 | tf_op jit(solution)/shard_map/join/pallas_call | solution.py:252
  62.8 13.7 %all_to_all.20.parts_ref = f32[16,8,8,128]{3,2,1,0:T(8,128)S(1)} all-to-all(f32[16,8,8,128]{3,2,1,0:T(8,128)S(1)} %join.1), channel_id=1, replica_groups=mesh['yh'=2,'core'=2,'yl'=2,'x'=4,'za'=8,'zb'=2] {'yl','x','zb'}, dimensions={0} | all-to-all | bytes 1048576 | tf_op jit(solution)/shard_map/sum_move/all_to_all | solution.py:262
  76.5 0.1 sum.1
  76.6 13.6 %all_to_all.21.parts_ref = f32[8,8,128]{2,1,0:T(8,128)S(1)} all-to-all(f32[8,8,128]{2,1,0:T(8,128)S(1)} %sum.1), channel_id=1, replica_groups={{8,10,12,14,0,2,4,6},{9,11,13,15,1,3,5,7},{24,26,28,30,16,18,20,22},{25..., dimensions={0} | all-to-all | bytes 65536 | tf_op jit(solution)/shard_map/last_move/all_to_all | solution.py:273
  90.1 0.6 finish.1
Async XLA Ops:
  2.2 8.1 %copy-start = (f32[2,2,128,4]{2,3,1,0:T(4,128)S(1)}, f32[2,2,128,4]{2,3,1,0:T(4,128)}, u32[]{:S(2)}) copy-start(f32[2,2,128,4]{2,3,1,0:T(4,128)} %param.5) | copy-start | bytes 24580
  2.2 18.4 %all-to-all-start = ((f32[16,132,128]{2,1,0:T(8,128)}), f32[16,132,128]{2,1,0:T(8,128)S(1)}, u32[]{:S(2)}, u32[]{:S(2)}) async-start(f32[16,132,128]{2,1,0:T(8,128)} %pack.1), calls=%async_computation | async-start | bytes 2228224 | tf_op jit(solution)/shard_map/near_move/all_to_all | solution.py:220
  21.4 40.3 %all-to-all-start.1 = ((f32[32,16,128]{2,1,0:T(8,128)}), f32[32,16,128]{2,1,0:T(8,128)S(1)}, u32[]{:S(2)}, u32[]{:S(2)}) async-start(f32[32,16,128]{2,1,0:T(8,128)} %bitcast.6), calls=%async_computation.1 | async-start | bytes 524288 | tf_op jit(solution)/shard_map/right_move/all_to_all | solution.py:234
  45.4 9.6 %collective-permute-start.1 = (f32[32,1024]{1,0:T(8,128)S(1)}, f32[32,1024]{1,0:T(8,128)S(1)}, u32[]{:S(2)}, u32[]{:S(2)}) collective-permute-start(f32[32,1024]{1,0:T(8,128)S(1)} %get-tuple-element.9), channel_id=1, source_target_pairs={{0,256},{256,0},{1,257},{257,1},{2,258},{258,2},{3,259},{259,3},{4... | collective-permute-start | bytes 393224 | tf_op jit(solution)/shard_map/cuts_gather/ppermute | solution.py:248
  47.6 10.5 %collective-permute-start.2 = (f32[32,1024]{1,0:T(8,128)S(1)}, f32[32,1024]{1,0:T(8,128)S(1)}, u32[]{:S(2)}, u32[]{:S(2)}) collective-permute-start(f32[32,1024]{1,0:T(8,128)S(1)} %get-tuple-element.10), channel_id=1, source_target_pairs={{0,256},{256,0},{1,257},{257,1},{2,258},{258,2},{3,259},{259,3},{4... | collective-permute-start | bytes 393224 | tf_op jit(solution)/shard_map/cuts_gather/ppermute | solution.py:248
  52.2 9.5 %collective-permute-start = (f32[64,1024]{1,0:T(8,128)S(1)}, f32[64,1024]{1,0:T(8,128)S(1)}, u32[]{:S(2)}, u32[]{:S(2)}) collective-permute-start(f32[64,1024]{1,0:T(8,128)S(1)} %get-tuple-element.8.refs_0_), channel_id=1, source_target_pairs={{0,128},{128,0},{1,129},{129,1},{2,130},{130,2},{3,131},{131,3},{4... | collective-permute-start | bytes 786440 | tf_op jit(solution)/shard_map/cuts_gather/ppermute | solution.py:249
  55.0 5.7 %collective-permute-start.3 = (f32[32,1024]{1,0:T(8,128)S(1)}, f32[32,1024]{1,0:T(8,128)S(1)}, u32[]{:S(2)}, u32[]{:S(2)}) collective-permute-start(f32[32,1024]{1,0:T(8,128)S(1)} %collective-permute-done.1.refs_2_), channel_id=1, source_target_pairs={{0,128},{128,0},{1,129},{129,1},{2,130},{130,2},{3,131},{131,3},{4... | collective-permute-start | bytes 393224 | tf_op jit(solution)/shard_map/cuts_gather/ppermute | solution.py:250
  58.1 3.6 %collective-permute-start.4 = (f32[32,1024]{1,0:T(8,128)S(1)}, f32[32,1024]{1,0:T(8,128)S(1)}, u32[]{:S(2)}, u32[]{:S(2)}) collective-permute-start(f32[32,1024]{1,0:T(8,128)S(1)} %collective-permute-done.2.refs_3_), channel_id=1, source_target_pairs={{0,128},{128,0},{1,129},{129,1},{2,130},{130,2},{3,131},{131,3},{4... | collective-permute-start | bytes 393224 | tf_op jit(solution)/shard_map/cuts_gather/ppermute | solution.py:250

commit v20 on v17

--- a/solution.py
+++ b/solution.py
@@ -153,7 +153,7 @@
             rhs[im, half:] = x_ref[:, :half]
     for j in range(0, wide // LANES, 2):
         right = rhs[:, pl.ds(j * LANES, 2 * LANES)]
-        out = jnp.dot(lhs[...], right, precision=lax.Precision.HIGHEST, preferred_element_type=F32)
+        out = jnp.dot(lhs[...], right, precision=lax.Precision.HIGH, preferred_element_type=F32)
         out_ref[:, j, :, :] = out[:, :LANES].reshape(16, 8, LANES)
         out_ref[:, j + 1, :, :] = out[:, LANES:].reshape(16, 8, LANES)
 

time: 91.3 us -> 90.9 us (level)
  no operation moved by 1% of the time
where the time goes in v20:
time: 90.9 us; the launch traced here: 89.3 us
  starting transfers between devices  45.9 us (50%)
  blocking collectives  26.7 us (29%)
  waiting for transfers between devices  11.5 us (13%)
  Pallas kernels  5.07 us (6%)
    all_to_all x1, starting transfers between devices, shards(): lax.all_to_all(r, CUTS + (FAR,), 0, 0, tiled=True, axis_index_groups=[gro...  22.4 us
    all_to_all x1, blocking collectives, shards(): p = lax.all_to_all(p, FAR, 0, 0, tiled=True, axis_index_groups=[group])  13.9 us
    all_to_all x1, blocking collectives, shards(): p = lax.all_to_all(p, NEAR, 0, 0, tiled=True)  12.8 us
    all_to_all x1, waiting for transfers between devices, shards(): x = lax.all_to_all(x, NEAR, 0, 0, tiled=True, axis_index_groups=[ORDER])  10.2 us
    all_to_all x1, starting transfers between devices, shards(): x = lax.all_to_all(x, NEAR, 0, 0, tiled=True, axis_index_groups=[ORDER])  8.11 us
    ppermute x2, starting transfers between devices, shards(): x2 = [lax.ppermute(piece, 'yh', swap) for piece in pieces]  6.79 us
    ppermute x2, starting transfers between devices, shards(): x3 = [lax.ppermute(piece, 'core', swap) for piece in x2]  5.75 us
    ppermute x1, starting transfers between devices, shards(): x1 = lax.ppermute(x0, 'core', swap)  2.81 us
  transfers between devices with their start and end apart: 7, of which 3 were waited for; matrix products, arithmetic and copies ran while one was open for 0% of the time, Pallas kernels for 1%

profile of v20, /device:TPU:1, one launch (start us, length us, event | category | flops | bytes accessed | tf_op | source)
XLA Modules:
  0.0 89.3 jit_solution(10578894192263422870)
XLA Ops:
  0.0 2.2 %pack.1 = f32[16,132,128]{2,1,0:T(8,128)} custom-call(f32[2,2,16,32,128]{4,3,2,1,0:T(8,128)} %bitcast.12, f32[2,2,4,512]{3,2,1,0:T(4,128)} %bitcast.13), custom_call_target="tpu_custom_call" | custom-call | bytes 2097152 | tf_op jit(solution)/shard_map/pack/pallas_call | solution.py:202
  2.2 0.0 copy-start
  2.2 8.1 %all-to-all-start = ((f32[16,132,128]{2,1,0:T(8,128)}), f32[16,132,128]{2,1,0:T(8,128)S(1)}, u32[]{:S(2)}, u32[]{:S(2)}) async-start(f32[16,132,128]{2,1,0:T(8,128)} %pack.1), calls=%async_computation | async-start | bytes 2228224 | tf_op jit(solution)/shard_map/near_move/all_to_all | solution.py:220
  10.3 0.0 copy-done
  10.3 0.1 coef.1.coef_ref
  10.4 10.2 %all-to-all-done.near_ref.left_ref = f32[16,132,128]{2,1,0:T(8,128)S(1)} async-done(((f32[16,132,128]{2,1,0:T(8,128)}), f32[16,132,128]{2,1,0:T(8,128)S(1)}, u32[]{:S(2)}, u32[]{:S(2)}) %all-to-all-start) | async-done | bytes 1081376 | tf_op jit(solution)/shard_map/near_move/all_to_all | solution.py:220
  20.6 0.7 spread.1
  21.4 22.4 %all-to-all-start.1 = ((f32[32,16,128]{2,1,0:T(8,128)}), f32[32,16,128]{2,1,0:T(8,128)S(1)}, u32[]{:S(2)}, u32[]{:S(2)}) async-start(f32[32,16,128]{2,1,0:T(8,128)} %bitcast.6), calls=%async_computation.1 | async-start | bytes 524288 | tf_op jit(solution)/shard_map/right_move/all_to_all | solution.py:234
  43.8 0.6 close.1
  44.4 2.2 %collective-permute-start.1 = (f32[32,1024]{1,0:T(8,128)S(1)}, f32[32,1024]{1,0:T(8,128)S(1)}, u32[]{:S(2)}, u32[]{:S(2)}) collective-permute-start(f32[32,1024]{1,0:T(8,128)S(1)} %get-tuple-element.9), channel_id=1, source_target_pairs={{0,256},{256,0},{1,257},{257,1},{2,258},{258,2},{3,259},{259,3},{4... | collective-permute-start | bytes 393224 | tf_op jit(solution)/shard_map/cuts_gather/ppermute | solution.py:248
  46.6 4.6 %collective-permute-start.2 = (f32[32,1024]{1,0:T(8,128)S(1)}, f32[32,1024]{1,0:T(8,128)S(1)}, u32[]{:S(2)}, u32[]{:S(2)}) collective-permute-start(f32[32,1024]{1,0:T(8,128)S(1)} %get-tuple-element.10), channel_id=1, source_target_pairs={{0,256},{256,0},{1,257},{257,1},{2,258},{258,2},{3,259},{259,3},{4... | collective-permute-start | bytes 393224 | tf_op jit(solution)/shard_map/cuts_gather/ppermute | solution.py:248
  51.3 2.8 %collective-permute-start = (f32[64,1024]{1,0:T(8,128)S(1)}, f32[64,1024]{1,0:T(8,128)S(1)}, u32[]{:S(2)}, u32[]{:S(2)}) collective-permute-start(f32[64,1024]{1,0:T(8,128)S(1)} %get-tuple-element.8.refs_0_), channel_id=1, source_target_pairs={{0,128},{128,0},{1,129},{129,1},{2,130},{130,2},{3,131},{131,3},{4... | collective-permute-start | bytes 786440 | tf_op jit(solution)/shard_map/cuts_gather/ppermute | solution.py:249
  54.1 0.0 collective-permute-done.1.refs_2_
  54.1 3.1 %collective-permute-start.3 = (f32[32,1024]{1,0:T(8,128)S(1)}, f32[32,1024]{1,0:T(8,128)S(1)}, u32[]{:S(2)}, u32[]{:S(2)}) collective-permute-start(f32[32,1024]{1,0:T(8,128)S(1)} %collective-permute-done.1.refs_2_), channel_id=1, source_target_pairs={{0,128},{128,0},{1,129},{129,1},{2,130},{130,2},{3,131},{131,3},{4... | collective-permute-start | bytes 393224 | tf_op jit(solution)/shard_map/cuts_gather/ppermute | solution.py:250
  57.1 0.0 collective-permute-done.2.refs_3_
  57.2 2.7 %collective-permute-start.4 = (f32[32,1024]{1,0:T(8,128)S(1)}, f32[32,1024]{1,0:T(8,128)S(1)}, u32[]{:S(2)}, u32[]{:S(2)}) collective-permute-start(f32[32,1024]{1,0:T(8,128)S(1)} %collective-permute-done.2.refs_3_), channel_id=1, source_target_pairs={{0,128},{128,0},{1,129},{129,1},{2,130},{130,2},{3,131},{131,3},{4... | collective-permute-start | bytes 393224 | tf_op jit(solution)/shard_map/cuts_gather/ppermute | solution.py:250
  59.9 0.0 collective-permute-done.3.refs_4_
  59.9 0.9 %collective-permute-done.4.refs_5_ = f32[32,1024]{1,0:T(8,128)S(1)} collective-permute-done((f32[32,1024]{1,0:T(8,128)S(1)}, f32[32,1024]{1,0:T(8,128)S(1)}, u32[]{:S(2)}, u32[]{:S(2)}) %collective-permute-start.4) | collective-permute-done | bytes 131104 | tf_op jit(solution)/shard_map/cuts_gather/ppermute | solution.py:250
  60.8 0.0 collective-permute-done.refs_1_
  60.8 0.3 all-to-all-done.1
  61.2 0.7 join.1
  61.9 12.8 %all_to_all.20.parts_ref = f32[16,8,8,128]{3,2,1,0:T(8,128)S(1)} all-to-all(f32[16,8,8,128]{3,2,1,0:T(8,128)S(1)} %join.1), channel_id=1, replica_groups=mesh['yh'=2,'core'=2,'yl'=2,'x'=4,'za'=8,'zb'=2] {'yl','x','zb'}, dimensions={0} | all-to-all | bytes 1048576 | tf_op jit(solution)/shard_map/sum_move/all_to_all | solution.py:262
  74.8 0.1 sum.1
  74.8 13.9 %all_to_all.21.parts_ref = f32[8,8,128]{2,1,0:T(8,128)S(1)} all-to-all(f32[8,8,128]{2,1,0:T(8,128)S(1)} %sum.1), channel_id=1, replica_groups={{8,10,12,14,0,2,4,6},{9,11,13,15,1,3,5,7},{24,26,28,30,16,18,20,22},{25..., dimensions={0} | all-to-all | bytes 65536 | tf_op jit(solution)/shard_map/last_move/all_to_all | solution.py:273
  88.7 0.6 finish.1
Async XLA Ops:
  2.2 8.1 %copy-start = (f32[2,2,128,4]{2,3,1,0:T(4,128)S(1)}, f32[2,2,128,4]{2,3,1,0:T(4,128)}, u32[]{:S(2)}) copy-start(f32[2,2,128,4]{2,3,1,0:T(4,128)} %param.5) | copy-start | bytes 24580
  2.2 18.4 %all-to-all-start = ((f32[16,132,128]{2,1,0:T(8,128)}), f32[16,132,128]{2,1,0:T(8,128)S(1)}, u32[]{:S(2)}, u32[]{:S(2)}) async-start(f32[16,132,128]{2,1,0:T(8,128)} %pack.1), calls=%async_computation | async-start | bytes 2228224 | tf_op jit(solution)/shard_map/near_move/all_to_all | solution.py:220
  21.4 39.8 %all-to-all-start.1 = ((f32[32,16,128]{2,1,0:T(8,128)}), f32[32,16,128]{2,1,0:T(8,128)S(1)}, u32[]{:S(2)}, u32[]{:S(2)}) async-start(f32[32,16,128]{2,1,0:T(8,128)} %bitcast.6), calls=%async_computation.1 | async-start | bytes 524288 | tf_op jit(solution)/shard_map/right_move/all_to_all | solution.py:234
  44.4 9.6 %collective-permute-start.1 = (f32[32,1024]{1,0:T(8,128)S(1)}, f32[32,1024]{1,0:T(8,128)S(1)}, u32[]{:S(2)}, u32[]{:S(2)}) collective-permute-start(f32[32,1024]{1,0:T(8,128)S(1)} %get-tuple-element.9), channel_id=1, source_target_pairs={{0,256},{256,0},{1,257},{257,1},{2,258},{258,2},{3,259},{259,3},{4... | collective-permute-start | bytes 393224 | tf_op jit(solution)/shard_map/cuts_gather/ppermute | solution.py:248
  46.6 10.5 %collective-permute-start.2 = (f32[32,1024]{1,0:T(8,128)S(1)}, f32[32,1024]{1,0:T(8,128)S(1)}, u32[]{:S(2)}, u32[]{:S(2)}) collective-permute-start(f32[32,1024]{1,0:T(8,128)S(1)} %get-tuple-element.10), channel_id=1, source_target_pairs={{0,256},{256,0},{1,257},{257,1},{2,258},{258,2},{3,259},{259,3},{4... | collective-permute-start | bytes 393224 | tf_op jit(solution)/shard_map/cuts_gather/ppermute | solution.py:248
  51.3 9.6 %collective-permute-start = (f32[64,1024]{1,0:T(8,128)S(1)}, f32[64,1024]{1,0:T(8,128)S(1)}, u32[]{:S(2)}, u32[]{:S(2)}) collective-permute-start(f32[64,1024]{1,0:T(8,128)S(1)} %get-tuple-element.8.refs_0_), channel_id=1, source_target_pairs={{0,128},{128,0},{1,129},{129,1},{2,130},{130,2},{3,131},{131,3},{4... | collective-permute-start | bytes 786440 | tf_op jit(solution)/shard_map/cuts_gather/ppermute | solution.py:249
  54.1 5.8 %collective-permute-start.3 = (f32[32,1024]{1,0:T(8,128)S(1)}, f32[32,1024]{1,0:T(8,128)S(1)}, u32[]{:S(2)}, u32[]{:S(2)}) collective-permute-start(f32[32,1024]{1,0:T(8,128)S(1)} %collective-permute-done.1.refs_2_), channel_id=1, source_target_pairs={{0,128},{128,0},{1,129},{129,1},{2,130},{130,2},{3,131},{131,3},{4... | collective-permute-start | bytes 393224 | tf_op jit(solution)/shard_map/cuts_gather/ppermute | solution.py:250
  57.2 3.7 %collective-permute-start.4 = (f32[32,1024]{1,0:T(8,128)S(1)}, f32[32,1024]{1,0:T(8,128)S(1)}, u32[]{:S(2)}, u32[]{:S(2)}) collective-permute-start(f32[32,1024]{1,0:T(8,128)S(1)} %collective-permute-done.2.refs_3_), channel_id=1, source_target_pairs={{0,128},{128,0},{1,129},{129,1},{2,130},{130,2},{3,131},{131,3},{4... | collective-permute-start | bytes 393224 | tf_op jit(solution)/shard_map/cuts_gather/ppermute | solution.py:250

commit v21 on v17

--- a/solution.py
+++ b/solution.py
@@ -17,7 +17,7 @@
 F32 = jnp.float32
 LANES = 128
 MID = 6
-HALF = 2
+HALF = 0
 LAST = 4
 ORDER = [yl * 8 + x * 2 + zb for x in (3, 1, 2, 0) for yl in (1, 0) for zb in range(2)]
 SMEM = pl.BlockSpec(memory_space=pltpu.SMEM)

time: 91.3 us -> 92.3 us (1.011)
  the two profiles are of different devices: /device:TPU:1 before, /device:TPU:8 now
where the time goes in v21:
time: 92.3 us; the launch traced here: 91.8 us
  starting transfers between devices  40.2 us (44%)
  blocking collectives  30.4 us (33%)
  waiting for transfers between devices  15.7 us (17%)
  Pallas kernels  5.46 us (6%)
    all_to_all x1, starting transfers between devices, shards(): lax.all_to_all(r, CUTS + (FAR,), 0, 0, tiled=True, axis_index_groups=[gro...  17.3 us
    all_to_all x1, blocking collectives, shards(): p = lax.all_to_all(p, NEAR, 0, 0, tiled=True)  15.9 us
    all_to_all x1, blocking collectives, shards(): p = lax.all_to_all(p, FAR, 0, 0, tiled=True, axis_index_groups=[group])  14.5 us
    all_to_all x1, waiting for transfers between devices, shards(): x = lax.all_to_all(x, NEAR, 0, 0, tiled=True, axis_index_groups=[ORDER])  11.7 us
    all_to_all x1, starting transfers between devices, shards(): x = lax.all_to_all(x, NEAR, 0, 0, tiled=True, axis_index_groups=[ORDER])  9.8 us
    ppermute x2, starting transfers between devices, shards(): x2 = [lax.ppermute(piece, 'yh', swap) for piece in pieces]  7.35 us
    ppermute x2, starting transfers between devices, shards(): x3 = [lax.ppermute(piece, 'core', swap) for piece in x2]  3.82 us
    ppermute x2, waiting for transfers between devices, shards(): x2 = [lax.ppermute(piece, 'yh', swap) for piece in pieces]  2.69 us
  transfers between devices with their start and end apart: 7, of which 4 were waited for; matrix products, arithmetic and copies ran while one was open for 0% of the time, Pallas kernels for 1%

profile of v21, /device:TPU:8, one launch (start us, length us, event | category | flops | bytes accessed | tf_op | source)
XLA Modules:
  0.0 91.8 jit_solution(17308777483311467596)
XLA Ops:
  0.0 2.2 %pack.1 = f32[16,132,128]{2,1,0:T(8,128)} custom-call(f32[2,2,16,32,128]{4,3,2,1,0:T(8,128)} %bitcast.12, f32[2,2,4,512]{3,2,1,0:T(4,128)} %bitcast.13), custom_call_target="tpu_custom_call" | custom-call | bytes 2097152 | tf_op jit(solution)/shard_map/pack/pallas_call | solution.py:202
  2.2 0.0 copy-start
  2.2 9.8 %all-to-all-start = ((f32[16,132,128]{2,1,0:T(8,128)}), f32[16,132,128]{2,1,0:T(8,128)S(1)}, u32[]{:S(2)}, u32[]{:S(2)}) async-start(f32[16,132,128]{2,1,0:T(8,128)} %pack.1), calls=%async_computation | async-start | bytes 2228224 | tf_op jit(solution)/shard_map/near_move/all_to_all | solution.py:220
  12.0 0.0 copy-done
  12.0 0.1 coef.1.coef_ref
  12.1 11.7 %all-to-all-done.near_ref.left_ref = f32[16,132,128]{2,1,0:T(8,128)S(1)} async-done(((f32[16,132,128]{2,1,0:T(8,128)}), f32[16,132,128]{2,1,0:T(8,128)S(1)}, u32[]{:S(2)}, u32[]{:S(2)}) %all-to-all-start) | async-done | bytes 1081376 | tf_op jit(solution)/shard_map/near_move/all_to_all | solution.py:220
  23.9 0.7 spread.1
  24.6 17.3 %all-to-all-start.1 = ((f32[32,16,128]{2,1,0:T(8,128)}), f32[32,16,128]{2,1,0:T(8,128)S(1)}, u32[]{:S(2)}, u32[]{:S(2)}) async-start(f32[32,16,128]{2,1,0:T(8,128)} %bitcast.6), calls=%async_computation.1 | async-start | bytes 524288 | tf_op jit(solution)/shard_map/right_move/all_to_all | solution.py:234
  41.9 0.6 close.1
  42.5 4.9 %collective-permute-start.1 = (f32[32,1024]{1,0:T(8,128)S(1)}, f32[32,1024]{1,0:T(8,128)S(1)}, u32[]{:S(2)}, u32[]{:S(2)}) collective-permute-start(f32[32,1024]{1,0:T(8,128)S(1)} %get-tuple-element.9), channel_id=1, source_target_pairs={{0,256},{256,0},{1,257},{257,1},{2,258},{258,2},{3,259},{259,3},{4... | collective-permute-start | bytes 393224 | tf_op jit(solution)/shard_map/cuts_gather/ppermute | solution.py:248
  47.4 2.5 %collective-permute-start.2 = (f32[32,1024]{1,0:T(8,128)S(1)}, f32[32,1024]{1,0:T(8,128)S(1)}, u32[]{:S(2)}, u32[]{:S(2)}) collective-permute-start(f32[32,1024]{1,0:T(8,128)S(1)} %get-tuple-element.10), channel_id=1, source_target_pairs={{0,256},{256,0},{1,257},{257,1},{2,258},{258,2},{3,259},{259,3},{4... | collective-permute-start | bytes 393224 | tf_op jit(solution)/shard_map/cuts_gather/ppermute | solution.py:248
  49.9 1.9 %collective-permute-start = (f32[64,1024]{1,0:T(8,128)S(1)}, f32[64,1024]{1,0:T(8,128)S(1)}, u32[]{:S(2)}, u32[]{:S(2)}) collective-permute-start(f32[64,1024]{1,0:T(8,128)S(1)} %get-tuple-element.8.refs_0_), channel_id=1, source_target_pairs={{0,128},{128,0},{1,129},{129,1},{2,130},{130,2},{3,131},{131,3},{4... | collective-permute-start | bytes 786440 | tf_op jit(solution)/shard_map/cuts_gather/ppermute | solution.py:249
  51.8 0.8 collective-permute-done.1.refs_2_
  52.6 1.9 %collective-permute-start.3 = (f32[32,1024]{1,0:T(8,128)S(1)}, f32[32,1024]{1,0:T(8,128)S(1)}, u32[]{:S(2)}, u32[]{:S(2)}) collective-permute-start(f32[32,1024]{1,0:T(8,128)S(1)} %collective-permute-done.1.refs_2_), channel_id=1, source_target_pairs={{0,128},{128,0},{1,129},{129,1},{2,130},{130,2},{3,131},{131,3},{4... | collective-permute-start | bytes 393224 | tf_op jit(solution)/shard_map/cuts_gather/ppermute | solution.py:250
  54.5 1.9 %collective-permute-done.2.refs_3_ = f32[32,1024]{1,0:T(8,128)S(1)} collective-permute-done((f32[32,1024]{1,0:T(8,128)S(1)}, f32[32,1024]{1,0:T(8,128)S(1)}, u32[]{:S(2)}, u32[]{:S(2)}) %collective-permute-start.2) | collective-permute-done | bytes 131104 | tf_op jit(solution)/shard_map/cuts_gather/ppermute | solution.py:248
  56.4 1.9 %collective-permute-start.4 = (f32[32,1024]{1,0:T(8,128)S(1)}, f32[32,1024]{1,0:T(8,128)S(1)}, u32[]{:S(2)}, u32[]{:S(2)}) collective-permute-start(f32[32,1024]{1,0:T(8,128)S(1)} %collective-permute-done.2.refs_3_), channel_id=1, source_target_pairs={{0,128},{128,0},{1,129},{129,1},{2,130},{130,2},{3,131},{131,3},{4... | collective-permute-start | bytes 393224 | tf_op jit(solution)/shard_map/cuts_gather/ppermute | solution.py:250
  58.3 0.0 collective-permute-done.3.refs_4_
  58.3 1.3 %collective-permute-done.4.refs_5_ = f32[32,1024]{1,0:T(8,128)S(1)} collective-permute-done((f32[32,1024]{1,0:T(8,128)S(1)}, f32[32,1024]{1,0:T(8,128)S(1)}, u32[]{:S(2)}, u32[]{:S(2)}) %collective-permute-start.4) | collective-permute-done | bytes 131104 | tf_op jit(solution)/shard_map/cuts_gather/ppermute | solution.py:250
  59.6 0.0 collective-permute-done.refs_1_
  59.6 0.0 all-to-all-done.1
  59.6 1.1 %join.1 = f32[16,8,8,128]{3,2,1,0:T(8,128)S(1)} custom-call(s32[1]{0:T(128)} %bitcast.cut_ref, f32[4,8,16,128]{3,2,1,0:T(8,128)S(1)} %bitcast.10, f32[64,1024]{1,0:T(8,128)S(1)} %get-tuple-element.8.refs_0_, f32[64,1024]{1,0:T(8,128)S(1)} %collective-permute-done.refs_1_, f32[32,1024]{1,0:T(8,128)S(1)} %collective-permute-done.1.refs_2_, ...), custom_call_target="tpu_custom_call" | custom-call | flops 134217728 | bytes 2097152 | tf_op jit(solution)/shard_map/join/pallas_call | solution.py:252
  60.8 15.9 %all_to_all.20.parts_ref = f32[16,8,8,128]{3,2,1,0:T(8,128)S(1)} all-to-all(f32[16,8,8,128]{3,2,1,0:T(8,128)S(1)} %join.1), channel_id=1, replica_groups=mesh['yh'=2,'core'=2,'yl'=2,'x'=4,'za'=8,'zb'=2] {'yl','x','zb'}, dimensions={0} | all-to-all | bytes 1048576 | tf_op jit(solution)/shard_map/sum_move/all_to_all | solution.py:262
  76.7 0.1 sum.1
  76.7 14.5 %all_to_all.21.parts_ref = f32[8,8,128]{2,1,0:T(8,128)S(1)} all-to-all(f32[8,8,128]{2,1,0:T(8,128)S(1)} %sum.1), channel_id=1, replica_groups={{8,10,12,14,0,2,4,6},{9,11,13,15,1,3,5,7},{24,26,28,30,16,18,20,22},{25..., dimensions={0} | all-to-all | bytes 65536 | tf_op jit(solution)/shard_map/last_move/all_to_all | solution.py:273
  91.2 0.6 finish.1
Async XLA Ops:
  2.2 9.8 %copy-start = (f32[2,2,128,4]{2,3,1,0:T(4,128)S(1)}, f32[2,2,128,4]{2,3,1,0:T(4,128)}, u32[]{:S(2)}) copy-start(f32[2,2,128,4]{2,3,1,0:T(4,128)} %param.5) | copy-start | bytes 24580
  2.2 21.6 %all-to-all-start = ((f32[16,132,128]{2,1,0:T(8,128)}), f32[16,132,128]{2,1,0:T(8,128)S(1)}, u32[]{:S(2)}, u32[]{:S(2)}) async-start(f32[16,132,128]{2,1,0:T(8,128)} %pack.1), calls=%async_computation | async-start | bytes 2228224 | tf_op jit(solution)/shard_map/near_move/all_to_all | solution.py:220
  24.6 35.0 %all-to-all-start.1 = ((f32[32,16,128]{2,1,0:T(8,128)}), f32[32,16,128]{2,1,0:T(8,128)S(1)}, u32[]{:S(2)}, u32[]{:S(2)}) async-start(f32[32,16,128]{2,1,0:T(8,128)} %bitcast.6), calls=%async_computation.1 | async-start | bytes 524288 | tf_op jit(solution)/shard_map/right_move/all_to_all | solution.py:234
  42.5 10.1 %collective-permute-start.1 = (f32[32,1024]{1,0:T(8,128)S(1)}, f32[32,1024]{1,0:T(8,128)S(1)}, u32[]{:S(2)}, u32[]{:S(2)}) collective-permute-start(f32[32,1024]{1,0:T(8,128)S(1)} %get-tuple-element.9), channel_id=1, source_target_pairs={{0,256},{256,0},{1,257},{257,1},{2,258},{258,2},{3,259},{259,3},{4... | collective-permute-start | bytes 393224 | tf_op jit(solution)/shard_map/cuts_gather/ppermute | solution.py:248
  47.4 9.0 %collective-permute-start.2 = (f32[32,1024]{1,0:T(8,128)S(1)}, f32[32,1024]{1,0:T(8,128)S(1)}, u32[]{:S(2)}, u32[]{:S(2)}) collective-permute-start(f32[32,1024]{1,0:T(8,128)S(1)} %get-tuple-element.10), channel_id=1, source_target_pairs={{0,256},{256,0},{1,257},{257,1},{2,258},{258,2},{3,259},{259,3},{4... | collective-permute-start | bytes 393224 | tf_op jit(solution)/shard_map/cuts_gather/ppermute | solution.py:248
  49.9 9.8 %collective-permute-start = (f32[64,1024]{1,0:T(8,128)S(1)}, f32[64,1024]{1,0:T(8,128)S(1)}, u32[]{:S(2)}, u32[]{:S(2)}) collective-permute-start(f32[64,1024]{1,0:T(8,128)S(1)} %get-tuple-element.8.refs_0_), channel_id=1, source_target_pairs={{0,128},{128,0},{1,129},{129,1},{2,130},{130,2},{3,131},{131,3},{4... | collective-permute-start | bytes 786440 | tf_op jit(solution)/shard_map/cuts_gather/ppermute | solution.py:249
  52.6 5.7 %collective-permute-start.3 = (f32[32,1024]{1,0:T(8,128)S(1)}, f32[32,1024]{1,0:T(8,128)S(1)}, u32[]{:S(2)}, u32[]{:S(2)}) collective-permute-start(f32[32,1024]{1,0:T(8,128)S(1)} %collective-permute-done.1.refs_2_), channel_id=1, source_target_pairs={{0,128},{128,0},{1,129},{129,1},{2,130},{130,2},{3,131},{131,3},{4... | collective-permute-start | bytes 393224 | tf_op jit(solution)/shard_map/cuts_gather/ppermute | solution.py:250
  56.4 3.2 %collective-permute-start.4 = (f32[32,1024]{1,0:T(8,128)S(1)}, f32[32,1024]{1,0:T(8,128)S(1)}, u32[]{:S(2)}, u32[]{:S(2)}) collective-permute-start(f32[32,1024]{1,0:T(8,128)S(1)} %collective-permute-done.2.refs_3_), channel_id=1, source_target_pairs={{0,128},{128,0},{1,129},{129,1},{2,130},{130,2},{3,131},{131,3},{4... | collective-permute-start | bytes 393224 | tf_op jit(solution)/shard_map/cuts_gather/ppermute | solution.py:250
